TPU v7x, 32 devices: a whole 2x2x4 slice. The times are simulated.
32 devices in a mesh: tp: 4 (over y, x), dp: 8 (over z, core).
Axes of the slice: x: 2, y: 2, z: 4, core: 2. Of those that a mesh axis runs over, the one named last changes fastest.
Arguments:
- tokens: bfloat16 [16384, 1152], P('dp')
- cotangent: bfloat16 [16384, 1152], P('dp')
- quarter_ids: int32 [64], P('dp'), may hold values from 0 to 63, as said below
- labels: int32 [64], P('dp'), may hold values from 0 to 1000
- timesteps: int32 [64], P('dp'), may hold values from 0 to 999
- qkv_weight: float32 [1152, 3, 1152], P('dp', None, 'tp')
- qkv_moment: float32 [1152, 3, 1152], P('dp', None, 'tp'), may hold values from -0.0029296875 to 0.0029296875
- qkv_second: float32 [1152, 3, 1152], P('dp', None, 'tp'), may hold values from 3.993447e-08 to 1.5973788e-07
- qkv_average: float32 [1152, 3, 1152], P('dp', None, 'tp')
- proj_weight: float32 [1152, 1152], P('tp', 'dp'), may hold values from -1.5 to 1.5
- proj_moment: float32 [1152, 1152], P('tp', 'dp'), may hold values from -0.0029296875 to 0.0029296875
- proj_second: float32 [1152, 1152], P('tp', 'dp'), may hold values from 3.993447e-08 to 1.5973788e-07
- proj_average: float32 [1152, 1152], P('tp', 'dp'), may hold values from -1.5 to 1.5
- up_weight: float32 [1152, 4608], P('dp', 'tp')
- up_moment: float32 [1152, 4608], P('dp', 'tp'), may hold values from -0.00021362305 to 0.00021362305
- up_second: float32 [1152, 4608], P('dp', 'tp'), may hold values from 2.4959043e-10 to 9.983617e-10
- up_average: float32 [1152, 4608], P('dp', 'tp')
- down_weight: float32 [4608, 1152], P('tp', 'dp'), may hold values from -0.09375 to 0.09375
- down_moment: float32 [4608, 1152], P('tp', 'dp'), may hold values from -0.0029296875 to 0.0029296875
- down_second: float32 [4608, 1152], P('tp', 'dp'), may hold values from 3.993447e-08 to 1.5973788e-07
- down_average: float32 [4608, 1152], P('tp', 'dp'), may hold values from -0.09375 to 0.09375
- ada_weight: float32 [1152, 6, 1152], P('dp', None, 'tp'), may hold values from -0.1875 to 0.1875
- ada_moment: float32 [1152, 6, 1152], P('dp', None, 'tp'), may hold values from -0.0029296875 to 0.0029296875
- ada_second: float32 [1152, 6, 1152], P('dp', None, 'tp'), may hold values from 3.993447e-08 to 1.5973788e-07
- ada_average: float32 [1152, 6, 1152], P('dp', None, 'tp'), may hold values from -0.1875 to 0.1875
- table_weight: float32 [1001, 1152], P(None, 'dp'), may hold values from -6 to 6
- table_moment: float32 [1001, 1152], P(None, 'dp'), may hold values from -0.0029296875 to 0.0029296875
- table_second: float32 [1001, 1152], P(None, 'dp'), may hold values from 1.9967235e-09 to 7.986894e-09
- table_average: float32 [1001, 1152], P(None, 'dp'), may hold values from -6 to 6
Outputs:
- block_out: bfloat16 [16384, 1152], P('dp')
- token_grad: bfloat16 [16384, 1152], P('dp')
- grad_norm: float32 [], replicated
- qkv_moment_new: float32 [1152, 3, 1152], P('dp', None, 'tp')
- qkv_second_new: float32 [1152, 3, 1152], P('dp', None, 'tp')
- qkv_weight_new: float32 [1152, 3, 1152], P('dp', None, 'tp')
- qkv_average_new: float32 [1152, 3, 1152], P('dp', None, 'tp')
- proj_moment_new: float32 [1152, 1152], P('tp', 'dp')
- proj_second_new: float32 [1152, 1152], P('tp', 'dp')
- proj_weight_new: float32 [1152, 1152], P('tp', 'dp')
- proj_average_new: float32 [1152, 1152], P('tp', 'dp')
- up_moment_new: float32 [1152, 4608], P('dp', 'tp')
- up_second_new: float32 [1152, 4608], P('dp', 'tp')
- up_weight_new: float32 [1152, 4608], P('dp', 'tp')
- up_average_new: float32 [1152, 4608], P('dp', 'tp')
- down_moment_new: float32 [4608, 1152], P('tp', 'dp')
- down_second_new: float32 [4608, 1152], P('tp', 'dp')
- down_weight_new: float32 [4608, 1152], P('tp', 'dp')
- down_average_new: float32 [4608, 1152], P('tp', 'dp')
- ada_moment_new: float32 [1152, 6, 1152], P('dp', None, 'tp')
- ada_second_new: float32 [1152, 6, 1152], P('dp', None, 'tp')
- ada_weight_new: float32 [1152, 6, 1152], P('dp', None, 'tp')
- ada_average_new: float32 [1152, 6, 1152], P('dp', None, 'tp')
- table_moment_new: float32 [1001, 1152], P(None, 'dp')
- table_second_new: float32 [1001, 1152], P(None, 'dp')
- table_weight_new: float32 [1001, 1152], P(None, 'dp')
- table_average_new: float32 [1001, 1152], P(None, 'dp')
Inputs may be any that keep to these rules, and one draw needn't show every extreme that they name: `quarter_ids`: for each aligned group of four entries starting at index 4k, the entries are either all 4k (one image of 1024 tokens) or 4k, 4k + 1, 4k + 2, 4k + 3 (four images of 256 tokens); the last group is always four images of 256 tokens. An image's label and timestep are those at its slot's index; the other entries of labels and timesteps are unused.
All inputs are finite; a program needn't handle non-finite values.
Results may differ from a plain program's by a relative error of at most 0.015.
The roundings to bfloat16 on the way count: a program that leaves them out, or rounds other values in their place, can miss the bound.
Values may be sent and summed in bfloat16 or wider, within the bound.
A program may use at most 320 MiB of HBM per device.

v0:
```python
import math

import jax
import jax.numpy as jnp
from jax import lax
from jax.sharding import PartitionSpec as P

D = 1152
HD = 72
FF = 4608
STEP = 5


HIGHEST = lax.Precision.HIGHEST
clip_limit = 1.0


def layer_norm(values):
    centre = values - jnp.mean(values, axis=-1, keepdims=True)
    spread = jnp.mean(centre * centre, axis=-1, keepdims=True)
    return centre * lax.rsqrt(spread + 1e-06)


def modulate(rows, shift, scale):
    return layer_norm(rows) * (1.0 + scale[:, None, :]) + shift[:, None, :]


def time_embed(stamps, width):
    half_width = width // 2
    freqs = jnp.exp(-math.log(10000.0) * jnp.arange(half_width, dtype=jnp.float32) / half_width)
    angles = (stamps.astype(jnp.float32) / 1000.0)[:, None] * freqs[None, :]
    return jnp.concatenate([jnp.cos(angles), jnp.sin(angles)], axis=-1)


def gelu_tanh(values):
    return jax.nn.gelu(values, approximate=True)


def span_scores(queries, keys_in, member):
    scores = jnp.einsum(
        "qhe,khe->hqk", queries, keys_in, preferred_element_type=jnp.float32
    ) * HD ** (-0.5)
    same_image = member[:, None] == member[None, :]
    return jnp.where(same_image[None], scores, -1000000000.0)


def attend_span(inputs):
    span_qkv, member = inputs
    scores = span_scores(span_qkv[:, 0], span_qkv[:, 1], member)
    top_score = jnp.max(scores, axis=-1, keepdims=True)
    expo = jnp.exp(scores - top_score)
    total = jnp.sum(expo, axis=-1, keepdims=True)
    probs = expo / total
    head_out = jnp.einsum(
        "hqk,khe->qhe",
        probs.astype(jnp.bfloat16),
        span_qkv[:, 2],
        preferred_element_type=jnp.float32,
    )
    return (head_out.astype(jnp.bfloat16), top_score + jnp.log(total))


def span_backward(inputs):
    span_qkv, member, log_total, grad_out = inputs
    queries = span_qkv[:, 0]
    keys_in = span_qkv[:, 1]
    values_in = span_qkv[:, 2]
    probs = jnp.exp(span_scores(queries, keys_in, member) - log_total)
    grad_prob = jnp.einsum("qhe,khe->hqk", grad_out, values_in, preferred_element_type=jnp.float32)
    grad_score = probs * (grad_prob - jnp.sum(probs * grad_prob, axis=-1, keepdims=True))
    grad_low = grad_score.astype(jnp.bfloat16)
    grad_query = jnp.einsum(
        "hqk,khe->qhe", grad_low, keys_in, preferred_element_type=jnp.float32
    ) * HD ** (-0.5)
    grad_key = jnp.einsum(
        "hqk,qhe->khe", grad_low, queries, preferred_element_type=jnp.float32
    ) * HD ** (-0.5)
    grad_value = jnp.einsum(
        "hqk,qhe->khe", probs.astype(jnp.bfloat16), grad_out, preferred_element_type=jnp.float32
    )
    return jnp.stack([grad_query, grad_key, grad_value], axis=1).astype(jnp.bfloat16)


def adam_step(weight, moment, second, average, gradient, rate):
    moment = 0.5 * moment + 0.5 * gradient
    second = 0.5 * second + 0.5 * gradient * gradient
    correct = 1.0 - 0.5**STEP
    weight = weight - rate * (
        moment / correct / (jnp.sqrt(second / correct) + 1e-08) + 0.1 * weight
    )
    keep_rate = min(0.9999, (1.0 + STEP) / (10.0 + STEP))
    average = keep_rate * average + (1.0 - keep_rate) * weight
    return (moment, second, weight, average)


def per_device(
    tokens,
    cotangent,
    quarter_ids,
    labels,
    timesteps,
    qkv_weight,
    qkv_moment,
    qkv_second,
    qkv_average,
    proj_weight,
    proj_moment,
    proj_second,
    proj_average,
    up_weight,
    up_moment,
    up_second,
    up_average,
    down_weight,
    down_moment,
    down_second,
    down_average,
    ada_weight,
    ada_moment,
    ada_second,
    ada_average,
    table_weight,
    table_moment,
    table_second,
    table_average,
):
    row_count, width = tokens.shape
    slot_count = quarter_ids.shape[0]
    small_len = row_count // slot_count
    span_len = 4 * small_len
    span_count = slot_count // 4
    bf16 = jnp.bfloat16
    tp_count = lax.axis_size("tp")
    tp_place = lax.axis_index("tp")
    wqkv, wproj, w_up, w_down, wada, table = (
        lax.all_gather(qkv_weight.astype(bf16), "dp", axis=0, tiled=True),
        lax.all_gather(proj_weight.astype(bf16), "dp", axis=1, tiled=True),
        lax.all_gather(up_weight.astype(bf16), "dp", axis=0, tiled=True),
        lax.all_gather(down_weight.astype(bf16), "dp", axis=1, tiled=True),
        lax.all_gather(ada_weight.astype(bf16), "dp", axis=0, tiled=True),
        lax.all_gather(table_weight.astype(bf16), "dp", axis=1, tiled=True),
    )
    local_width = wqkv.shape[2]
    heads_local = local_width // HD
    slot_base = lax.axis_index("dp") * slot_count
    choose = (
        quarter_ids[:, None] - slot_base == jnp.arange(slot_count, dtype=jnp.int32)[None, :]
    ).astype(jnp.float32)
    class_onehot = (labels[:, None] == jnp.arange(table.shape[0], dtype=jnp.int32)[None, :]).astype(
        bf16
    )
    embed = jnp.dot(class_onehot, table, preferred_element_type=jnp.float32) + time_embed(
        timesteps, width
    )
    cond_low = jax.nn.silu(embed).astype(bf16)
    mod_part = jnp.einsum("qd,dke->qke", cond_low, wada, preferred_element_type=jnp.float32)
    modulation = lax.all_gather(mod_part, "tp", axis=2, tiled=True)
    quarter_mod = jnp.einsum("ps,ske->pke", choose, modulation, precision=HIGHEST)
    shift_one = quarter_mod[:, 0]
    scale_one = quarter_mod[:, 1]
    gate_one = quarter_mod[:, 2]
    shift_two = quarter_mod[:, 3]
    scale_two = quarter_mod[:, 4]
    gate_two = quarter_mod[:, 5]
    rows_in = tokens.astype(jnp.float32).reshape(slot_count, small_len, width)
    first_in = modulate(rows_in, shift_one, scale_one).astype(bf16).reshape(row_count, width)
    qkv_all = jnp.einsum("nd,dke->nke", first_in, wqkv, preferred_element_type=jnp.float32).astype(
        bf16
    )
    span_qkv = qkv_all.reshape(span_count, span_len, 3, heads_local, HD)
    member = jnp.repeat(quarter_ids, small_len).reshape(span_count, span_len)
    head_out, log_total = lax.map(attend_span, (span_qkv, member))
    attended = head_out.reshape(row_count, local_width)
    branch_part = jnp.dot(attended, wproj, preferred_element_type=jnp.float32)
    grad_out = cotangent.astype(jnp.float32).reshape(slot_count, small_len, width)
    grad_mixed = (grad_out * gate_two[:, None, :]).astype(bf16).reshape(row_count, width)
    branch = lax.psum(branch_part, "tp").reshape(slot_count, small_len, width)
    middle = rows_in + gate_one[:, None, :] * branch
    second_in = modulate(middle, shift_two, scale_two).astype(bf16).reshape(row_count, width)
    hidden = jnp.dot(second_in, w_up, preferred_element_type=jnp.float32)
    active = gelu_tanh(hidden).astype(bf16)
    mixed = lax.psum(
        jnp.dot(active, w_down, preferred_element_type=jnp.float32).astype(jnp.bfloat16), "tp"
    ).astype(jnp.float32)
    mixed = mixed.reshape(slot_count, small_len, width)
    block_out = (middle + gate_two[:, None, :] * mixed).reshape(row_count, width).astype(bf16)
    grad_gate_two = jnp.sum(grad_out * mixed, axis=1)
    grad_down = jnp.einsum("nf,nd->fd", active, grad_mixed, preferred_element_type=jnp.float32)
    grad_active = jnp.einsum("nd,fd->nf", grad_mixed, w_down, preferred_element_type=jnp.float32)
    unused, gelu_back = jax.vjp(gelu_tanh, hidden)
    grad_hidden = gelu_back(grad_active)[0].astype(bf16)
    grad_up = jnp.einsum("nd,nf->df", second_in, grad_hidden, preferred_element_type=jnp.float32)
    second_back = jnp.einsum("nf,df->nd", grad_hidden, w_up, preferred_element_type=jnp.float32)
    grad_second = lax.psum(second_back, "tp")
    unused, norm_back_two = jax.vjp(modulate, middle, shift_two, scale_two)
    grad_middle, grad_shift_two, grad_scale_two = norm_back_two(
        grad_second.reshape(slot_count, small_len, width)
    )
    grad_middle = grad_middle + grad_out
    grad_gate_one = jnp.sum(grad_middle * branch, axis=1)
    grad_branch = (grad_middle * gate_one[:, None, :]).astype(bf16).reshape(row_count, width)
    grad_proj = jnp.einsum("nc,nd->cd", attended, grad_branch, preferred_element_type=jnp.float32)
    grad_attended = jnp.einsum(
        "nd,cd->nc", grad_branch, wproj, preferred_element_type=jnp.float32
    ).astype(bf16)
    grad_heads = grad_attended.reshape(span_count, span_len, heads_local, HD)
    grad_qkv = lax.map(span_backward, (span_qkv, member, log_total, grad_heads)).reshape(
        row_count, 3, local_width
    )
    grad_qkv_w = jnp.einsum("nd,nke->dke", first_in, grad_qkv, preferred_element_type=jnp.float32)
    first_back = jnp.einsum("nke,dke->nd", grad_qkv, wqkv, preferred_element_type=jnp.float32)
    grad_first = lax.psum(first_back, "tp")
    unused, norm_back_one = jax.vjp(modulate, rows_in, shift_one, scale_one)
    grad_rows, grad_shift_one, grad_scale_one = norm_back_one(
        grad_first.reshape(slot_count, small_len, width)
    )
    token_grad = (grad_rows + grad_middle).reshape(row_count, width).astype(bf16)
    grad_quarter = jnp.stack(
        [
            grad_shift_one,
            grad_scale_one,
            grad_gate_one,
            grad_shift_two,
            grad_scale_two,
            grad_gate_two,
        ],
        axis=1,
    )
    grad_mod = jnp.einsum("ps,pke->ske", choose, grad_quarter, precision=HIGHEST)
    col_start = tp_place * local_width
    grad_mod_low = lax.dynamic_slice_in_dim(grad_mod, col_start, local_width, 2).astype(bf16)
    grad_ada = jnp.einsum("qd,qke->dke", cond_low, grad_mod_low, preferred_element_type=jnp.float32)
    grad_cond = lax.psum(
        jnp.einsum("qke,dke->qd", grad_mod_low, wada, preferred_element_type=jnp.float32), "tp"
    )
    unused, silu_back = jax.vjp(jax.nn.silu, embed)
    grad_embed = silu_back(grad_cond)[0]
    grad_table = jnp.einsum(
        "qc,qd->cd", class_onehot.astype(jnp.float32), grad_embed, precision=HIGHEST
    )
    qkv_reduced, proj_reduced, up_reduced, down_reduced, ada_reduced, table_reduced = (
        lax.psum_scatter(grad_qkv_w, "dp", scatter_dimension=0, tiled=True),
        lax.psum_scatter(grad_proj, "dp", scatter_dimension=1, tiled=True),
        lax.psum_scatter(grad_up, "dp", scatter_dimension=0, tiled=True),
        lax.psum_scatter(grad_down, "dp", scatter_dimension=1, tiled=True),
        lax.psum_scatter(grad_ada, "dp", scatter_dimension=0, tiled=True),
        lax.psum_scatter(grad_table, "dp", scatter_dimension=1, tiled=True),
    )
    local_squares = jnp.sum(qkv_reduced * qkv_reduced) + jnp.sum(proj_reduced * proj_reduced)
    local_squares = (
        local_squares + jnp.sum(up_reduced * up_reduced) + jnp.sum(down_reduced * down_reduced)
    )
    local_squares = local_squares + jnp.sum(ada_reduced * ada_reduced)
    local_squares = local_squares + jnp.sum(table_reduced * table_reduced) / tp_count
    grad_norm = jnp.sqrt(lax.psum(local_squares, ("tp", "dp")))
    factor = jnp.minimum(1.0, clip_limit / (grad_norm + 1e-06))
    qkv_new = adam_step(
        qkv_weight, qkv_moment, qkv_second, qkv_average, qkv_reduced * factor, 0.5 * D ** (-0.5)
    )
    proj_new = adam_step(
        proj_weight,
        proj_moment,
        proj_second,
        proj_average,
        proj_reduced * factor,
        4.0 * D ** (-0.5),
    )
    up_new = adam_step(
        up_weight, up_moment, up_second, up_average, up_reduced * factor, 0.5 * D ** (-0.5)
    )
    down_new = adam_step(
        down_weight,
        down_moment,
        down_second,
        down_average,
        down_reduced * factor,
        0.5 * FF ** (-0.5),
    )
    ada_new = adam_step(
        ada_weight, ada_moment, ada_second, ada_average, ada_reduced * factor, 0.5 * D ** (-0.5)
    )
    table_new = adam_step(
        table_weight, table_moment, table_second, table_average, table_reduced * factor, 0.5
    )
    return (
        block_out,
        token_grad,
        grad_norm,
        qkv_new[0],
        qkv_new[1],
        qkv_new[2],
        qkv_new[3],
        proj_new[0],
        proj_new[1],
        proj_new[2],
        proj_new[3],
        up_new[0],
        up_new[1],
        up_new[2],
        up_new[3],
        down_new[0],
        down_new[1],
        down_new[2],
        down_new[3],
        ada_new[0],
        ada_new[1],
        ada_new[2],
        ada_new[3],
        table_new[0],
        table_new[1],
        table_new[2],
        table_new[3],
    )


def solution(mesh):
    placed = (
        P("dp", None),
        P("dp", None),
        P("dp"),
        P("dp"),
        P("dp"),
        P("dp", None, "tp"),
        P("dp", None, "tp"),
        P("dp", None, "tp"),
        P("dp", None, "tp"),
        P("tp", "dp"),
        P("tp", "dp"),
        P("tp", "dp"),
        P("tp", "dp"),
        P("dp", "tp"),
        P("dp", "tp"),
        P("dp", "tp"),
        P("dp", "tp"),
        P("tp", "dp"),
        P("tp", "dp"),
        P("tp", "dp"),
        P("tp", "dp"),
        P("dp", None, "tp"),
        P("dp", None, "tp"),
        P("dp", None, "tp"),
        P("dp", None, "tp"),
        P(None, "dp"),
        P(None, "dp"),
        P(None, "dp"),
        P(None, "dp"),
    )
    return jax.shard_map(
        per_device,
        mesh=mesh,
        in_specs=placed,
        out_specs=(
            P("dp", None),
            P("dp", None),
            P(),
            P("dp", None, "tp"),
            P("dp", None, "tp"),
            P("dp", None, "tp"),
            P("dp", None, "tp"),
            P("tp", "dp"),
            P("tp", "dp"),
            P("tp", "dp"),
            P("tp", "dp"),
            P("dp", "tp"),
            P("dp", "tp"),
            P("dp", "tp"),
            P("dp", "tp"),
            P("tp", "dp"),
            P("tp", "dp"),
            P("tp", "dp"),
            P("tp", "dp"),
            P("dp", None, "tp"),
            P("dp", None, "tp"),
            P("dp", None, "tp"),
            P("dp", None, "tp"),
            P(None, "dp"),
            P(None, "dp"),
            P(None, "dp"),
            P(None, "dp"),
        ),
        check_vma=False,
    )
```

profile of v0, /device:TPU:0, one launch (start us, length us, event | category | flops | bytes accessed | tf_op | source)
XLA Modules:
  0.0 1607.9 jit_solution(3344844201945199420)
XLA Ops:
  25.1 24.1 %all_gather.25 = bf16[288,1152]{0,1:T(8,128)(2,1)} all-gather(bf16[288,144]{0,1:T(8,128)(2,1)S(1)} %convert_element_type.107), channel_id=1, replica_groups=mesh['tp'=4,'dp'=8] {'dp'}, dimensions={1}, use_global_device_ids=true | all-gather | bytes 746496 | tf_op jit(solution)/shard_map/all_gather | solution.py:137
  54.0 55.6 %all-gather.8.cloned.1.call-done = bf16[1152,6,288]{2,0,1:T(8,128)(2,1)} async-done(((bf16[144,6,288]{2,0,1:T(8,128)(2,1)}), bf16[1152,6,288]{2,0,1:T(8,128)(2,1)}) %all-gather.8.cloned.1.call-update) | async-done | bytes 3981328 | tf_op jit(solution)/shard_map/all_gather | solution.py:140
  113.4 45.7 %all_gather.23 = f32[8,6,1152]{1,0,2:T(8,128)} all-gather(f32[8,6,288]{1,0,2:T(8,128)S(1)} %copy.80), channel_id=1, replica_groups=mesh['tp'=4,'dp'=8] {'tp'}, dimensions={2}, use_global_device_ids=true | all-gather | bytes 276480 | tf_op jit(solution)/shard_map/all_gather | solution.py:157
  190.2 32.6 %while.22 = (s32[]{:T(128)}, bf16[2,1024,4,72]{1,3,2,0:T(8,128)(2,1)}, f32[2,4,1024,1]{2,1,3,0:T(4,128)}, bf16[2,1024,3,4,72]{1,4,3,2,0:T(8,128)(2,1)}, s32[2,1024]{1,0:T(2,128)S(1)}, /*index=5*/s32[]{:T(128)}) while((s32[]{:T(128)}, bf16[2,1024,4,72]{1,3,2,0:T(8,128)(2,1)}, f32[2,4,1024,1]{2,1,3,0:T(4,128)}, ...), condition=%wide.region_5.6_spmd, body=%wide.region_2.5_spmd.sunk | while | flops 1259630592 | bytes 70267088 | solution.py:172
  249.9 168.6 %all-reduce.5.cloned.1.call-done = f32[2048,1152]{1,0:T(8,128)} async-done(((f32[2048,1152]{1,0:T(8,128)}), f32[2048,1152]{1,0:T(8,128)}) %all-reduce.5.cloned.1.call-update) | async-done | bytes 9437200 | tf_op jit(solution)/shard_map/psum | solution.py:177
  438.5 16.3 %all-gather.12.cloned.1.call-done = bf16[1152,1152]{1,0:T(8,128)(2,1)} async-done(((bf16[144,1152]{1,0:T(8,128)(2,1)}), bf16[1152,1152]{1,0:T(8,128)(2,1)}) %all-gather.12.cloned.1.call-update) | async-done | bytes 2654224 | tf_op jit(solution)/shard_map/all_gather | solution.py:138
  454.8 18.3 %fusion.34 = (bf16[2048,1152]{1,0:T(8,128)(2,1)S(1)}, f32[2048,1152]{1,0:T(8,128)}) fusion(f32[2048,1152]{1,0:T(8,128)} %fusion.102, bf16[2048,1152]{1,0:T(8,128)(2,1)} %fusion.47, bf16[1152,1152]{1,0:T(8,128)(2,1)} %all-gather.12.cloned.1.call-done), kind=kOutput, calls=%fused_computation.66 | convolution fusion | flops 5483003904 | bytes 30965760 | tf_op jit(solution)/shard_map/dot_general | solution.py:180
  497.8 174.7 %all-reduce.9.cloned.1.call-done = f32[2048,1152]{1,0:T(8,128)} async-done(((f32[2048,1152]{1,0:T(8,128)}), f32[2048,1152]{1,0:T(8,128)}) %all-reduce.9.cloned.1.call-update) | async-done | bytes 9437200 | tf_op jit(solution)/shard_map/psum | solution.py:194
  680.2 108.6 %all-reduce.7.cloned.1.call-done = bf16[2048,1152]{1,0:T(8,128)(2,1)} async-done(((bf16[2048,1152]{1,0:T(8,128)(2,1)}), bf16[2048,1152]{1,0:T(8,128)(2,1)}) %all-reduce.7.cloned.1.call-update) | async-done | bytes 4718608 | tf_op jit(solution)/shard_map/psum | solution.py:182
  788.9 13.5 fusion.98
  815.3 114.8 %while.23 = (s32[]{:T(128)}, bf16[2,1024,3,4,72]{1,4,3,2,0:T(8,128)(2,1)}, bf16[2,1024,3,4,72]{1,4,3,2,0:T(8,128)(2,1)}, s32[2,1024]{1,0:T(2,128)S(1)}, f32[2,4,...) while((s32[]{:T(128)}, bf16[2,1024,3,4,72]{1,4,3,2,0:T(8,128)(2,1)}, ...), condition=%wide.region_15.16_spmd, body=%wide.region_13.15_spmd.sunk | while | flops 3065475072 | bytes 269971680 | solution.py:207
  840.0 15.4 multiply_convert_fusion.8
  897.1 15.4 multiply_convert_fusion.8
  964.7 14.6 fusion.90
  997.2 143.4 %all-reduce.11.cloned.1.call-done = f32[2048,1152]{1,0:T(8,128)} async-done(((f32[2048,1152]{1,0:T(8,128)}), f32[2048,1152]{1,0:T(8,128)}) %all-reduce.11.cloned.1.call-update) | async-done | bytes 9437200 | tf_op jit(solution)/shard_map/psum | solution.py:212
  1140.7 18.6 %fusion.49 = (f32[8,1152]{1,0:T(8,128)S(1)}, f32[8,1152]{1,0:T(8,128)S(1)}, f32[8,1152]{1,0:T(8,128)S(1)}, f32[8,1152]{1,0:T(8,128)S(1)}, f32[8,1152]{1,0:T(8,128)S(1)}, /*index=5*/f32[8,1152]{1,0:T(8,128)S(1)}) fusion(f32[2048,1152]{1,0:T(8,128)} %all-reduce.9.cloned.1.call-done, f32[2048,1152]{1,0:T(8,128)} %all-reduce.5.cloned.1.call-done, ...), kind=kLoop, calls=%fused_computation.85 | loop fusion | flops 61286400 | bytes 42811392 | tf_op jit(solution)/shard_map/transpose(jvp())/reduce_sum | solution.py:25
  1161.2 15.9 psum.46
  1187.4 15.9 reduce-scatter.11.cloned.1.call-done
  1205.2 59.4 %reduce-scatter.13.cloned.1.call-done = f32[1152,144]{0,1:T(8,128)} async-done(((f32[1152,1152]{0,1:T(8,128)}), f32[1152,144]{0,1:T(8,128)}) %reduce-scatter.13.cloned.1.call-update) | async-done | bytes 663568 | tf_op jit(solution)/shard_map/reduce_scatter | solution.py:245
  1266.5 33.6 %reduce-scatter.9.cloned.1.call-done = f32[288,144]{0,1:T(8,128)} async-done(((f32[288,1152]{0,1:T(8,128)}), f32[288,144]{0,1:T(8,128)}) %reduce-scatter.9.cloned.1.call-update) | async-done | bytes 165904 | tf_op jit(solution)/shard_map/reduce_scatter | solution.py:243
  1301.7 59.4 %reduce-scatter.7.cloned.1.call-done = f32[144,3,288]{2,0,1:T(8,128)} async-done(((f32[1152,3,288]{2,0,1:T(8,128)}), f32[144,3,288]{2,0,1:T(8,128)}) %reduce-scatter.7.cloned.1.call-update) | async-done | bytes 497680 | tf_op jit(solution)/shard_map/reduce_scatter | solution.py:242
  1378.2 38.9 %reduce-scatter.17.cloned.1.call-done = f32[1001,144]{0,1:T(8,128)} async-done(((f32[1001,1152]{0,1:T(8,128)}), f32[1001,144]{0,1:T(8,128)}) %reduce-scatter.17.cloned.1.call-update) | async-done | bytes 576592 | tf_op jit(solution)/shard_map/reduce_scatter | solution.py:247
  1419.6 108.7 %reduce-scatter.15.cloned.1.call-done = f32[144,6,288]{2,0,1:T(8,128)} async-done(((f32[1152,6,288]{2,0,1:T(8,128)}), f32[144,6,288]{2,0,1:T(8,128)}) %reduce-scatter.15.cloned.1.call-update) | async-done | bytes 995344 | tf_op jit(solution)/shard_map/reduce_scatter | solution.py:246
  1544.3 38.0 %psum.47 = f32[]{:T(128)} all-reduce(f32[]{:T(128)S(6)} %add.312), channel_id=1, replica_groups=mesh['tp'=4,'dp'=8] {'tp','dp'}, use_global_device_ids=true, to_apply=%region_38.39 | all-reduce | flops 1 | bytes 8 | tf_op jit(solution)/shard_map/psum | solution.py:255
  (310 shorter events, 382.8 us)
Async XLA Ops:
  7.2 44.5 %all-gather.6.cloned.1.call-start = ((), (), s32[]{:S(2)}) async-start(), calls=%async_computation.6 | async-start | bytes 2654208 | tf_op jit(solution)/shard_map/all_gather | solution.py:141
  9.2 100.4 %all-gather.8.cloned.1.call-start = ((), (), s32[]{:S(2)}) async-start(), calls=%async_computation.7 | async-start | bytes 5971968 | tf_op jit(solution)/shard_map/all_gather | solution.py:140
  11.5 158.2 %all-gather.10.cloned.1.call-start = ((), (), s32[]{:S(2)}) async-start(), calls=%async_computation.8 | async-start | bytes 2985984 | tf_op jit(solution)/shard_map/all_gather | solution.py:136
  13.4 224.8 %all-gather.14.cloned.1.call-start = ((), (), s32[]{:S(2)}) async-start(), calls=%async_computation.11 | async-start | bytes 2985984 | tf_op jit(solution)/shard_map/all_gather | solution.py:139
  15.3 403.2 %all-reduce.5.cloned.1.call-start = ((), (), s32[]{:S(2)}) async-start(), calls=%async_computation.9 | async-start | bytes 18874368 | tf_op jit(solution)/shard_map/psum | solution.py:177
  16.8 145.8 %copy-start.58 = (s32[8]{0:T(128)}, s32[8]{0:T(128)S(1)}, u32[]{:S(2)}) copy-start(s32[8]{0:T(128)S(1)} %broadcast_subtract_fusion) | copy-start | bytes 100
  231.8 223.0 %all-gather.12.cloned.1.call-start = ((), (), s32[]{:S(2)}) async-start(), calls=%async_computation.10 | async-start | bytes 2985984 | tf_op jit(solution)/shard_map/all_gather | solution.py:138
  232.7 439.8 %all-reduce.9.cloned.1.call-start = ((), (), s32[]{:S(2)}) async-start(), calls=%async_computation.13 | async-start | bytes 18874368 | tf_op jit(solution)/shard_map/psum | solution.py:194
  238.2 180.4 %copy-start.36 = (f32[8,1152]{1,0:T(8,128)S(1)}, f32[8,1152]{1,0:T(8,128)}, u32[]{:S(2)}) copy-start(f32[8,1152]{1,0:T(8,128)} %get-tuple-element.191) | copy-start | bytes 110596
  428.5 360.4 %copy-start.43 = (f32[2048]{0:T(1024)}, f32[2048]{0:T(1024)S(1)}, u32[]{:S(2)}) copy-start(f32[2048]{0:T(1024)S(1)} %broadcast_multiply_fusion) | copy-start | bytes 24580
  484.6 304.2 %all-reduce.7.cloned.1.call-start = ((), (), s32[]{:S(2)}) async-start(), calls=%async_computation.12 | async-start | bytes 9437184 | tf_op jit(solution)/shard_map/psum | solution.py:182
  497.7 642.9 %all-reduce.11.cloned.1.call-start = ((), (), s32[]{:S(2)}) async-start(), calls=%async_computation.14 | async-start | bytes 18874368 | tf_op jit(solution)/shard_map/psum | solution.py:212
  951.8 251.5 %reduce-scatter.11.cloned.1.call-start = ((), (), s32[]{:S(2)}) async-start(), calls=%async_computation.17 | async-start | bytes 5971968 | tf_op jit(solution)/shard_map/reduce_scatter | solution.py:244
  964.4 300.2 %reduce-scatter.13.cloned.1.call-start = ((), (), s32[]{:S(2)}) async-start(), calls=%async_computation.18 | async-start | bytes 5971968 | tf_op jit(solution)/shard_map/reduce_scatter | solution.py:245
  979.2 320.8 %reduce-scatter.9.cloned.1.call-start = ((), (), s32[]{:S(2)}) async-start(), calls=%async_computation.16 | async-start | bytes 1990656 | tf_op jit(solution)/shard_map/reduce_scatter | solution.py:243
  985.7 155.0 %copy-start.27 = (f32[8,1152]{1,0:T(8,128)S(1)}, f32[8,1152]{1,0:T(8,128)}, u32[]{:S(2)}) copy-start(f32[8,1152]{1,0:T(8,128)} %get-tuple-element.186) | copy-start | bytes 110596
  985.7 155.0 %copy-start.37 = (f32[8,1152]{1,0:T(8,128)S(1)}, f32[8,1152]{1,0:T(8,128)}, u32[]{:S(2)}) copy-start(f32[8,1152]{1,0:T(8,128)} %get-tuple-element.191) | copy-start | bytes 110596
  985.7 375.4 %reduce-scatter.7.cloned.1.call-start = ((), (), s32[]{:S(2)}) async-start(), calls=%async_computation.15 | async-start | bytes 5971968 | tf_op jit(solution)/shard_map/reduce_scatter | solution.py:242
  996.6 163.1 %slice-start.2 = ((s8[5308416]{0:T(1024)(128)(4,1)}), s8[1114112]{0:T(1024)(128)(4,1)S(1)}, s32[]{:S(2)}) async-start(s8[5308416]{0:T(1024)(128)(4,1)} %bitcast.265), calls=%async_computation.23 | async-start | bytes 2228224
  996.6 420.5 %reduce-scatter.17.cloned.1.call-start = ((), (), s32[]{:S(2)}) async-start(), calls=%async_computation.20 | async-start | bytes 5308416 | tf_op jit(solution)/shard_map/reduce_scatter | solution.py:247
  1181.4 184.1 %copy-start.25 = (f32[8,1152]{1,0:T(8,128)S(1)}, f32[8,1152]{1,0:T(8,128)}, u32[]{:S(2)}) copy-start(f32[8,1152]{1,0:T(8,128)} %copy-done.24) | copy-start | bytes 110596
  1181.4 346.9 %reduce-scatter.15.cloned.1.call-start = ((), (), s32[]{:S(2)}) async-start(), calls=%async_computation.19 | async-start | bytes 11943936 | tf_op jit(solution)/shard_map/reduce_scatter | solution.py:246
  1187.4 185.5 %copy-start.54 = (f32[2048]{0:T(1024)S(1)}, f32[2048]{0:T(1024)}, u32[]{:S(2)}) copy-start(f32[2048]{0:T(1024)} %copy-done.53) | copy-start | bytes 24580
  1187.4 185.5 %slice-start = ((s8[4718592]{0:T(1024)(128)(4,1)}), s8[524288]{0:T(1024)(128)(4,1)S(1)}, s32[]{:S(2)}) async-start(s8[4718592]{0:T(1024)(128)(4,1)} %bitcast.263), calls=%async_computation.21 | async-start | bytes 1048576
  (67 other events, 1369.7 us)
Sparse Core Ops, SparseCore 0:
  10.3 41.3 all-gather.5
  53.9 55.6 all-gather.7
  111.8 32.9 all-gather.9
  146.9 33.1 all-gather.13
  231.9 186.5 all-reduce.4
  420.6 34.1 all-gather.11
  484.8 187.6 all-reduce.8
  676.3 112.4 all-reduce.6
  952.0 188.6 all-reduce.10
  1142.8 60.5 reduce-scatter.10
  1205.7 58.8 reduce-scatter.12
  1266.8 33.2 reduce-scatter.8
  1302.4 58.6 reduce-scatter.6
  1363.8 53.3 reduce-scatter.16
  1419.3 109.0 reduce-scatter.14
where the time goes:
time: 1610 us
  waiting for transfers between devices  986 us (61%)
  matrix products  227 us (14%)
  other arithmetic  189 us (12%)
  blocking collectives  124 us (8%)
  local copies, waits for them, and re-layouts  59 us (4%)
  between operations  20.9 us (1%)
    psum x1, waiting for transfers between devices, per_device(): grad_second = lax.psum(second_back, 'tp')  175 us
    psum x1, waiting for transfers between devices, per_device(): branch = lax.psum(branch_part, 'tp').reshape(slot_count, small_len, width)  169 us
    psum x1, waiting for transfers between devices, per_device(): grad_first = lax.psum(first_back, 'tp')  143 us
    reduce_scatter x1, waiting for transfers between devices, per_device(): lax.psum_scatter(grad_ada, 'dp', scatter_dimension=0, tiled=True)  109 us
    psum x1, waiting for transfers between devices, per_device(): lax.psum(jnp.dot(active, w_down, preferred_element_type=jnp.float32).asty...  109 us
    reduce_scatter x1, waiting for transfers between devices, per_device(): lax.psum_scatter(grad_qkv_w, 'dp', scatter_dimension=0, tiled=True)  59.4 us
    reduce_scatter x1, waiting for transfers between devices, per_device(): lax.psum_scatter(grad_down, 'dp', scatter_dimension=1, tiled=True)  59.4 us
    all_gather x1, waiting for transfers between devices, per_device(): lax.all_gather(ada_weight.astype(bf16), 'dp', axis=0, tiled=True)  55.6 us
  transfers between devices with their start and end apart: 15, of which 13 were waited for; matrix products, arithmetic and copies ran while one was open for 15% of the time, Pallas kernels for 0%

commit v1 on v0

v1 whole, which is shorter than its diff:
```python
import functools
import math

import jax
import jax.numpy as jnp
from jax import lax
from jax.experimental import pallas as pl
from jax.experimental.pallas import tpu as pltpu
from jax.sharding import PartitionSpec as P

D = 1152
HD = 72
FF = 4608
STEP = 5

HIGHEST = lax.Precision.HIGHEST
F32 = jnp.float32
BF16 = jnp.bfloat16
clip_limit = 1.0
HEAD_SCALE = HD**-0.5
LOG2_SCALE = HEAD_SCALE * math.log2(math.e)


def dot32(a, b, dims):
    return lax.dot_general(a, b, (dims, ((), ())), preferred_element_type=F32)


def norm_parts(values):
    centre = values - jnp.mean(values, axis=-1, keepdims=True)
    spread = jnp.mean(centre * centre, axis=-1, keepdims=True)
    rstd = lax.rsqrt(spread + 1e-06)
    return centre * rstd, rstd


def norm_back(hat, rstd, grad_hat):
    first = jnp.mean(grad_hat, axis=-1, keepdims=True)
    second = jnp.mean(grad_hat * hat, axis=-1, keepdims=True)
    return rstd * (grad_hat - first - hat * second)


def time_embed(stamps, width):
    half_width = width // 2
    freqs = jnp.exp(-math.log(10000.0) * jnp.arange(half_width, dtype=jnp.float32) / half_width)
    angles = (stamps.astype(jnp.float32) / 1000.0)[:, None] * freqs[None, :]
    return jnp.concatenate([jnp.cos(angles), jnp.sin(angles)], axis=-1)


def attend_kernel(small_len, ids_ref, q_ref, k_ref, v_ref, out_ref, log_ref):
    count = q_ref.shape[-1] // small_len
    for qb in range(count):
        cols = pl.ds(qb * small_len, small_len)
        scores = dot32(k_ref[0, 0, 0], q_ref[0, 0, 0, :, cols], ((0,), (0,)))
        same = [ids_ref[kb] == ids_ref[qb] for kb in range(count)]
        blocks = [scores[kb * small_len : (kb + 1) * small_len] for kb in range(count)]
        top = jnp.full((1, small_len), -jnp.inf, F32)
        for kb in range(count):
            block_top = jnp.max(blocks[kb], axis=0, keepdims=True)
            top = jnp.maximum(top, jnp.where(same[kb], block_top, -jnp.inf))
        top = top * LOG2_SCALE
        total = jnp.zeros((1, small_len), F32)
        mixed = jnp.zeros((HD, small_len), F32)
        for kb in range(count):
            base = top + jnp.where(same[kb], 0.0, 1e9)
            expo = jnp.exp2(blocks[kb] * LOG2_SCALE - base)
            total = total + jnp.sum(expo, axis=0, keepdims=True)
            values = v_ref[0, 0, 0, :, pl.ds(kb * small_len, small_len)]
            mixed = mixed + dot32(values, expo.astype(BF16), ((1,), (0,)))
        out_ref[0, :, cols] = (mixed / total).astype(BF16)
        log_ref[0, :, cols] = top + jnp.log2(total)


def attend(qkv, ids, small_len):
    pair, _, heads, _, length = qkv.shape
    spec = lambda kind: pl.BlockSpec(
        (1, 1, 1, HD, length), lambda h: (h // heads, kind, h % heads, 0, 0)
    )
    return pl.pallas_call(
        functools.partial(attend_kernel, small_len),
        grid=(pair * heads,),
        in_specs=[pl.BlockSpec(memory_space=pltpu.SMEM), spec(0), spec(1), spec(2)],
        out_specs=[
            pl.BlockSpec((1, HD, length), lambda h: (h, 0, 0)),
            pl.BlockSpec((1, 1, length), lambda h: (h, 0, 0)),
        ],
        out_shape=[
            jax.ShapeDtypeStruct((pair * heads, HD, length), BF16),
            jax.ShapeDtypeStruct((pair * heads, 1, length), F32),
        ],
        compiler_params=pltpu.CompilerParams(vmem_limit_bytes=40 << 20),
    )(ids, qkv, qkv, qkv)


def attend_back_kernel(
    small_len, ids_ref, q_ref, k_ref, v_ref, go_ref, out_ref, log_ref, gq_ref, gk_ref, gv_ref
):
    length = q_ref.shape[-1]
    count = length // small_len
    grad_k = jnp.zeros((HD, length), F32)
    grad_v = jnp.zeros((HD, length), F32)
    for qb in range(count):
        cols = pl.ds(qb * small_len, small_len)
        queries = q_ref[0, 0, 0, :, cols]
        grad_out = go_ref[0, :, cols]
        delta = jnp.sum(
            grad_out.astype(F32) * out_ref[0, :, cols].astype(F32), axis=0, keepdims=True
        )
        scores = dot32(k_ref[0, 0, 0], queries, ((0,), (0,)))
        grad_prob = dot32(v_ref[0, 0, 0], grad_out, ((0,), (0,)))
        probs_low, score_low = [], []
        for kb in range(count):
            rows = slice(kb * small_len, (kb + 1) * small_len)
            base = log_ref[0, :, cols] + jnp.where(ids_ref[kb] == ids_ref[qb], 0.0, 1e9)
            probs = jnp.exp2(scores[rows] * LOG2_SCALE - base)
            probs_low.append(probs.astype(BF16))
            score_low.append((probs * (grad_prob[rows] - delta)).astype(BF16))
        probs_low = jnp.concatenate(probs_low, axis=0)
        score_low = jnp.concatenate(score_low, axis=0)
        grad_q = dot32(k_ref[0, 0, 0], score_low, ((1,), (0,)))
        gq_ref[0, 0, 0, :, cols] = (grad_q * HEAD_SCALE).astype(BF16)
        grad_k = grad_k + dot32(queries, score_low, ((1,), (1,)))
        grad_v = grad_v + dot32(grad_out, probs_low, ((1,), (1,)))
    gk_ref[0, 0, 0] = (grad_k * HEAD_SCALE).astype(BF16)
    gv_ref[0, 0, 0] = grad_v.astype(BF16)


def attend_back_whole(small_len, ids, q, k, v, go, out, log, dqkv):
    attend_back_kernel(
        small_len,
        ids,
        q,
        k,
        v,
        go,
        out,
        log,
        dqkv.at[:, 0:1],
        dqkv.at[:, 1:2],
        dqkv.at[:, 2:3],
    )


def attend_back(qkv, ids, grad_out, out, log_total, small_len):
    pair, _, heads, _, length = qkv.shape
    spec = lambda kind: pl.BlockSpec(
        (1, 1, 1, HD, length), lambda h: (h // heads, kind, h % heads, 0, 0)
    )
    head = lambda rows: pl.BlockSpec((1, rows, length), lambda h: (h, 0, 0))
    return pl.pallas_call(
        functools.partial(attend_back_whole, small_len),
        grid=(pair * heads,),
        in_specs=[
            pl.BlockSpec(memory_space=pltpu.SMEM),
            spec(0),
            spec(1),
            spec(2),
            head(HD),
            head(HD),
            head(1),
        ],
        out_specs=pl.BlockSpec(
            (1, 3, 1, HD, length), lambda h: (h // heads, 0, h % heads, 0, 0)
        ),
        out_shape=jax.ShapeDtypeStruct((pair, 3, heads, HD, length), BF16),
        compiler_params=pltpu.CompilerParams(vmem_limit_bytes=48 << 20),
    )(ids, qkv, qkv, qkv, grad_out, out, log_total)


def adam_step(weight, moment, second, average, gradient, rate):
    moment = 0.5 * moment + 0.5 * gradient
    second = 0.5 * second + 0.5 * gradient * gradient
    correct = 1.0 - 0.5**STEP
    weight = weight - rate * (
        moment / correct / (jnp.sqrt(second / correct) + 1e-08) + 0.1 * weight
    )
    keep_rate = min(0.9999, (1.0 + STEP) / (10.0 + STEP))
    average = keep_rate * average + (1.0 - keep_rate) * weight
    return (moment, second, weight, average)


def swap(value, axis, bit):
    count = lax.axis_size(axis)
    return lax.ppermute(value, axis, [(i, i ^ bit) for i in range(count)])


def shift(value, steps):
    count = lax.axis_size("dp")
    return lax.ppermute(value, "dp", [(i, (i + 2 * steps) % count) for i in range(count)])


def gather_rows(block):
    core = lax.axis_index("dp") % 2
    place = lax.axis_index("dp") // 2
    planes = lax.axis_size("dp") // 2
    rows, cols = block.shape
    whole = jnp.zeros((2, planes, 2, rows, cols), block.dtype)
    column = jnp.zeros((2, planes, rows, cols), block.dtype)
    for step in range(planes):
        piece = block if step == 0 else shift(block, step)
        both = jnp.stack([piece, swap(piece, "tp", 2)])[:, None]
        column = lax.dynamic_update_slice(column, both, (0, (place - step) % planes, 0, 0))
    other = swap(column, "dp", 1)
    first = jnp.where(core == 0, column, other)
    second = jnp.where(core == 0, other, column)
    whole = jnp.stack([first, second], axis=2)
    return whole.reshape(2, planes * 2 * rows, cols)


def scatter_rows(grad):
    core = lax.axis_index("dp") % 2
    place = lax.axis_index("dp") // 2
    planes = lax.axis_size("dp") // 2
    rows = grad.shape[1] // (2 * planes)
    parts = grad.reshape(2, planes, 2, rows, grad.shape[2])
    mine = lax.dynamic_index_in_dim(parts, core, 2, keepdims=False)
    theirs = lax.dynamic_index_in_dim(parts, 1 - core, 2, keepdims=False).astype(BF16)
    column = mine + swap(theirs, "dp", 1)
    column = column[0] + swap(column[1].astype(BF16), "tp", 2)
    total = lax.dynamic_index_in_dim(column, place, 0, keepdims=False)
    low = column.astype(BF16)
    for step in range(1, planes):
        part = lax.dynamic_index_in_dim(low, (place + step) % planes, 0, keepdims=False)
        total = total + shift(part, step)
    return total


def spread_rows(own, half_rows):
    side = lax.axis_index("tp") % 2
    span = lax.axis_index("tp") // 2
    other = swap(own, "tp", 1)
    rows, width = own.shape
    both = jnp.zeros((2, rows, width), own.dtype)
    both = lax.dynamic_update_slice(both, own[None], (side, 0, 0))
    both = lax.dynamic_update_slice(both, other[None], (1 - side, 0, 0))
    far = swap(both, "tp", 2)
    whole = jnp.zeros((2, 2, rows, width), own.dtype)
    whole = lax.dynamic_update_slice(whole, both[None], (span, 0, 0, 0))
    whole = lax.dynamic_update_slice(whole, far[None], (1 - span, 0, 0, 0))
    return whole.reshape(4 * rows, width)


def per_device(
    tokens,
    cotangent,
    quarter_ids,
    labels,
    timesteps,
    qkv_weight,
    qkv_moment,
    qkv_second,
    qkv_average,
    proj_weight,
    proj_moment,
    proj_second,
    proj_average,
    up_weight,
    up_moment,
    up_second,
    up_average,
    down_weight,
    down_moment,
    down_second,
    down_average,
    ada_weight,
    ada_moment,
    ada_second,
    ada_average,
    table_weight,
    table_moment,
    table_second,
    table_average,
):
    row_count, width = tokens.shape
    slot_count = quarter_ids.shape[0]
    small_len = row_count // slot_count
    span_len = row_count // 2
    own_len = row_count // 4
    shard_rows, _, quarter_width = qkv_weight.shape
    heads = quarter_width // HD
    tp_place = lax.axis_index("tp")
    dp_place = lax.axis_index("dp")
    span = tp_place // 2
    side = tp_place % 2

    attn_block = jnp.concatenate(
        [qkv_weight[:, 0], qkv_weight[:, 1], qkv_weight[:, 2], proj_weight.T], axis=1
    ).astype(BF16)
    w_attn = gather_rows(attn_block)
    w_up = gather_rows(up_weight.astype(BF16))
    w_down = gather_rows(down_weight.T.astype(BF16))
    w_qkv = w_attn[:, :, : 3 * quarter_width]
    w_proj = w_attn[:, :, 3 * quarter_width :]

    marks = lax.all_gather(jnp.stack([labels, timesteps]), "dp", axis=1, tiled=True)
    class_onehot = (
        marks[0][:, None] == jnp.arange(table_weight.shape[0], dtype=jnp.int32)[None, :]
    )
    stamps = time_embed(marks[1], width)
    embed = jnp.dot(
        class_onehot.astype(BF16), table_weight.astype(BF16), preferred_element_type=F32
    ) + lax.dynamic_slice_in_dim(stamps, dp_place * shard_rows, shard_rows, 1)
    cond_low = jax.nn.silu(embed).astype(BF16)
    w_ada = ada_weight.astype(BF16)
    mod_part = jnp.einsum("qd,dke->qke", cond_low, w_ada, preferred_element_type=F32)
    mod_part = lax.psum_scatter(mod_part, "dp", scatter_dimension=0, tiled=True)
    modulation = lax.all_gather(mod_part, "tp", axis=2, tiled=True)
    slot_base = dp_place * slot_count
    choose = (
        quarter_ids[:, None] - slot_base == jnp.arange(slot_count, dtype=jnp.int32)[None, :]
    ).astype(F32)
    quarter_mod = jnp.einsum("ps,ske->pke", choose, modulation, precision=HIGHEST)

    def own_first(array, size):
        mine = lax.dynamic_slice_in_dim(array, (span * 2 + side) * size, size, 0)
        other = lax.dynamic_slice_in_dim(array, (span * 2 + 1 - side) * size, size, 0)
        return jnp.concatenate([mine, other], axis=0)

    quarters = slot_count // 4
    mods = own_first(quarter_mod, quarters)
    ids = own_first(quarter_ids, quarters)
    rows = own_first(tokens, own_len)
    grad_rows = own_first(cotangent, own_len)

    def per_token(index, count):
        return mods[:count, index][:, None, :]

    def blocks(array):
        return array.reshape(-1, small_len, width)

    rows_in = blocks(rows.astype(F32))
    hat, rstd = norm_parts(rows_in)
    first_in = (hat * (1.0 + per_token(1, None)) + per_token(0, None)).astype(BF16)
    first_in = first_in.reshape(span_len, width)
    qkv = jnp.einsum("nd,ydc->ycn", first_in, w_qkv, preferred_element_type=F32).astype(BF16)
    qkv = qkv.reshape(2, 3, heads, HD, span_len)
    head_out, log_total = attend(qkv, ids, small_len)
    attended = head_out.reshape(2, quarter_width, span_len)
    branch_part = jnp.einsum("ycn,ydc->nd", attended, w_proj, preferred_element_type=F32)
    branch = branch_part[:own_len] + swap(branch_part[own_len:].astype(BF16), "tp", 1)
    branch = blocks(branch)

    own_grad = blocks(grad_rows[:own_len].astype(F32))
    middle = blocks(rows[:own_len].astype(F32)) + per_token(2, quarters) * branch
    hat_two, rstd_two = norm_parts(middle)
    own_second = hat_two * (1.0 + per_token(4, quarters)) + per_token(3, quarters)
    own_second = own_second.astype(BF16).reshape(own_len, width)
    second_in = jnp.concatenate([own_second, swap(own_second, "tp", 1)], axis=0)
    grad_mixed = (blocks(grad_rows.astype(F32)) * per_token(5, None)).astype(BF16)
    grad_mixed = grad_mixed.reshape(span_len, width)
    hidden = jnp.einsum("nd,ydf->nyf", second_in, w_up, preferred_element_type=F32)
    active, gelu_back = jax.vjp(lambda v: jax.nn.gelu(v, approximate=True), hidden)
    active = active.astype(BF16)
    mixed_part = jnp.einsum("nyf,ydf->nd", active, w_down, preferred_element_type=F32)
    mixed = mixed_part[:own_len] + swap(mixed_part[own_len:].astype(BF16), "tp", 1)
    mixed = blocks(mixed)
    block_out = (middle + per_token(5, quarters) * mixed).astype(BF16).reshape(own_len, width)
    block_out = spread_rows(block_out, own_len)
    grad_gate_two = jnp.sum(own_grad * mixed, axis=1)
    grad_active = jnp.einsum("nd,ydf->nyf", grad_mixed, w_down, preferred_element_type=F32)
    grad_hidden = gelu_back(grad_active)[0].astype(BF16)
    grad_down = jnp.einsum("nyf,nd->ydf", active, grad_mixed, preferred_element_type=F32)
    grad_up = jnp.einsum("nd,nyf->ydf", second_in, grad_hidden, preferred_element_type=F32)
    back_part = jnp.einsum("nyf,ydf->nd", grad_hidden, w_up, preferred_element_type=F32)
    grad_second = back_part[:own_len] + swap(back_part[own_len:].astype(BF16), "tp", 1)
    grad_second = blocks(grad_second)
    grad_shift_two = jnp.sum(grad_second, axis=1)
    grad_scale_two = jnp.sum(grad_second * hat_two, axis=1)
    grad_middle = own_grad + norm_back(
        hat_two, rstd_two, grad_second * (1.0 + per_token(4, quarters))
    )
    grad_gate_one = jnp.sum(grad_middle * branch, axis=1)

    own_branch = (grad_middle * per_token(2, quarters)).astype(BF16).reshape(own_len, width)
    grad_branch = jnp.concatenate([own_branch, swap(own_branch, "tp", 1)], axis=0)
    grad_proj = jnp.einsum("nd,ycn->ydc", grad_branch, attended, preferred_element_type=F32)
    grad_heads = jnp.einsum("nd,ydc->ycn", grad_branch, w_proj, preferred_element_type=F32)
    grad_heads = grad_heads.astype(BF16).reshape(2 * heads, HD, span_len)
    grad_qkv = attend_back(qkv, ids, grad_heads, head_out, log_total, small_len)
    grad_qkv = grad_qkv.reshape(2, 3 * quarter_width, span_len)
    grad_qkv_w = jnp.einsum("nd,ycn->ydc", first_in, grad_qkv, preferred_element_type=F32)
    first_part = jnp.einsum("ycn,ydc->nd", grad_qkv, w_qkv, preferred_element_type=F32)
    grad_first = first_part[:own_len] + swap(first_part[own_len:].astype(BF16), "tp", 1)
    grad_first = blocks(grad_first)
    own_hat = hat[:quarters]
    grad_shift_one = jnp.sum(grad_first, axis=1)
    grad_scale_one = jnp.sum(grad_first * own_hat, axis=1)
    token_grad = grad_middle + norm_back(
        own_hat, rstd[:quarters], grad_first * (1.0 + per_token(1, quarters))
    )
    token_grad = spread_rows(token_grad.astype(BF16).reshape(own_len, width), own_len)

    grad_quarter = jnp.stack(
        [
            grad_shift_one,
            grad_scale_one,
            grad_gate_one,
            grad_shift_two,
            grad_scale_two,
            grad_gate_two,
        ],
        axis=1,
    )
    grad_quarter = lax.all_gather(grad_quarter, "tp", axis=0, tiled=True)
    grad_quarter = lax.dynamic_slice_in_dim(
        grad_quarter, tp_place * quarter_width, quarter_width, 2
    )
    grad_mod = jnp.einsum("ps,pke->ske", choose, grad_quarter, precision=HIGHEST).astype(BF16)
    grad_mod = lax.all_gather(grad_mod, "dp", axis=0, tiled=True)
    grad_ada = jnp.einsum("qd,qke->dke", cond_low, grad_mod, preferred_element_type=F32)
    grad_cond = lax.psum(
        jnp.einsum("qke,dke->qd", grad_mod, w_ada, preferred_element_type=F32), "tp"
    )
    unused, silu_back = jax.vjp(jax.nn.silu, embed)
    grad_embed = silu_back(grad_cond)[0]
    grad_table = jnp.einsum("qc,qd->cd", class_onehot.astype(F32), grad_embed, precision=HIGHEST)

    up_reduced = scatter_rows(grad_up)
    down_reduced = scatter_rows(grad_down).T
    attn_reduced = scatter_rows(jnp.concatenate([grad_qkv_w, grad_proj], axis=2))
    qkv_reduced = attn_reduced[:, : 3 * quarter_width].reshape(shard_rows, 3, quarter_width)
    proj_reduced = attn_reduced[:, 3 * quarter_width :].T

    local_squares = (
        jnp.sum(attn_reduced * attn_reduced)
        + jnp.sum(up_reduced * up_reduced)
        + jnp.sum(down_reduced * down_reduced)
        + jnp.sum(grad_ada * grad_ada)
        + jnp.sum(grad_table * grad_table) / lax.axis_size("tp")
    )
    grad_norm = jnp.sqrt(lax.psum(local_squares, ("tp", "dp")))
    factor = jnp.minimum(1.0, clip_limit / (grad_norm + 1e-06))
    qkv_new = adam_step(
        qkv_weight, qkv_moment, qkv_second, qkv_average, qkv_reduced * factor, 0.5 * D ** (-0.5)
    )
    proj_new = adam_step(
        proj_weight,
        proj_moment,
        proj_second,
        proj_average,
        proj_reduced * factor,
        4.0 * D ** (-0.5),
    )
    up_new = adam_step(
        up_weight, up_moment, up_second, up_average, up_reduced * factor, 0.5 * D ** (-0.5)
    )
    down_new = adam_step(
        down_weight,
        down_moment,
        down_second,
        down_average,
        down_reduced * factor,
        0.5 * FF ** (-0.5),
    )
    ada_new = adam_step(
        ada_weight, ada_moment, ada_second, ada_average, grad_ada * factor, 0.5 * D ** (-0.5)
    )
    table_new = adam_step(
        table_weight, table_moment, table_second, table_average, grad_table * factor, 0.5
    )
    return (
        block_out,
        token_grad,
        grad_norm,
        *qkv_new,
        *proj_new,
        *up_new,
        *down_new,
        *ada_new,
        *table_new,
    )


def solution(mesh):
    rows = P("dp", None)
    marks = P("dp")
    cubes = (P("dp", None, "tp"),) * 4
    across = (P("tp", "dp"),) * 4
    along = (P("dp", "tp"),) * 4
    table = (P(None, "dp"),) * 4
    states = (*cubes, *across, *along, *across, *cubes, *table)
    return jax.shard_map(
        per_device,
        mesh=mesh,
        in_specs=(rows, rows, marks, marks, marks, *states),
        out_specs=(rows, rows, P(), *states),
        check_vma=False,
    )
```

time: 1610 us -> 879 us (0.55)
  waiting for transfers between devices: 986 us -> 161 us
  matrix products: 227 us -> 99.2 us
  blocking collectives: 124 us -> 227 us
  starting transfers between devices: 1.41 us -> 94.8 us
  other arithmetic: 189 us -> 117 us
  Pallas kernels: 0 us -> 51.8 us
  local copies, waits for them, and re-layouts: 59 us -> 99 us
    psum x4 -> x0, waiting for transfers between devices: 595 us -> none  [the longest x1 175 us: per_device(): grad_second = lax.psum(second_back, 'tp')]
    reduce_scatter x6 -> x1, waiting for transfers between devices: 316 us -> 0.01 us  [per_device(): mod_part = lax.psum_scatter(mod_part, 'dp', scatter_dimension=0, tiled=True)]
    ppermute x0 -> x49, waiting for transfers between devices: none -> 161 us  [the longest x31 137 us: swap(): return lax.ppermute(value, axis, [(i, i ^ bit) for i in range(count)])]
    dot_general x31 -> x17, matrix products: 226 us -> 98.1 us  [the longest x1 12.4 us: per_device(): jnp.einsum('nd,nyf->ydf', second_in, grad_hidden, preferred_element_type=...]
    ppermute x0 -> x49, starting transfers between devices: none -> 94.8 us  [the longest x18 68.5 us: shift(): lax.ppermute(value, 'dp', [(i, (i + 2 * steps) % count) for i in range(co...]
    all_gather x5 -> x0, waiting for transfers between devices: 74.3 us -> none  [the longest x1 55.6 us: per_device(): lax.all_gather(ada_weight.astype(bf16), 'dp', axis=0, tiled=True)]
    reduce_sum x15 -> x10, other arithmetic: 89.1 us -> 17.2 us  [the longest x1 4.65 us: per_device(): grad_scale_two = jnp.sum(grad_second * hat_two, axis=1)]
    all_gather x1 -> x3, blocking collectives: 24.1 us -> 90.6 us  [the longest x1 49.3 us: per_device(): grad_quarter = lax.all_gather(grad_quarter, 'tp', axis=0, tiled=True)]
  transfers between devices with their start and end apart: 15 -> 50, of which waited for: 13 -> 18; matrix products, arithmetic and copies ran while one was open for 15% -> 28% of each run, Pallas kernels for 0% -> 6%
where the time goes in v1:
time: 879 us; the launch traced here: 871 us
  blocking collectives  227 us (26%)
  waiting for transfers between devices  161 us (18%)
  other arithmetic  117 us (13%)
  matrix products  99.2 us (11%)
  local copies, waits for them, and re-layouts  99 us (11%)
  starting transfers between devices  94.8 us (11%)
  Pallas kernels  51.8 us (6%)
  between operations  21 us (2%)
    ppermute x31, waiting for transfers between devices, swap(): return lax.ppermute(value, axis, [(i, i ^ bit) for i in range(count)])  137 us
    psum x1, blocking collectives, per_device(): grad_norm = jnp.sqrt(lax.psum(local_squares, ('tp', 'dp')))  74.2 us
    ppermute x18, starting transfers between devices, shift(): lax.ppermute(value, 'dp', [(i, (i + 2 * steps) % count) for i in range(co...  68.5 us
    all_gather x1, blocking collectives, per_device(): grad_quarter = lax.all_gather(grad_quarter, 'tp', axis=0, tiled=True)  49.3 us
    all_gather x1, blocking collectives, per_device(): modulation = lax.all_gather(mod_part, 'tp', axis=2, tiled=True)  45.9 us
    pallas_call x1, Pallas kernels, attend_back(): pl.pallas_call(functools.partial(attend_back_whole, small_len), grid=(pai...  26.8 us
    ppermute x31, starting transfers between devices, swap(): return lax.ppermute(value, axis, [(i, i ^ bit) for i in range(count)])  26.3 us
    pallas_call x1, Pallas kernels, attend(): pl.pallas_call(functools.partial(attend_kernel, small_len), grid=(pair *...  25 us
  transfers between devices with their start and end apart: 50, of which 18 were waited for; matrix products, arithmetic and copies ran while one was open for 28% of the time, Pallas kernels for 6%

profile of v1, /device:TPU:0, one launch (start us, length us, event | category | flops | bytes accessed | tf_op | source)
XLA Modules:
  0.0 870.8 jit_solution(10262067102993047118)
XLA Ops:
  20.8 21.0 %all-gather = s32[8,8,2]{1,2,0:T(2,128)S(1)} all-gather(s32[1,8,2]{1,2,0:T(2,128)S(1)} %add_bitcast_fusion), channel_id=1, replica_groups=mesh['tp'=4,'dp'=8] {'dp'}, dimensions={0}, use_global_device_ids=true | all-gather | bytes 576 | tf_op jit(solution)/shard_map/all_gather | solution.py:293
  90.1 19.7 %collective-permute-start.15 = (bf16[144,1152]{1,0:T(8,128)(2,1)S(1)}, bf16[144,1152]{1,0:T(8,128)(2,1)S(1)}, u32[]{:S(2)}, u32[]{:S(2)}) collective-permute-start(bf16[144,1152]{1,0:T(8,128)(2,1)S(1)} %copy-done.49), channel_id=1, source_target_pairs={{0,6},{1,7},{2,0},{3,1},{4,2},{5,3},{6,4},{7,5},{8,14},{9,15},{10,... | collective-permute-start | bytes 995336 | tf_op jit(solution)/shard_map/ppermute | solution.py:187
  147.7 45.9 %all_gather.13 = f32[8,6,1152]{1,0,2:T(8,128)} all-gather(f32[8,6,288]{1,0,2:T(8,128)S(1)} %copy.141), channel_id=1, replica_groups=mesh['tp'=4,'dp'=8] {'tp'}, dimensions={2}, use_global_device_ids=true | all-gather | bytes 276480 | tf_op jit(solution)/shard_map/all_gather | solution.py:305
  209.7 25.0 %shard_map.484 = (bf16[8,72,1024]{2,1,0:T(8,128)(2,1)S(1)}, f32[8,1,1024]{2,1,0:T(1,128)S(1)}) custom-call(s32[4]{0:T(128)S(1)} %pad_add_fusion.ids_ref.ids, bf16[2,3,4,72,1024]{4,3,2,1,0:T(8,128)(2,1)S(1)} %bitcast.405, bf16[2,3,4,72,1024]{4,3,2,1,0:T(8,128)(2,1)S(1)} %bitcast.406, bf16[2,3,4,72,1024]{4,3,2,1,0:T(8,128)(2,1)S(1)} %bitcast.407), custom_call_target="tpu_custom_call" | custom-call | tf_op jit(solution)/shard_map/pallas_call | solution.py:77
  243.4 21.8 %collective-permute-done.8 = bf16[512,1152]{1,0:T(8,128)(2,1)S(1)} collective-permute-done((bf16[512,1152]{1,0:T(8,128)(2,1)S(1)}, bf16[512,1152]{1,0:T(8,128)(2,1)S(1)}, u32[]{:S(2)}, u32[]{:S(2)}) %collective-permute-start.8) | collective-permute-done | bytes 1179680 | tf_op jit(solution)/shard_map/ppermute | solution.py:182
  275.4 19.3 %collective-permute-done.9 = bf16[512,1152]{1,0:T(8,128)(2,1)S(1)} collective-permute-done((bf16[512,1152]{1,0:T(8,128)(2,1)S(1)}, bf16[512,1152]{1,0:T(8,128)(2,1)S(1)}, u32[]{:S(2)}, u32[]{:S(2)}) %collective-permute-start.9) | collective-permute-done | bytes 1179680 | tf_op jit(solution)/shard_map/ppermute | solution.py:182
  295.6 9.5 %fusion.41 = f32[1024,2,1152]{2,0,1:T(8,128)S(1)} fusion(bf16[2,1152,1152]{2,1,0:T(8,128)(2,1)} %bitcast.447, bf16[512,1152]{1,0:T(8,128)(2,1)} %copy-done.79, bf16[512,1152]{1,0:T(8,128)(2,1)} %copy-done.36), kind=kOutput, calls=%fused_computation.113 | convolution fusion | flops 5440536576 | bytes 17104896 | tf_op jit(solution)/shard_map/nd,ydf->nyf/dot_general | solution.py:349
  305.2 9.8 %convolution_bitcast_fusion.4 = f32[1024,1152]{1,0:T(8,128)} fusion(bf16[2,1152,1152]{2,1,0:T(8,128)(2,1)S(1)} %bitcast.443, f32[1024,2,1152]{2,0,1:T(8,128)S(1)} %fusion.41), kind=kOutput, calls=%fused_computation.33 | convolution fusion | flops 5457051648 | bytes 19464192 | tf_op jit(solution)/shard_map/nyf,ydf->nd/dot_general | solution.py:352
  328.2 15.3 %collective-permute-done.26 = bf16[512,1152]{1,0:T(8,128)(2,1)} collective-permute-done((bf16[512,1152]{1,0:T(8,128)(2,1)}, bf16[512,1152]{1,0:T(8,128)(2,1)}, u32[]{:S(2)}, u32[]{:S(2)}) %collective-permute-start.26) | collective-permute-done | bytes 1179680 | tf_op jit(solution)/shard_map/ppermute | solution.py:182
  351.2 11.1 %fusion.6 = bf16[1024,2,1152]{2,0,1:T(8,128)(2,1)} fusion(f32[1024,2,1152]{2,0,1:T(8,128)S(1)} %bitcast.432, bf16[1024,1152,1]{1,0,2:T(8,128)(2,1)S(1)} %bitcast.459, bf16[2,1152,1152]{2,1,0:T(8,128)(2,1)S(1)} %bitcast.446), kind=kOutput, calls=%fused_computation.9 | convolution fusion | flops 5483003904 | bytes 21823488 | tf_op jit(solution)/shard_map/nd,ydf->nyf/dot_general | solution.py:358
  362.2 9.7 %convolution_bitcast_fusion.3 = f32[1024,1152]{1,0:T(8,128)S(1)} fusion(bf16[1024,2,1152]{2,0,1:T(8,128)(2,1)} %fusion.6, bf16[2,1152,1152]{2,1,0:T(8,128)(2,1)} %bitcast.448), kind=kOutput, calls=%fused_computation.32 | convolution fusion | flops 5435817984 | bytes 14745600 | tf_op jit(solution)/shard_map/nyf,ydf->nd/dot_general | solution.py:362
  384.8 12.4 %fusion.40 = f32[2,1152,1152]{1,2,0:T(8,128)} fusion(bf16[1024,2,1152]{2,0,1:T(8,128)(2,1)} %fusion.6, bf16[512,1152]{1,0:T(8,128)(2,1)S(1)} %copy-done.80, bf16[512,1152]{1,0:T(8,128)(2,1)S(1)} %copy-done.37), kind=kOutput, calls=%fused_computation.112 | convolution fusion | flops 5440536576 | bytes 17694720 | tf_op jit(solution)/shard_map/nd,nyf->ydf/dot_general | solution.py:361
  417.9 12.1 %collective-permute-done.30 = bf16[512,1152]{1,0:T(8,128)(2,1)} collective-permute-done((bf16[512,1152]{1,0:T(8,128)(2,1)}, bf16[512,1152]{1,0:T(8,128)(2,1)}, u32[]{:S(2)}, u32[]{:S(2)}) %collective-permute-start.30) | collective-permute-done | bytes 1179680 | tf_op jit(solution)/shard_map/ppermute | solution.py:182
  435.0 26.8 %shard_map.485 = bf16[2,3,4,72,1024]{4,3,2,1,0:T(8,128)(2,1)S(1)} custom-call(s32[4]{0:T(128)S(1)} %pad_add_fusion.ids_ref.ids, bf16[2,3,4,72,1024]{4,3,2,1,0:T(8,128)(2,1)} %bitcast.408, bf16[2,3,4,72,1024]{4,3,2,1,0:T(8,128)(2,1)} %bitcast.409, bf16[2,3,4,72,1024]{4,3,2,1,0:T(8,128)(2,1)} %bitcast.410, bf16[8,72,1024]{2,1,0:T(8,128)(2,1)S(1)} %bitcast.415, ...), custom_call_target="tpu_custom_call" | custom-call | tf_op jit(solution)/shard_map/pallas_call | solution.py:148
  490.7 12.8 %copy.158 = f32[2,1152,1152]{2,1,0:T(8,128)} copy(f32[2,1152,1152]{1,2,0:T(8,128)} %pad_maximum_fusion) | data formatting | bytes 21233664 | tf_op jit(solution)/shard_map/concatenate | solution.py:418
  536.3 49.3 %all_gather.14 = f32[8,6,1152]{2,1,0:T(8,128)S(1)} all-gather(f32[2,6,1152]{2,1,0:T(8,128)S(1)} %stack.216), channel_id=1, replica_groups=mesh['tp'=4,'dp'=8] {'tp'}, dimensions={0}, use_global_device_ids=true | all-gather | bytes 276480 | tf_op jit(solution)/shard_map/all_gather | solution.py:402
  586.5 20.3 %all_gather.15 = bf16[64,6,288]{2,0,1:T(8,128)(2,1)S(1)} all-gather(bf16[8,6,288]{2,0,1:T(8,128)(2,1)S(1)} %convolution_convert_fusion), channel_id=1, replica_groups=mesh['tp'=4,'dp'=8] {'dp'}, dimensions={0}, use_global_device_ids=true | all-gather | bytes 248832 | tf_op jit(solution)/shard_map/all_gather | solution.py:407
  609.2 16.7 %psum.14 = f32[64,144]{1,0:T(8,128)} all-reduce(f32[64,144]{1,0:T(8,128)S(1)} %convolution_bitcast_fusion.6), channel_id=1, replica_groups=mesh['tp'=4,'dp'=8] {'tp'}, use_global_device_ids=true, to_apply=%region_19.20 | all-reduce | flops 9216 | bytes 73728 | tf_op jit(solution)/shard_map/psum | solution.py:409
  647.6 11.7 %collective-permute-start.42 = (bf16[144,1152]{1,0:T(8,128)(2,1)}, bf16[144,1152]{1,0:T(8,128)(2,1)}, u32[]{:S(2)}, u32[]{:S(2)}) collective-permute-start(bf16[144,1152]{1,0:T(8,128)(2,1)} %get-tuple-element.157), channel_id=1, source_target_pairs={{0,4},{1,5},{2,6},{3,7},{4,0},{5,1},{6,2},{7,3},{8,12},{9,13},{10,... | collective-permute-start | bytes 995336 | tf_op jit(solution)/shard_map/ppermute | solution.py:187
  665.3 11.7 %collective-permute-start.43 = (bf16[144,1152]{1,0:T(8,128)(2,1)}, bf16[144,1152]{1,0:T(8,128)(2,1)}, u32[]{:S(2)}, u32[]{:S(2)}) collective-permute-start(bf16[144,1152]{1,0:T(8,128)(2,1)} %get-tuple-element.156), channel_id=1, source_target_pairs={{0,6},{1,7},{2,0},{3,1},{4,2},{5,3},{6,4},{7,5},{8,14},{9,15},{10,... | collective-permute-start | bytes 995336 | tf_op jit(solution)/shard_map/ppermute | solution.py:187
  691.4 18.1 %collective-permute-done.35 = bf16[4,144,1152]{2,1,0:T(8,128)(2,1)} collective-permute-done((bf16[4,144,1152]{2,1,0:T(8,128)(2,1)}, bf16[4,144,1152]{2,1,0:T(8,128)(2,1)}, u32[]{:S(2)}, u32[]{:S(2)}) %collective-permute-start.35) | collective-permute-done | bytes 1327136 | tf_op jit(solution)/shard_map/ppermute | solution.py:182
  720.3 10.0 %collective-permute-done.37 = bf16[144,1152]{1,0:T(8,128)(2,1)S(1)} collective-permute-done((bf16[144,1152]{1,0:T(8,128)(2,1)S(1)}, bf16[144,1152]{1,0:T(8,128)(2,1)S(1)}, u32[]{:S(2)}, u32[]{:S(2)}) %collective-permute-start.37) | collective-permute-done | bytes 331808 | tf_op jit(solution)/shard_map/ppermute | solution.py:187
  733.7 26.3 %collective-permute-done.28 = bf16[2,512,1152]{2,1,0:T(8,128)(2,1)} collective-permute-done((bf16[2,512,1152]{2,1,0:T(8,128)(2,1)}, bf16[2,512,1152]{2,1,0:T(8,128)(2,1)}, u32[]{:S(2)}, u32[]{:S(2)}) %collective-permute-start.28) | collective-permute-done | bytes 2359328 | tf_op jit(solution)/shard_map/ppermute | solution.py:182
  763.2 74.2 %psum.15 = f32[]{:T(128)} all-reduce(f32[]{:T(128)S(6)} %add.567), channel_id=1, replica_groups=mesh['tp'=4,'dp'=8] {'tp','dp'}, use_global_device_ids=true, to_apply=%region_21.22 | all-reduce | flops 1 | bytes 8 | tf_op jit(solution)/shard_map/psum | solution.py:429
  (461 shorter events, 339.7 us)
Async XLA Ops:
  7.3 139.1 %reduce-scatter.2.cloned.1.call-start = ((), (), s32[]{:S(2)}) async-start(), calls=%async_computation.1 | async-start | bytes 663552 | tf_op jit(solution)/shard_map/reduce_scatter | solution.py:304
  9.3 45.5 %collective-permute-start.18 = (bf16[144,1152]{1,0:T(8,128)(2,1)}, bf16[144,1152]{1,0:T(8,128)(2,1)}, u32[]{:S(2)}, u32[]{:S(2)}) collective-permute-start(bf16[144,1152]{1,0:T(8,128)(2,1)} %get-tuple-element.162), channel_id=1, source_target_pairs={{0,16},{8,24},{16,0},{24,8},{1,17},{9,25},{17,1},{25,9},{2,18},{10... | collective-permute-start | bytes 995336 | tf_op jit(solution)/shard_map/ppermute | solution.py:182
  12.3 67.4 %collective-permute-start.19 = (bf16[144,1152]{1,0:T(8,128)(2,1)}, bf16[144,1152]{1,0:T(8,128)(2,1)}, u32[]{:S(2)}, u32[]{:S(2)}) collective-permute-start(bf16[144,1152]{1,0:T(8,128)(2,1)} %get-tuple-element.162), channel_id=1, source_target_pairs={{0,2},{1,3},{2,4},{3,5},{4,6},{5,7},{6,0},{7,1},{8,10},{9,11},{10,... | collective-permute-start | bytes 995336 | tf_op jit(solution)/shard_map/ppermute | solution.py:187
  17.7 49.0 %collective-permute-start = (bf16[144,1152]{1,0:T(8,128)(2,1)}, bf16[144,1152]{1,0:T(8,128)(2,1)}, u32[]{:S(2)}, u32[]{:S(2)}) collective-permute-start(bf16[144,1152]{1,0:T(8,128)(2,1)} %concatenate.53), channel_id=1, source_target_pairs={{0,16},{8,24},{16,0},{24,8},{1,17},{9,25},{17,1},{25,9},{2,18},{10... | collective-permute-start | bytes 995336 | tf_op jit(solution)/shard_map/ppermute | solution.py:182
  18.2 44.4 %collective-permute-start.1 = (bf16[144,1152]{1,0:T(8,128)(2,1)}, bf16[144,1152]{1,0:T(8,128)(2,1)}, u32[]{:S(2)}, u32[]{:S(2)}) collective-permute-start(bf16[144,1152]{1,0:T(8,128)(2,1)} %concatenate.53), channel_id=1, source_target_pairs={{0,2},{1,3},{2,4},{3,5},{4,6},{5,7},{6,0},{7,1},{8,10},{9,11},{10,... | collective-permute-start | bytes 995336 | tf_op jit(solution)/shard_map/ppermute | solution.py:187
  19.8 46.9 %collective-permute-start.3 = (bf16[144,1152]{1,0:T(8,128)(2,1)}, bf16[144,1152]{1,0:T(8,128)(2,1)}, u32[]{:S(2)}, u32[]{:S(2)}) collective-permute-start(bf16[144,1152]{1,0:T(8,128)(2,1)} %concatenate.53), channel_id=1, source_target_pairs={{0,4},{1,5},{2,6},{3,7},{4,0},{5,1},{6,2},{7,3},{8,12},{9,13},{10,... | collective-permute-start | bytes 995336 | tf_op jit(solution)/shard_map/ppermute | solution.py:187
  110.8 89.7 %collective-permute-start.7 = (bf16[2,4,144,1152]{3,2,1,0:T(8,128)(2,1)}, bf16[2,4,144,1152]{3,2,1,0:T(8,128)(2,1)}, u32[]{:S(2)}, u32[]{:S(2)}) collective-permute-start(bf16[2,4,144,1152]{3,2,1,0:T(8,128)(2,1)} %fusion.52), channel_id=1, source_target_pairs={{0,1},{1,0},{2,3},{3,2},{4,5},{5,4},{6,7},{7,6},{8,9},{9,8},{10,11... | collective-permute-start | bytes 7962632 | tf_op jit(solution)/shard_map/ppermute | solution.py:182
  125.1 113.6 %collective-permute-start.25 = (bf16[2,4,144,1152]{3,2,1,0:T(8,128)(2,1)}, bf16[2,4,144,1152]{3,2,1,0:T(8,128)(2,1)}, u32[]{:S(2)}, u32[]{:S(2)}) collective-permute-start(bf16[2,4,144,1152]{3,2,1,0:T(8,128)(2,1)} %fusion.60), channel_id=1, source_target_pairs={{0,1},{1,0},{2,3},{3,2},{4,5},{5,4},{6,7},{7,6},{8,9},{9,8},{10,11... | collective-permute-start | bytes 7962632 | tf_op jit(solution)/shard_map/ppermute | solution.py:182
  146.3 122.7 %collective-permute-start.17 = (bf16[2,4,144,1152]{3,2,1,0:T(8,128)(2,1)}, bf16[2,4,144,1152]{3,2,1,0:T(8,128)(2,1)}, u32[]{:S(2)}, u32[]{:S(2)}) collective-permute-start(bf16[2,4,144,1152]{3,2,1,0:T(8,128)(2,1)} %fusion.56), channel_id=1, source_target_pairs={{0,1},{1,0},{2,3},{3,2},{4,5},{5,4},{6,7},{7,6},{8,9},{9,8},{10,11... | collective-permute-start | bytes 7962632 | tf_op jit(solution)/shard_map/ppermute | solution.py:182
  384.0 128.5 %collective-permute-start.44 = (bf16[2,4,144,1152]{3,2,1,0:T(8,128)(2,1)}, bf16[2,4,144,1152]{3,2,1,0:T(8,128)(2,1)}, u32[]{:S(2)}, u32[]{:S(2)}) collective-permute-start(bf16[2,4,144,1152]{3,2,1,0:T(8,128)(2,1)} %fusion.14), channel_id=1, source_target_pairs={{0,1},{1,0},{2,3},{3,2},{4,5},{5,4},{6,7},{7,6},{8,9},{9,8},{10,11... | collective-permute-start | bytes 7962632 | tf_op jit(solution)/shard_map/ppermute | solution.py:182
  406.7 115.5 %collective-permute-start.39 = (bf16[2,4,144,1152]{3,2,1,0:T(8,128)(2,1)}, bf16[2,4,144,1152]{3,2,1,0:T(8,128)(2,1)}, u32[]{:S(2)}, u32[]{:S(2)}) collective-permute-start(bf16[2,4,144,1152]{3,2,1,0:T(8,128)(2,1)} %fusion.13), channel_id=1, source_target_pairs={{0,1},{1,0},{2,3},{3,2},{4,5},{5,4},{6,7},{7,6},{8,9},{9,8},{10,11... | collective-permute-start | bytes 7962632 | tf_op jit(solution)/shard_map/ppermute | solution.py:182
  415.7 92.1 %collective-permute-start.27 = (bf16[512,1152]{1,0:T(8,128)(2,1)}, bf16[512,1152]{1,0:T(8,128)(2,1)S(1)}, u32[]{:S(2)}, u32[]{:S(2)}) collective-permute-start(bf16[512,1152]{1,0:T(8,128)(2,1)} %get-tuple-element.151), channel_id=1, source_target_pairs={{0,8},{8,0},{16,24},{24,16},{1,9},{9,1},{17,25},{25,17},{2,10},{10... | collective-permute-start | bytes 3538952 | tf_op jit(solution)/shard_map/ppermute | solution.py:182
  468.0 59.3 %collective-permute-start.31 = (bf16[512,1152]{1,0:T(8,128)(2,1)}, bf16[512,1152]{1,0:T(8,128)(2,1)}, u32[]{:S(2)}, u32[]{:S(2)}) collective-permute-start(bf16[512,1152]{1,0:T(8,128)(2,1)} %slice.227), channel_id=1, source_target_pairs={{0,8},{8,0},{16,24},{24,16},{1,9},{9,1},{17,25},{25,17},{2,10},{10... | collective-permute-start | bytes 3538952 | tf_op jit(solution)/shard_map/ppermute | solution.py:182
  507.8 133.3 %collective-permute-start.34 = (bf16[2,4,144,1152]{3,2,1,0:T(8,128)(2,1)}, bf16[2,4,144,1152]{3,2,1,0:T(8,128)(2,1)}, u32[]{:S(2)}, u32[]{:S(2)}) collective-permute-start(bf16[2,4,144,1152]{3,2,1,0:T(8,128)(2,1)} %fusion.12), channel_id=1, source_target_pairs={{0,1},{1,0},{2,3},{3,2},{4,5},{5,4},{6,7},{7,6},{8,9},{9,8},{10,11... | collective-permute-start | bytes 7962632 | tf_op jit(solution)/shard_map/ppermute | solution.py:182
  520.7 108.2 %collective-permute-start.45 = (bf16[4,144,1152]{2,1,0:T(8,128)(2,1)}, bf16[4,144,1152]{2,1,0:T(8,128)(2,1)}, u32[]{:S(2)}, u32[]{:S(2)}) collective-permute-start(bf16[4,144,1152]{2,1,0:T(8,128)(2,1)} %fusion.45), channel_id=1, source_target_pairs={{0,16},{8,24},{16,0},{24,8},{1,17},{9,25},{17,1},{25,9},{2,18},{10... | collective-permute-start | bytes 3981320 | tf_op jit(solution)/shard_map/ppermute | solution.py:182
  526.0 108.2 %collective-permute-start.40 = (bf16[4,144,1152]{2,1,0:T(8,128)(2,1)}, bf16[4,144,1152]{2,1,0:T(8,128)(2,1)}, u32[]{:S(2)}, u32[]{:S(2)}) collective-permute-start(bf16[4,144,1152]{2,1,0:T(8,128)(2,1)} %fusion.44), channel_id=1, source_target_pairs={{0,16},{8,24},{16,0},{24,8},{1,17},{9,25},{17,1},{25,9},{2,18},{10... | collective-permute-start | bytes 3981320 | tf_op jit(solution)/shard_map/ppermute | solution.py:182
  534.5 154.7 %collective-permute-start.32 = (bf16[512,1152]{1,0:T(8,128)(2,1)S(1)}, bf16[512,1152]{1,0:T(8,128)(2,1)}, u32[]{:S(2)}, u32[]{:S(2)}) collective-permute-start(bf16[512,1152]{1,0:T(8,128)(2,1)S(1)} %bitcast.452), channel_id=1, source_target_pairs={{0,8},{8,0},{16,24},{24,16},{1,9},{9,1},{17,25},{25,17},{2,10},{10... | collective-permute-start | bytes 3538952 | tf_op jit(solution)/shard_map/ppermute | solution.py:182
  633.1 32.2 %collective-permute-start.47 = (bf16[144,1152]{1,0:T(8,128)(2,1)S(1)}, bf16[144,1152]{1,0:T(8,128)(2,1)S(1)}, u32[]{:S(2)}, u32[]{:S(2)}) collective-permute-start(bf16[144,1152]{1,0:T(8,128)(2,1)S(1)} %get-tuple-element.154), channel_id=1, source_target_pairs={{0,4},{1,5},{2,6},{3,7},{4,0},{5,1},{6,2},{7,3},{8,12},{9,13},{10,... | collective-permute-start | bytes 995336 | tf_op jit(solution)/shard_map/ppermute | solution.py:187
  634.2 42.9 %collective-permute-start.48 = (bf16[144,1152]{1,0:T(8,128)(2,1)S(1)}, bf16[144,1152]{1,0:T(8,128)(2,1)S(1)}, u32[]{:S(2)}, u32[]{:S(2)}) collective-permute-start(bf16[144,1152]{1,0:T(8,128)(2,1)S(1)} %get-tuple-element.153), channel_id=1, source_target_pairs={{0,6},{1,7},{2,0},{3,1},{4,2},{5,3},{6,4},{7,5},{8,14},{9,15},{10,... | collective-permute-start | bytes 995336 | tf_op jit(solution)/shard_map/ppermute | solution.py:187
  641.1 42.3 %collective-permute-start.41 = (bf16[144,1152]{1,0:T(8,128)(2,1)}, bf16[144,1152]{1,0:T(8,128)(2,1)}, u32[]{:S(2)}, u32[]{:S(2)}) collective-permute-start(bf16[144,1152]{1,0:T(8,128)(2,1)} %get-tuple-element.155), channel_id=1, source_target_pairs={{0,2},{1,3},{2,4},{3,5},{4,6},{5,7},{6,0},{7,1},{8,10},{9,11},{10,... | collective-permute-start | bytes 995336 | tf_op jit(solution)/shard_map/ppermute | solution.py:187
  647.6 37.2 %collective-permute-start.42 = (bf16[144,1152]{1,0:T(8,128)(2,1)}, bf16[144,1152]{1,0:T(8,128)(2,1)}, u32[]{:S(2)}, u32[]{:S(2)}) collective-permute-start(bf16[144,1152]{1,0:T(8,128)(2,1)} %get-tuple-element.157), channel_id=1, source_target_pairs={{0,4},{1,5},{2,6},{3,7},{4,0},{5,1},{6,2},{7,3},{8,12},{9,13},{10,... | collective-permute-start | bytes 995336 | tf_op jit(solution)/shard_map/ppermute | solution.py:187
  677.0 32.4 %collective-permute-start.35 = (bf16[4,144,1152]{2,1,0:T(8,128)(2,1)}, bf16[4,144,1152]{2,1,0:T(8,128)(2,1)}, u32[]{:S(2)}, u32[]{:S(2)}) collective-permute-start(bf16[4,144,1152]{2,1,0:T(8,128)(2,1)} %fusion.43), channel_id=1, source_target_pairs={{0,16},{8,24},{16,0},{24,8},{1,17},{9,25},{17,1},{25,9},{2,18},{10... | collective-permute-start | bytes 3981320 | tf_op jit(solution)/shard_map/ppermute | solution.py:182
  683.4 76.6 %collective-permute-start.28 = (bf16[2,512,1152]{2,1,0:T(8,128)(2,1)}, bf16[2,512,1152]{2,1,0:T(8,128)(2,1)}, u32[]{:S(2)}, u32[]{:S(2)}) collective-permute-start(bf16[2,512,1152]{2,1,0:T(8,128)(2,1)} %copy-done.15), channel_id=1, source_target_pairs={{0,16},{8,24},{16,0},{24,8},{1,17},{9,25},{17,1},{25,9},{2,18},{10... | collective-permute-start | bytes 7077896 | tf_op jit(solution)/shard_map/ppermute | solution.py:182
  690.6 167.6 %collective-permute-start.33 = (bf16[2,512,1152]{2,1,0:T(8,128)(2,1)S(1)}, bf16[2,512,1152]{2,1,0:T(8,128)(2,1)}, u32[]{:S(2)}, u32[]{:S(2)}) collective-permute-start(bf16[2,512,1152]{2,1,0:T(8,128)(2,1)S(1)} %bitcast_dynamic-update-slice_fusion.4), channel_id=1, source_target_pairs={{0,16},{8,24},{16,0},{24,8},{1,17},{9,25},{17,1},{25,9},{2,18},{10... | collective-permute-start | bytes 7077896 | tf_op jit(solution)/shard_map/ppermute | solution.py:182
  (132 other events, 1735.6 us)
Sparse Core Ops, SparseCore 0:
  44.7 37.1 reduce-scatter.1

commit v2 on v1

--- a/solution.py
+++ b/solution.py
@@ -163,6 +163,259 @@
         out_shape=jax.ShapeDtypeStruct((pair, 3, heads, HD, length), BF16),
         compiler_params=pltpu.CompilerParams(vmem_limit_bytes=48 << 20),
     )(ids, qkv, qkv, qkv, grad_out, out, log_total)
+
+MESH = pl.DeviceIdType.MESH
+
+
+def remote(src, dst, send_sem, recv_sem, tp, dp):
+    return pltpu.make_async_remote_copy(
+        src_ref=src,
+        dst_ref=dst,
+        send_sem=send_sem,
+        recv_sem=recv_sem,
+        device_id=(tp, dp),
+        device_id_type=MESH,
+    )
+
+
+def greet(peers):
+    barrier = pltpu.get_barrier_semaphore()
+    for tp, dp in peers:
+        pl.semaphore_signal(barrier, inc=1, device_id=(tp, dp), device_id_type=MESH)
+    pl.semaphore_wait(barrier, len(peers))
+
+
+def other_core(dp):
+    return dp + 1 - 2 * lax.rem(dp, 2)
+
+
+def x_neighbour(tp):
+    return tp + 1 - 2 * lax.rem(tp, 2)
+
+
+def y_neighbour(tp):
+    return lax.rem(tp + 2, 4)
+
+
+class GatherRows:
+    def __init__(self, block, whole, sems, planes):
+        self.block, self.whole, self.planes = block, whole, planes
+        self.local, self.sends, self.recvs = sems
+        self.tp, self.dp = lax.axis_index("tp"), lax.axis_index("dp")
+        self.core = lax.rem(self.dp, 2)
+        self.place = lax.div(self.dp, 2)
+
+    def at(self, quarter, step):
+        place = lax.rem(self.place - step + self.planes, self.planes)
+        return self.whole.at[quarter, place, self.core]
+
+    def along(self, step):
+        count = 2 * self.planes
+        dp = lax.rem(self.dp + 2 * step, count)
+        return remote(
+            self.block, self.at(0, 0), self.sends.at[step], self.recvs.at[step], self.tp, dp
+        )
+
+    def across(self, step):
+        place = self.planes + step
+        src = self.block if step == 0 else self.at(0, step)
+        return remote(
+            src,
+            self.at(1, step),
+            self.sends.at[place],
+            self.recvs.at[place],
+            y_neighbour(self.tp),
+            self.dp,
+        )
+
+    def over(self, quarter, step):
+        place = (2 + quarter) * self.planes + step
+        src = self.block if quarter == 0 and step == 0 else self.at(quarter, step)
+        return remote(
+            src,
+            self.at(quarter, step),
+            self.sends.at[place],
+            self.recvs.at[place],
+            self.tp,
+            other_core(self.dp),
+        )
+
+    def own(self):
+        return pltpu.make_async_copy(self.block, self.at(0, 0), self.local)
+
+    def start(self):
+        self.own().start()
+        for step in range(1, self.planes):
+            self.along(step).start()
+        self.across(0).start()
+        self.over(0, 0).start()
+
+    def relay(self):
+        for step in range(self.planes):
+            if step > 0:
+                self.along(step).wait_recv()
+                self.across(step).start()
+                self.over(0, step).start()
+        for step in range(self.planes):
+            self.across(step).wait_recv()
+            self.over(1, step).start()
+
+    def finish(self):
+        self.own().wait()
+        for step in range(self.planes):
+            if step > 0:
+                self.along(step).wait_send()
+            self.across(step).wait_send()
+            for quarter in range(2):
+                self.over(quarter, step).wait_send()
+                self.over(quarter, step).wait_recv()
+
+
+def gather_sems(planes):
+    return [
+        pltpu.SemaphoreType.DMA,
+        pltpu.SemaphoreType.DMA((4 * planes,)),
+        pltpu.SemaphoreType.DMA((4 * planes,)),
+    ]
+
+
+def front_kernel(
+    planes,
+    marks_ref,
+    freqs_ref,
+    table_ref,
+    ada_ref,
+    attn_ref,
+    up_ref,
+    down_ref,
+    mods_ref,
+    marks_all_ref,
+    embed_ref,
+    cond_ref,
+    attn_out,
+    up_out,
+    down_out,
+    part,
+    landed,
+    mark_send,
+    mark_recv,
+    part_send,
+    part_recv,
+    mod_send,
+    mod_recv,
+    *gather_refs,
+):
+    tp, dp = lax.axis_index("tp"), lax.axis_index("dp")
+    count = 2 * planes
+    slots = marks_ref.shape[0]
+    kinds = ada_ref.shape[0]
+    around = [(tp, lax.rem(dp + step, count)) for step in range(1, count)]
+    others = [(lax.rem(tp + step, 4), dp) for step in range(1, 4)]
+    greet(around + others)
+
+    gathers = [
+        GatherRows(block, whole, gather_refs[3 * i : 3 * i + 3], planes)
+        for i, (block, whole) in enumerate(
+            ((attn_ref, attn_out), (up_ref, up_out), (down_ref, down_out))
+        )
+    ]
+    mark_copies = [
+        remote(
+            marks_ref,
+            marks_all_ref.at[pl.ds(pl.multiple_of(dp * slots, slots), slots)],
+            mark_send.at[i],
+            mark_recv.at[i],
+            *peer,
+        )
+        for i, peer in enumerate(around)
+    ]
+    for copy in mark_copies:
+        copy.start()
+    gathers[0].start()
+    marks_all_ref[pl.ds(pl.multiple_of(dp * slots, slots), slots)] = marks_ref[...]
+    for copy in mark_copies:
+        copy.wait()
+
+    labels = marks_all_ref[:, 0:1]
+    stamps = marks_all_ref[:, 64:65].astype(F32) / 1000.0
+    angles = stamps * freqs_ref[0:1]
+    stamp_embed = jnp.where(freqs_ref[1:2] > 0.0, jnp.cos(angles), jnp.sin(angles))
+    classes = lax.broadcasted_iota(jnp.int32, (count * slots, table_ref.shape[1]), 1)
+    onehot = jnp.where(classes == labels, 1.0, 0.0).astype(BF16)
+    embed = dot32(onehot, table_ref[...], ((1,), (1,))) + stamp_embed
+    embed_ref[...] = embed
+    cond = (embed / (1.0 + jnp.exp(-embed))).astype(BF16)
+    cond_ref[...] = cond
+    for kind in range(kinds):
+        rows = dot32(cond, ada_ref[kind], ((1,), (0,)))
+        part[:, kind * slots : (kind + 1) * slots, :] = rows.reshape(count, slots, rows.shape[1])
+    part_copies = [
+        remote(part.at[peer[1]], landed.at[i], part_send.at[i], part_recv.at[i], *peer)
+        for i, peer in enumerate(around)
+    ]
+    for copy in part_copies:
+        copy.start()
+    for copy in part_copies:
+        copy.wait_recv()
+    total = part[dp]
+    for i in range(count - 1):
+        total = total + landed[i]
+    mods_ref[tp] = total
+    mod_copies = [
+        remote(mods_ref.at[tp], mods_ref.at[tp], mod_send.at[i], mod_recv.at[i], *peer)
+        for i, peer in enumerate(others)
+    ]
+    for copy in mod_copies:
+        copy.start()
+    gathers[1].start()
+    gathers[0].relay()
+    gathers[2].start()
+    gathers[1].relay()
+    gathers[2].relay()
+    for copy in part_copies:
+        copy.wait_send()
+    for copy in mod_copies:
+        copy.wait()
+    for gather in gathers:
+        gather.finish()
+
+
+def front(marks, freqs, table, ada, attn, up, down, planes):
+    slots = marks.shape[0]
+    count = 2 * planes
+    kinds, rows, cols = ada.shape
+    vmem = pl.BlockSpec(memory_space=pltpu.VMEM)
+    whole = pl.BlockSpec(memory_space=pl.ANY)
+    gathered = [
+        jax.ShapeDtypeStruct((2, planes, 2, *block.shape), BF16) for block in (attn, up, down)
+    ]
+    dma = pltpu.SemaphoreType.DMA
+    return pl.pallas_call(
+        functools.partial(front_kernel, planes),
+        in_specs=[vmem, vmem, vmem, vmem, whole, whole, whole],
+        out_specs=[vmem, vmem, vmem, vmem, whole, whole, whole],
+        out_shape=[
+            jax.ShapeDtypeStruct((4, kinds * slots, cols), F32),
+            jax.ShapeDtypeStruct((count * slots, 128), jnp.int32),
+            jax.ShapeDtypeStruct((count * slots, rows), F32),
+            jax.ShapeDtypeStruct((count * slots, rows), BF16),
+            *gathered,
+        ],
+        scratch_shapes=[
+            pltpu.VMEM((count, kinds * slots, cols), F32),
+            pltpu.VMEM((count - 1, kinds * slots, cols), F32),
+            dma((count - 1,)),
+            dma((count - 1,)),
+            dma((count - 1,)),
+            dma((count - 1,)),
+            dma((3,)),
+            dma((3,)),
+            *(gather_sems(planes) * 3),
+        ],
+        compiler_params=pltpu.CompilerParams(
+            collective_id=1, has_side_effects=True, vmem_limit_bytes=32 << 20
+        ),
+    )(marks, freqs, table, ada, attn, up, down)
 
 
 def adam_step(weight, moment, second, average, gradient, rate):
@@ -284,25 +537,43 @@
     attn_block = jnp.concatenate(
         [qkv_weight[:, 0], qkv_weight[:, 1], qkv_weight[:, 2], proj_weight.T], axis=1
     ).astype(BF16)
-    w_attn = gather_rows(attn_block)
-    w_up = gather_rows(up_weight.astype(BF16))
-    w_down = gather_rows(down_weight.T.astype(BF16))
+    planes = lax.axis_size("dp") // 2
+    marks = jnp.concatenate(
+        [
+            jnp.broadcast_to(labels[:, None], (slot_count, 64)),
+            jnp.broadcast_to(timesteps[:, None], (slot_count, 64)),
+        ],
+        axis=1,
+    )
+    column = dp_place * shard_rows + jnp.arange(shard_rows, dtype=jnp.int32)
+    half_width = width // 2
+    freqs = jnp.stack(
+        [
+            jnp.exp(-math.log(10000.0) * (column % half_width).astype(F32) / half_width),
+            (column < half_width).astype(F32),
+        ]
+    )
+    w_ada = ada_weight.transpose(1, 0, 2).astype(BF16)
+    classes = table_weight.shape[0]
+    table_low = jnp.pad(table_weight.T.astype(BF16), ((0, 0), (0, -classes % 128)))
+    mod_parts, marks, embed, cond_low, w_attn, w_up, w_down = front(
+        marks,
+        freqs,
+        table_low,
+        w_ada,
+        attn_block,
+        up_weight.astype(BF16),
+        down_weight.T.astype(BF16),
+        planes,
+    )
+    w_attn = w_attn.reshape(2, width, 4 * quarter_width)
+    w_up = w_up.reshape(2, width, 4 * quarter_width)
+    w_down = w_down.reshape(2, width, 4 * quarter_width)
     w_qkv = w_attn[:, :, : 3 * quarter_width]
     w_proj = w_attn[:, :, 3 * quarter_width :]
-
-    marks = lax.all_gather(jnp.stack([labels, timesteps]), "dp", axis=1, tiled=True)
-    class_onehot = (
-        marks[0][:, None] == jnp.arange(table_weight.shape[0], dtype=jnp.int32)[None, :]
-    )
-    stamps = time_embed(marks[1], width)
-    embed = jnp.dot(
-        class_onehot.astype(BF16), table_weight.astype(BF16), preferred_element_type=F32
-    ) + lax.dynamic_slice_in_dim(stamps, dp_place * shard_rows, shard_rows, 1)
-    cond_low = jax.nn.silu(embed).astype(BF16)
-    w_ada = ada_weight.astype(BF16)
-    mod_part = jnp.einsum("qd,dke->qke", cond_low, w_ada, preferred_element_type=F32)
-    mod_part = lax.psum_scatter(mod_part, "dp", scatter_dimension=0, tiled=True)
-    modulation = lax.all_gather(mod_part, "tp", axis=2, tiled=True)
+    class_onehot = marks[:, 0:1] == jnp.arange(classes, dtype=jnp.int32)[None, :]
+    modulation = mod_parts.reshape(4, 6, slot_count, quarter_width)
+    modulation = modulation.transpose(2, 1, 0, 3).reshape(slot_count, 6, width)
     slot_base = dp_place * slot_count
     choose = (
         quarter_ids[:, None] - slot_base == jnp.arange(slot_count, dtype=jnp.int32)[None, :]
@@ -407,7 +678,7 @@
     grad_mod = lax.all_gather(grad_mod, "dp", axis=0, tiled=True)
     grad_ada = jnp.einsum("qd,qke->dke", cond_low, grad_mod, preferred_element_type=F32)
     grad_cond = lax.psum(
-        jnp.einsum("qke,dke->qd", grad_mod, w_ada, preferred_element_type=F32), "tp"
+        jnp.einsum("qke,kde->qd", grad_mod, w_ada, preferred_element_type=F32), "tp"
     )
     unused, silu_back = jax.vjp(jax.nn.silu, embed)
     grad_embed = silu_back(grad_cond)[0]

time: 879 us -> 831 us (0.945)
  Pallas kernels: 51.8 us -> 186 us
  blocking collectives: 227 us -> 158 us
  starting transfers between devices: 94.8 us -> 48.9 us
  other arithmetic: 117 us -> 92.5 us
  waiting for transfers between devices: 161 us -> 143 us
  between operations: 21 us -> 7.82 us
  local copies, waits for them, and re-layouts: 99 us -> 86.6 us
    pallas_call x0 -> x1, Pallas kernels: none -> 135 us  [front(): pl.pallas_call(functools.partial(front_kernel, planes), in_specs=[vmem, v...]
    all_gather x2 -> x0, blocking collectives: 66.9 us -> none  [the longest x1 45.9 us: per_device(): modulation = lax.all_gather(mod_part, 'tp', axis=2, tiled=True)]
    ppermute x18 -> x9, starting transfers between devices: 68.5 us -> 34.2 us  [shift(): lax.ppermute(value, 'dp', [(i, (i + 2 * steps) % count) for i in range(co...]
    dynamic_update_slice x12 -> x0, other arithmetic: 15.9 us -> none  [gather_rows(): lax.dynamic_update_slice(column, both, (0, (place - step) % planes, 0, 0))]
    ppermute x31 -> x16, waiting for transfers between devices: 137 us -> 121 us  [swap(): return lax.ppermute(value, axis, [(i, i ^ bit) for i in range(count)])]
    another operation x8 -> x2, other arithmetic: 13.3 us -> 1.29 us  [the longest x6 11.3 us: gather_rows(): whole = jnp.stack([first, second], axis=2)]
    ppermute x31 -> x16, starting transfers between devices: 26.3 us -> 14.7 us  [swap(): return lax.ppermute(value, axis, [(i, i ^ bit) for i in range(count)])]
    unnamed x213 -> x232, local copies, waits for them, and re-layouts: 16.8 us -> 23.3 us
  transfers between devices with their start and end apart: 50 -> 25, of which waited for: 18 -> 11; matrix products, arithmetic and copies ran while one was open for 28% -> 22% of each run, Pallas kernels for 6% -> 3%
where the time goes in v2:
time: 831 us; the launch traced here: 823 us
  Pallas kernels  186 us (22%)
  blocking collectives  158 us (19%)
  waiting for transfers between devices  143 us (17%)
  matrix products  99.9 us (12%)
  other arithmetic  92.5 us (11%)
  local copies, waits for them, and re-layouts  86.6 us (10%)
  starting transfers between devices  48.9 us (6%)
    pallas_call x1, Pallas kernels, front(): pl.pallas_call(functools.partial(front_kernel, planes), in_specs=[vmem, v...  135 us
    ppermute x16, waiting for transfers between devices, swap(): return lax.ppermute(value, axis, [(i, i ^ bit) for i in range(count)])  121 us
    psum x1, blocking collectives, per_device(): grad_norm = jnp.sqrt(lax.psum(local_squares, ('tp', 'dp')))  75.1 us
    all_gather x1, blocking collectives, per_device(): grad_quarter = lax.all_gather(grad_quarter, 'tp', axis=0, tiled=True)  50.4 us
    ppermute x9, starting transfers between devices, shift(): lax.ppermute(value, 'dp', [(i, (i + 2 * steps) % count) for i in range(co...  34.2 us
    pallas_call x1, Pallas kernels, attend_back(): pl.pallas_call(functools.partial(attend_back_whole, small_len), grid=(pai...  26.4 us
    pallas_call x1, Pallas kernels, attend(): pl.pallas_call(functools.partial(attend_kernel, small_len), grid=(pair *...  24.7 us
    unnamed x232, local copies, waits for them, and re-layouts  23.3 us
  transfers between devices with their start and end apart: 25, of which 11 were waited for; matrix products, arithmetic and copies ran while one was open for 22% of the time, Pallas kernels for 3%

profile of v2, /device:TPU:0, one launch (start us, length us, event | category | flops | bytes accessed | tf_op | source)
XLA Modules:
  0.0 822.6 jit_solution(3038584081983142832)
XLA Ops:
  4.3 134.6 %shard_map.484 = (f32[4,48,288]{2,1,0:T(8,128)S(1)}, s32[64,128]{1,0:T(8,128)S(1)}, f32[64,144]{1,0:T(8,128)S(1)}, bf16[64,144]{1,0:T(8,128)(2,1)S(1)}, bf16[2,4...) custom-call(s32[8,128]{1,0:T(8,128)S(1)} %pad_add_fusion.marks_ref, ...), custom_call_target="tpu_custom_call" | custom-call | tf_op jit(solution)/shard_map/pallas_call | solution.py:393
  160.8 24.7 %shard_map.485 = (bf16[8,72,1024]{2,1,0:T(8,128)(2,1)S(1)}, f32[8,1,1024]{2,1,0:T(1,128)S(1)}) custom-call(s32[4]{0:T(128)S(1)} %pad_add_fusion.1.ids_ref.ids, bf16[2,3,4,72,1024]{4,3,2,1,0:T(8,128)(2,1)S(1)} %bitcast.287, bf16[2,3,4,72,1024]{4,3,2,1,0:T(8,128)(2,1)S(1)} %bitcast.288, bf16[2,3,4,72,1024]{4,3,2,1,0:T(8,128)(2,1)S(1)} %bitcast.289), custom_call_target="tpu_custom_call" | custom-call | tf_op jit(solution)/shard_map/pallas_call | solution.py:77
  195.3 25.6 %collective-permute-done = bf16[512,1152]{1,0:T(8,128)(2,1)S(1)} collective-permute-done((bf16[512,1152]{1,0:T(8,128)(2,1)S(1)}, bf16[512,1152]{1,0:T(8,128)(2,1)S(1)}, u32[]{:S(2)}, u32[]{:S(2)}) %collective-permute-start) | collective-permute-done | bytes 1179680 | tf_op jit(solution)/shard_map/ppermute | solution.py:435
  233.6 22.0 %collective-permute-done.1 = bf16[512,1152]{1,0:T(8,128)(2,1)} collective-permute-done((bf16[512,1152]{1,0:T(8,128)(2,1)}, bf16[512,1152]{1,0:T(8,128)(2,1)}, u32[]{:S(2)}, u32[]{:S(2)}) %collective-permute-start.1) | collective-permute-done | bytes 1179680 | tf_op jit(solution)/shard_map/ppermute | solution.py:435
  255.6 9.6 %fusion.41 = f32[1024,2,1152]{2,0,1:T(8,128)S(1)} fusion(bf16[2,1152,1152]{2,1,0:T(8,128)(2,1)} %bitcast.307, bf16[512,1152]{1,0:T(8,128)(2,1)} %collective-permute-done.1, bf16[512,1152]{1,0:T(8,128)(2,1)} %fusion.24), kind=kOutput, calls=%fused_computation.104 | convolution fusion | flops 5440536576 | bytes 17104896 | tf_op jit(solution)/shard_map/nd,ydf->nyf/dot_general | solution.py:620
  265.2 9.8 %convolution_bitcast_fusion.4 = f32[1024,1152]{1,0:T(8,128)} fusion(bf16[2,1152,1152]{2,1,0:T(8,128)(2,1)S(1)} %bitcast.313, f32[1024,2,1152]{2,0,1:T(8,128)S(1)} %fusion.41), kind=kOutput, calls=%fused_computation.30 | convolution fusion | flops 5457051648 | bytes 19464192 | tf_op jit(solution)/shard_map/nyf,ydf->nd/dot_general | solution.py:623
  287.9 16.8 %collective-permute-done.2 = bf16[512,1152]{1,0:T(8,128)(2,1)} collective-permute-done((bf16[512,1152]{1,0:T(8,128)(2,1)}, bf16[512,1152]{1,0:T(8,128)(2,1)}, u32[]{:S(2)}, u32[]{:S(2)}) %collective-permute-start.2) | collective-permute-done | bytes 1179680 | tf_op jit(solution)/shard_map/ppermute | solution.py:435
  311.7 14.1 %fusion.6 = bf16[1024,2,1152]{2,0,1:T(8,128)(2,1)} fusion(f32[1024,2,1152]{2,0,1:T(8,128)} %copy-done.27, bf16[1024,1152,1]{1,0,2:T(8,128)(2,1)S(1)} %bitcast.340, bf16[2,1152,1152]{2,1,0:T(8,128)(2,1)S(1)} %bitcast.316), kind=kOutput, calls=%fused_computation.9 | convolution fusion | flops 5483003904 | bytes 21823488 | tf_op jit(solution)/shard_map/nd,ydf->nyf/dot_general | solution.py:629
  325.8 8.6 %convolution_bitcast_fusion.3 = f32[1024,1152]{1,0:T(8,128)S(1)} fusion(bf16[1024,2,1152]{2,0,1:T(8,128)(2,1)} %fusion.6, bf16[2,1152,1152]{2,1,0:T(8,128)(2,1)S(1)} %bitcast.310), kind=kOutput, calls=%fused_computation.29 | convolution fusion | flops 5435817984 | bytes 14745600 | tf_op jit(solution)/shard_map/nyf,ydf->nd/dot_general | solution.py:633
  335.8 8.6 %fusion.25 = f32[1152,2,1152]{2,0,1:T(8,128)S(1)} fusion(bf16[1024,1152]{1,0:T(8,128)(2,1)S(1)} %fusion.7, f32[1024,2,1152]{2,0,1:T(8,128)} %copy-done.27), kind=kOutput, calls=%fused_computation.69 | convolution fusion | flops 5457051648 | bytes 22413312 | tf_op jit(solution)/shard_map/nyf,nd->ydf/dot_general | solution.py:631
  347.6 12.5 %fusion.40 = f32[2,1152,1152]{1,2,0:T(8,128)} fusion(bf16[1024,2,1152]{2,0,1:T(8,128)(2,1)} %fusion.6, bf16[512,1152]{1,0:T(8,128)(2,1)} %collective-permute-done.1, bf16[512,1152]{1,0:T(8,128)(2,1)} %fusion.24), kind=kOutput, calls=%fused_computation.103 | convolution fusion | flops 5440536576 | bytes 17694720 | tf_op jit(solution)/shard_map/nd,nyf->ydf/dot_general | solution.py:632
  380.3 12.5 %collective-permute-done.6 = bf16[512,1152]{1,0:T(8,128)(2,1)} collective-permute-done((bf16[512,1152]{1,0:T(8,128)(2,1)}, bf16[512,1152]{1,0:T(8,128)(2,1)}, u32[]{:S(2)}, u32[]{:S(2)}) %collective-permute-start.6) | collective-permute-done | bytes 1179680 | tf_op jit(solution)/shard_map/ppermute | solution.py:435
  397.9 26.4 %shard_map.486 = bf16[2,3,4,72,1024]{4,3,2,1,0:T(8,128)(2,1)S(1)} custom-call(s32[4]{0:T(128)S(1)} %pad_add_fusion.1.ids_ref.ids, bf16[2,3,4,72,1024]{4,3,2,1,0:T(8,128)(2,1)} %bitcast.290, bf16[2,3,4,72,1024]{4,3,2,1,0:T(8,128)(2,1)} %bitcast.291, bf16[2,3,4,72,1024]{4,3,2,1,0:T(8,128)(2,1)} %bitcast.292, bf16[8,72,1024]{2,1,0:T(8,128)(2,1)S(1)} %bitcast.297, ...), custom_call_target="tpu_custom_call" | custom-call | tf_op jit(solution)/shard_map/pallas_call | solution.py:148
  444.8 8.7 %pad_maximum_fusion = f32[2,1152,1152]{1,2,0:T(8,128)} fusion(f32[2,1152,288]{1,2,0:T(8,128)} %convolution_bitcast_fusion.5, f32[2,1152,864]{1,2,0:T(8,128)} %convolution_bitcast_fusion), kind=kLoop, calls=%fused_computation.2 | loop fusion | flops 2654208 | bytes 21233664 | tf_op jit(solution)/shard_map/concatenate | solution.py:689
  453.6 12.7 %copy.105 = f32[2,1152,1152]{2,1,0:T(8,128)} copy(f32[2,1152,1152]{1,2,0:T(8,128)} %pad_maximum_fusion) | data formatting | bytes 21233664 | tf_op jit(solution)/shard_map/concatenate | solution.py:689
  497.8 50.4 %all_gather.6 = f32[8,6,1152]{2,1,0:T(8,128)S(1)} all-gather(f32[2,6,1152]{2,1,0:T(8,128)S(1)} %stack.33), channel_id=1, replica_groups=mesh['tp'=4,'dp'=8] {'tp'}, dimensions={0}, use_global_device_ids=true | all-gather | bytes 276480 | tf_op jit(solution)/shard_map/all_gather | solution.py:673
  548.5 16.7 %all_gather.7 = bf16[64,6,288]{2,0,1:T(8,128)(2,1)S(1)} all-gather(bf16[8,6,288]{2,0,1:T(8,128)(2,1)S(1)} %convolution_convert_fusion), channel_id=1, replica_groups=mesh['tp'=4,'dp'=8] {'dp'}, dimensions={0}, use_global_device_ids=true | all-gather | bytes 248832 | tf_op jit(solution)/shard_map/all_gather | solution.py:678
  565.5 16.1 %psum.14 = f32[64,144]{1,0:T(8,128)S(1)} all-reduce(f32[64,144]{1,0:T(8,128)S(1)} %convolution_bitcast_fusion.6), channel_id=1, replica_groups=mesh['tp'=4,'dp'=8] {'tp'}, use_global_device_ids=true, to_apply=%region_18.19 | all-reduce | flops 9216 | bytes 73728 | tf_op jit(solution)/shard_map/psum | solution.py:680
  603.1 11.3 %collective-permute-start.18 = (bf16[144,1152]{1,0:T(8,128)(2,1)S(1)}, bf16[144,1152]{1,0:T(8,128)(2,1)}, u32[]{:S(2)}, u32[]{:S(2)}) collective-permute-start(bf16[144,1152]{1,0:T(8,128)(2,1)S(1)} %get-tuple-element.165), channel_id=1, source_target_pairs={{0,4},{1,5},{2,6},{3,7},{4,0},{5,1},{6,2},{7,3},{8,12},{9,13},{10,... | collective-permute-start | bytes 995336 | tf_op jit(solution)/shard_map/ppermute | solution.py:440
  621.9 12.6 %collective-permute-start.19 = (bf16[144,1152]{1,0:T(8,128)(2,1)S(1)}, bf16[144,1152]{1,0:T(8,128)(2,1)}, u32[]{:S(2)}, u32[]{:S(2)}) collective-permute-start(bf16[144,1152]{1,0:T(8,128)(2,1)S(1)} %get-tuple-element.164), channel_id=1, source_target_pairs={{0,6},{1,7},{2,0},{3,1},{4,2},{5,3},{6,4},{7,5},{8,14},{9,15},{10,... | collective-permute-start | bytes 995336 | tf_op jit(solution)/shard_map/ppermute | solution.py:440
  649.1 17.7 %collective-permute-done.11 = bf16[4,144,1152]{2,1,0:T(8,128)(2,1)} collective-permute-done((bf16[4,144,1152]{2,1,0:T(8,128)(2,1)}, bf16[4,144,1152]{2,1,0:T(8,128)(2,1)}, u32[]{:S(2)}, u32[]{:S(2)}) %collective-permute-start.11) | collective-permute-done | bytes 1327136 | tf_op jit(solution)/shard_map/ppermute | solution.py:435
  679.8 7.7 collective-permute-done.13
  690.9 26.5 %collective-permute-done.4 = bf16[2,512,1152]{2,1,0:T(8,128)(2,1)} collective-permute-done((bf16[2,512,1152]{2,1,0:T(8,128)(2,1)}, bf16[2,512,1152]{2,1,0:T(8,128)(2,1)}, u32[]{:S(2)}, u32[]{:S(2)}) %collective-permute-start.4) | collective-permute-done | bytes 2359328 | tf_op jit(solution)/shard_map/ppermute | solution.py:435
  720.7 75.1 %psum.15 = f32[]{:T(128)} all-reduce(f32[]{:T(128)S(6)} %add.536), channel_id=1, replica_groups=mesh['tp'=4,'dp'=8] {'tp','dp'}, use_global_device_ids=true, to_apply=%region_20.21 | all-reduce | flops 1 | bytes 8 | tf_op jit(solution)/shard_map/psum | solution.py:700
  (406 shorter events, 233.3 us)
Async XLA Ops:
  192.6 28.2 %collective-permute-start = (bf16[512,1152]{1,0:T(8,128)(2,1)S(1)}, bf16[512,1152]{1,0:T(8,128)(2,1)S(1)}, u32[]{:S(2)}, u32[]{:S(2)}) collective-permute-start(bf16[512,1152]{1,0:T(8,128)(2,1)S(1)} %slice.219), channel_id=1, source_target_pairs={{0,8},{8,0},{16,24},{24,16},{1,9},{9,1},{17,25},{25,17},{2,10},{10... | collective-permute-start | bytes 3538952 | tf_op jit(solution)/shard_map/ppermute | solution.py:435
  227.9 27.7 %collective-permute-start.1 = (bf16[512,1152]{1,0:T(8,128)(2,1)}, bf16[512,1152]{1,0:T(8,128)(2,1)}, u32[]{:S(2)}, u32[]{:S(2)}) collective-permute-start(bf16[512,1152]{1,0:T(8,128)(2,1)} %fusion.24), channel_id=1, source_target_pairs={{0,8},{8,0},{16,24},{24,16},{1,9},{9,1},{17,25},{25,17},{2,10},{10... | collective-permute-start | bytes 3538952 | tf_op jit(solution)/shard_map/ppermute | solution.py:435
  277.9 26.8 %collective-permute-start.2 = (bf16[512,1152]{1,0:T(8,128)(2,1)}, bf16[512,1152]{1,0:T(8,128)(2,1)}, u32[]{:S(2)}, u32[]{:S(2)}) collective-permute-start(bf16[512,1152]{1,0:T(8,128)(2,1)} %slice.218), channel_id=1, source_target_pairs={{0,8},{8,0},{16,24},{24,16},{1,9},{9,1},{17,25},{25,17},{2,10},{10... | collective-permute-start | bytes 3538952 | tf_op jit(solution)/shard_map/ppermute | solution.py:435
  334.5 25.7 %collective-permute-start.5 = (bf16[512,1152]{1,0:T(8,128)(2,1)S(1)}, bf16[512,1152]{1,0:T(8,128)(2,1)S(1)}, u32[]{:S(2)}, u32[]{:S(2)}) collective-permute-start(bf16[512,1152]{1,0:T(8,128)(2,1)S(1)} %slice.217), channel_id=1, source_target_pairs={{0,8},{8,0},{16,24},{24,16},{1,9},{9,1},{17,25},{25,17},{2,10},{10... | collective-permute-start | bytes 3538952 | tf_op jit(solution)/shard_map/ppermute | solution.py:435
  347.6 127.6 %collective-permute-start.20 = (bf16[2,4,144,1152]{3,2,1,0:T(8,128)(2,1)}, bf16[2,4,144,1152]{3,2,1,0:T(8,128)(2,1)}, u32[]{:S(2)}, u32[]{:S(2)}) collective-permute-start(bf16[2,4,144,1152]{3,2,1,0:T(8,128)(2,1)} %fusion.14), channel_id=1, source_target_pairs={{0,1},{1,0},{2,3},{3,2},{4,5},{5,4},{6,7},{7,6},{8,9},{9,8},{10,11... | collective-permute-start | bytes 7962632 | tf_op jit(solution)/shard_map/ppermute | solution.py:435
  363.6 29.3 %collective-permute-start.6 = (bf16[512,1152]{1,0:T(8,128)(2,1)}, bf16[512,1152]{1,0:T(8,128)(2,1)}, u32[]{:S(2)}, u32[]{:S(2)}) collective-permute-start(bf16[512,1152]{1,0:T(8,128)(2,1)} %get-tuple-element.158), channel_id=1, source_target_pairs={{0,8},{8,0},{16,24},{24,16},{1,9},{9,1},{17,25},{25,17},{2,10},{10... | collective-permute-start | bytes 3538952 | tf_op jit(solution)/shard_map/ppermute | solution.py:435
  369.3 115.6 %collective-permute-start.15 = (bf16[2,4,144,1152]{3,2,1,0:T(8,128)(2,1)}, bf16[2,4,144,1152]{3,2,1,0:T(8,128)(2,1)}, u32[]{:S(2)}, u32[]{:S(2)}) collective-permute-start(bf16[2,4,144,1152]{3,2,1,0:T(8,128)(2,1)} %fusion.13), channel_id=1, source_target_pairs={{0,1},{1,0},{2,3},{3,2},{4,5},{5,4},{6,7},{7,6},{8,9},{9,8},{10,11... | collective-permute-start | bytes 7962632 | tf_op jit(solution)/shard_map/ppermute | solution.py:435
  377.9 92.6 %collective-permute-start.3 = (bf16[512,1152]{1,0:T(8,128)(2,1)}, bf16[512,1152]{1,0:T(8,128)(2,1)S(1)}, u32[]{:S(2)}, u32[]{:S(2)}) collective-permute-start(bf16[512,1152]{1,0:T(8,128)(2,1)} %get-tuple-element.159), channel_id=1, source_target_pairs={{0,8},{8,0},{16,24},{24,16},{1,9},{9,1},{17,25},{25,17},{2,10},{10... | collective-permute-start | bytes 3538952 | tf_op jit(solution)/shard_map/ppermute | solution.py:435
  430.6 59.4 %collective-permute-start.7 = (bf16[512,1152]{1,0:T(8,128)(2,1)}, bf16[512,1152]{1,0:T(8,128)(2,1)}, u32[]{:S(2)}, u32[]{:S(2)}) collective-permute-start(bf16[512,1152]{1,0:T(8,128)(2,1)} %slice.216), channel_id=1, source_target_pairs={{0,8},{8,0},{16,24},{24,16},{1,9},{9,1},{17,25},{25,17},{2,10},{10... | collective-permute-start | bytes 3538952 | tf_op jit(solution)/shard_map/ppermute | solution.py:435
  470.5 126.7 %collective-permute-start.10 = (bf16[2,4,144,1152]{3,2,1,0:T(8,128)(2,1)}, bf16[2,4,144,1152]{3,2,1,0:T(8,128)(2,1)}, u32[]{:S(2)}, u32[]{:S(2)}) collective-permute-start(bf16[2,4,144,1152]{3,2,1,0:T(8,128)(2,1)} %fusion.12), channel_id=1, source_target_pairs={{0,1},{1,0},{2,3},{3,2},{4,5},{5,4},{6,7},{7,6},{8,9},{9,8},{10,11... | collective-permute-start | bytes 7962632 | tf_op jit(solution)/shard_map/ppermute | solution.py:435
  483.4 102.0 %collective-permute-start.21 = (bf16[4,144,1152]{2,1,0:T(8,128)(2,1)}, bf16[4,144,1152]{2,1,0:T(8,128)(2,1)}, u32[]{:S(2)}, u32[]{:S(2)}) collective-permute-start(bf16[4,144,1152]{2,1,0:T(8,128)(2,1)} %fusion.45), channel_id=1, source_target_pairs={{0,16},{8,24},{16,0},{24,8},{1,17},{9,25},{17,1},{25,9},{2,18},{10... | collective-permute-start | bytes 3981320 | tf_op jit(solution)/shard_map/ppermute | solution.py:435
  488.6 105.2 %collective-permute-start.16 = (bf16[4,144,1152]{2,1,0:T(8,128)(2,1)}, bf16[4,144,1152]{2,1,0:T(8,128)(2,1)}, u32[]{:S(2)}, u32[]{:S(2)}) collective-permute-start(bf16[4,144,1152]{2,1,0:T(8,128)(2,1)} %fusion.44), channel_id=1, source_target_pairs={{0,16},{8,24},{16,0},{24,8},{1,17},{9,25},{17,1},{25,9},{2,18},{10... | collective-permute-start | bytes 3981320 | tf_op jit(solution)/shard_map/ppermute | solution.py:435
  496.7 150.2 %collective-permute-start.8 = (bf16[512,1152]{1,0:T(8,128)(2,1)}, bf16[512,1152]{1,0:T(8,128)(2,1)}, u32[]{:S(2)}, u32[]{:S(2)}) collective-permute-start(bf16[512,1152]{1,0:T(8,128)(2,1)} %bitcast.54), channel_id=1, source_target_pairs={{0,8},{8,0},{16,24},{24,16},{1,9},{9,1},{17,25},{25,17},{2,10},{10... | collective-permute-start | bytes 3538952 | tf_op jit(solution)/shard_map/ppermute | solution.py:435
  589.5 13.5 %collective-permute-start.22 = (bf16[144,1152]{1,0:T(8,128)(2,1)S(1)}, bf16[144,1152]{1,0:T(8,128)(2,1)S(1)}, u32[]{:S(2)}, u32[]{:S(2)}) collective-permute-start(bf16[144,1152]{1,0:T(8,128)(2,1)S(1)} %get-tuple-element.160), channel_id=1, source_target_pairs={{0,2},{1,3},{2,4},{3,5},{4,6},{5,7},{6,0},{7,1},{8,10},{9,11},{10,... | collective-permute-start | bytes 995336 | tf_op jit(solution)/shard_map/ppermute | solution.py:440
  591.4 30.5 %collective-permute-start.23 = (bf16[144,1152]{1,0:T(8,128)(2,1)S(1)}, bf16[144,1152]{1,0:T(8,128)(2,1)S(1)}, u32[]{:S(2)}, u32[]{:S(2)}) collective-permute-start(bf16[144,1152]{1,0:T(8,128)(2,1)S(1)} %get-tuple-element.162), channel_id=1, source_target_pairs={{0,4},{1,5},{2,6},{3,7},{4,0},{5,1},{6,2},{7,3},{8,12},{9,13},{10,... | collective-permute-start | bytes 995336 | tf_op jit(solution)/shard_map/ppermute | solution.py:440
  593.8 40.7 %collective-permute-start.24 = (bf16[144,1152]{1,0:T(8,128)(2,1)S(1)}, bf16[144,1152]{1,0:T(8,128)(2,1)S(1)}, u32[]{:S(2)}, u32[]{:S(2)}) collective-permute-start(bf16[144,1152]{1,0:T(8,128)(2,1)S(1)} %get-tuple-element.161), channel_id=1, source_target_pairs={{0,6},{1,7},{2,0},{3,1},{4,2},{5,3},{6,4},{7,5},{8,14},{9,15},{10,... | collective-permute-start | bytes 995336 | tf_op jit(solution)/shard_map/ppermute | solution.py:440
  597.2 43.6 %collective-permute-start.17 = (bf16[144,1152]{1,0:T(8,128)(2,1)S(1)}, bf16[144,1152]{1,0:T(8,128)(2,1)}, u32[]{:S(2)}, u32[]{:S(2)}) collective-permute-start(bf16[144,1152]{1,0:T(8,128)(2,1)S(1)} %get-tuple-element.163), channel_id=1, source_target_pairs={{0,2},{1,3},{2,4},{3,5},{4,6},{5,7},{6,0},{7,1},{8,10},{9,11},{10,... | collective-permute-start | bytes 995336 | tf_op jit(solution)/shard_map/ppermute | solution.py:440
  603.1 39.2 %collective-permute-start.18 = (bf16[144,1152]{1,0:T(8,128)(2,1)S(1)}, bf16[144,1152]{1,0:T(8,128)(2,1)}, u32[]{:S(2)}, u32[]{:S(2)}) collective-permute-start(bf16[144,1152]{1,0:T(8,128)(2,1)S(1)} %get-tuple-element.165), channel_id=1, source_target_pairs={{0,4},{1,5},{2,6},{3,7},{4,0},{5,1},{6,2},{7,3},{8,12},{9,13},{10,... | collective-permute-start | bytes 995336 | tf_op jit(solution)/shard_map/ppermute | solution.py:440
  621.9 22.1 %collective-permute-start.19 = (bf16[144,1152]{1,0:T(8,128)(2,1)S(1)}, bf16[144,1152]{1,0:T(8,128)(2,1)}, u32[]{:S(2)}, u32[]{:S(2)}) collective-permute-start(bf16[144,1152]{1,0:T(8,128)(2,1)S(1)} %get-tuple-element.164), channel_id=1, source_target_pairs={{0,6},{1,7},{2,0},{3,1},{4,2},{5,3},{6,4},{7,5},{8,14},{9,15},{10,... | collective-permute-start | bytes 995336 | tf_op jit(solution)/shard_map/ppermute | solution.py:440
  634.5 32.4 %collective-permute-start.11 = (bf16[4,144,1152]{2,1,0:T(8,128)(2,1)}, bf16[4,144,1152]{2,1,0:T(8,128)(2,1)}, u32[]{:S(2)}, u32[]{:S(2)}) collective-permute-start(bf16[4,144,1152]{2,1,0:T(8,128)(2,1)} %fusion.43), channel_id=1, source_target_pairs={{0,16},{8,24},{16,0},{24,8},{1,17},{9,25},{17,1},{25,9},{2,18},{10... | collective-permute-start | bytes 3981320 | tf_op jit(solution)/shard_map/ppermute | solution.py:435
  640.8 76.6 %collective-permute-start.4 = (bf16[2,512,1152]{2,1,0:T(8,128)(2,1)}, bf16[2,512,1152]{2,1,0:T(8,128)(2,1)}, u32[]{:S(2)}, u32[]{:S(2)}) collective-permute-start(bf16[2,512,1152]{2,1,0:T(8,128)(2,1)} %copy-done.26), channel_id=1, source_target_pairs={{0,16},{8,24},{16,0},{24,8},{1,17},{9,25},{17,1},{25,9},{2,18},{10... | collective-permute-start | bytes 7077896 | tf_op jit(solution)/shard_map/ppermute | solution.py:435
  648.4 168.2 %collective-permute-start.9 = (bf16[2,512,1152]{2,1,0:T(8,128)(2,1)S(1)}, bf16[2,512,1152]{2,1,0:T(8,128)(2,1)}, u32[]{:S(2)}, u32[]{:S(2)}) collective-permute-start(bf16[2,512,1152]{2,1,0:T(8,128)(2,1)S(1)} %bitcast_dynamic-update-slice_fusion.4), channel_id=1, source_target_pairs={{0,16},{8,24},{16,0},{24,8},{1,17},{9,25},{17,1},{25,9},{2,18},{10... | collective-permute-start | bytes 7077896 | tf_op jit(solution)/shard_map/ppermute | solution.py:435
  668.7 18.9 %collective-permute-start.13 = (bf16[144,1152]{1,0:T(8,128)(2,1)S(1)}, bf16[144,1152]{1,0:T(8,128)(2,1)S(1)}, u32[]{:S(2)}, u32[]{:S(2)}) collective-permute-start(bf16[144,1152]{1,0:T(8,128)(2,1)S(1)} %get-tuple-element.168), channel_id=1, source_target_pairs={{0,4},{1,5},{2,6},{3,7},{4,0},{5,1},{6,2},{7,3},{8,12},{9,13},{10,... | collective-permute-start | bytes 995336 | tf_op jit(solution)/shard_map/ppermute | solution.py:440
  669.3 18.2 %collective-permute-start.14 = (bf16[144,1152]{1,0:T(8,128)(2,1)S(1)}, bf16[144,1152]{1,0:T(8,128)(2,1)S(1)}, u32[]{:S(2)}, u32[]{:S(2)}) collective-permute-start(bf16[144,1152]{1,0:T(8,128)(2,1)S(1)} %get-tuple-element.167), channel_id=1, source_target_pairs={{0,6},{1,7},{2,0},{3,1},{4,2},{5,3},{6,4},{7,5},{8,14},{9,15},{10,... | collective-permute-start | bytes 995336 | tf_op jit(solution)/shard_map/ppermute | solution.py:440
  (118 other events, 1344.2 us)

commit v3 on v2

v3 whole, which is shorter than its diff:
```python
import functools
import math

import jax
import jax.numpy as jnp
from jax import lax
from jax.experimental import pallas as pl
from jax.experimental.pallas import tpu as pltpu
from jax.sharding import PartitionSpec as P

D = 1152
HD = 72
FF = 4608
STEP = 5

HIGHEST = lax.Precision.HIGHEST
F32 = jnp.float32
BF16 = jnp.bfloat16
clip_limit = 1.0
HEAD_SCALE = HD**-0.5
LOG2_SCALE = HEAD_SCALE * math.log2(math.e)


def dot32(a, b, dims):
    return lax.dot_general(a, b, (dims, ((), ())), preferred_element_type=F32)


def norm_parts(values):
    centre = values - jnp.mean(values, axis=-1, keepdims=True)
    spread = jnp.mean(centre * centre, axis=-1, keepdims=True)
    rstd = lax.rsqrt(spread + 1e-06)
    return centre * rstd, rstd


def norm_back(hat, rstd, grad_hat):
    first = jnp.mean(grad_hat, axis=-1, keepdims=True)
    second = jnp.mean(grad_hat * hat, axis=-1, keepdims=True)
    return rstd * (grad_hat - first - hat * second)


def time_embed(stamps, width):
    half_width = width // 2
    freqs = jnp.exp(-math.log(10000.0) * jnp.arange(half_width, dtype=jnp.float32) / half_width)
    angles = (stamps.astype(jnp.float32) / 1000.0)[:, None] * freqs[None, :]
    return jnp.concatenate([jnp.cos(angles), jnp.sin(angles)], axis=-1)


def attend_softmax(scores, same, small_len):
    count = len(same)
    blocks = [scores[kb * small_len : (kb + 1) * small_len] for kb in range(count)]
    top = jnp.full((1, small_len), -jnp.inf, F32)
    for kb in range(count):
        block_top = jnp.max(blocks[kb], axis=0, keepdims=True)
        top = jnp.maximum(top, jnp.where(same[kb], block_top, -jnp.inf))
    top = top * LOG2_SCALE
    total = jnp.zeros((1, small_len), F32)
    probs = []
    for kb in range(count):
        base = top + jnp.where(same[kb], 0.0, 1e9)
        expo = jnp.exp2(blocks[kb] * LOG2_SCALE - base)
        total = total + jnp.sum(expo, axis=0, keepdims=True)
        probs.append(expo.astype(BF16))
    return jnp.concatenate(probs, axis=0), total, top


def attend_quarters(ids_ref, qkv_ref, out_ref, log_ref, pair, quarters, small_len):
    heads = qkv_ref.shape[2]
    count = qkv_ref.shape[-1] // small_len
    units = [(qb, h) for qb in quarters for h in range(heads)]
    scores, probs, outs = {}, {}, []
    for i in range(len(units) + 2):
        if i < len(units):
            qb, h = units[i]
            queries = qkv_ref[pair, 0, h, :, pl.ds(qb * small_len, small_len)]
            scores[i] = dot32(qkv_ref[pair, 1, h], queries, ((0,), (0,)))
        if i >= 2:
            qb, h = units[i - 2]
            cols = pl.ds(qb * small_len, small_len)
            low, total, top = probs.pop(i - 2)
            mixed = dot32(qkv_ref[pair, 2, h], low, ((1,), (0,)))
            outs.append(mixed / total)
            log_ref[pair * heads + h, :, cols] = top + jnp.log2(total)
            if h == heads - 1:
                out_ref[pair, :, cols] = jnp.concatenate(outs, axis=0).astype(BF16)
                outs = []
        if 1 <= i <= len(units):
            qb, h = units[i - 1]
            same = [ids_ref[kb] == ids_ref[qb] for kb in range(count)]
            probs[i - 1] = attend_softmax(scores.pop(i - 1), same, small_len)


def back_quarters(
    ids_ref, qkv_ref, out_ref, log_ref, go_ref, gq_ref, gk_ref, gv_ref, pair, quarters, small_len, add
):
    heads = qkv_ref.shape[2]
    count = qkv_ref.shape[-1] // small_len
    units = [(qb, h) for qb in quarters for h in range(heads)]
    firsts, seconds, outs = {}, {}, []
    for i in range(len(units) + 2):
        if i < len(units):
            qb, h = units[i]
            cols = pl.ds(qb * small_len, small_len)
            rows = pl.ds(h * HD, HD)
            grad_out = go_ref[pair, rows, cols]
            firsts[i] = (
                dot32(qkv_ref[pair, 1, h], qkv_ref[pair, 0, h, :, cols], ((0,), (0,))),
                dot32(qkv_ref[pair, 2, h], grad_out.astype(BF16), ((0,), (0,))),
            )
        if i >= 2:
            qb, h = units[i - 2]
            cols = pl.ds(qb * small_len, small_len)
            rows = pl.ds(h * HD, HD)
            probs, scores = seconds.pop(i - 2)
            grad_q = dot32(qkv_ref[pair, 1, h], scores, ((1,), (0,)))
            outs.append(grad_q * HEAD_SCALE)
            grad_k = dot32(qkv_ref[pair, 0, h, :, cols], scores, ((1,), (1,)))
            grad_v = dot32(go_ref[pair, rows, cols].astype(BF16), probs, ((1,), (1,)))
            if add or qb != quarters[0]:
                gk_ref[pair, rows] += grad_k
                gv_ref[pair, rows] += grad_v
            else:
                gk_ref[pair, rows] = grad_k
                gv_ref[pair, rows] = grad_v
            if h == heads - 1:
                place = pl.ds(0, heads * HD)
                gq_ref[pair, place, cols] = jnp.concatenate(outs, axis=0).astype(BF16)
                outs = []
        if 1 <= i <= len(units):
            qb, h = units[i - 1]
            cols = pl.ds(qb * small_len, small_len)
            scores, grad_prob = firsts.pop(i - 1)
            delta = jnp.sum(
                go_ref[pair, pl.ds(h * HD, HD), cols] * out_ref[pair * heads + h, :, cols].astype(F32),
                axis=0,
                keepdims=True,
            )
            probs_low, score_low = [], []
            for kb in range(count):
                part = slice(kb * small_len, (kb + 1) * small_len)
                base = log_ref[pair * heads + h, :, cols] + jnp.where(
                    ids_ref[kb] == ids_ref[qb], 0.0, 1e9
                )
                probs = jnp.exp2(scores[part] * LOG2_SCALE - base)
                probs_low.append(probs.astype(BF16))
                score_low.append((probs * (grad_prob[part] - delta)).astype(BF16))
            seconds[i - 1] = (
                jnp.concatenate(probs_low, axis=0),
                jnp.concatenate(score_low, axis=0),
            )


MESH = pl.DeviceIdType.MESH


def remote(src, dst, send_sem, recv_sem, tp, dp):
    return pltpu.make_async_remote_copy(
        src_ref=src,
        dst_ref=dst,
        send_sem=send_sem,
        recv_sem=recv_sem,
        device_id=(tp, dp),
        device_id_type=MESH,
    )


def greet(peers):
    barrier = pltpu.get_barrier_semaphore()
    for tp, dp in peers:
        pl.semaphore_signal(barrier, inc=1, device_id=(tp, dp), device_id_type=MESH)
    pl.semaphore_wait(barrier, len(peers))


def other_core(dp):
    return dp + 1 - 2 * lax.rem(dp, 2)


def x_neighbour(tp):
    return tp + 1 - 2 * lax.rem(tp, 2)


def y_neighbour(tp):
    return lax.rem(tp + 2, 4)


class GatherRows:
    def __init__(self, block, whole, sems, planes):
        self.block, self.whole, self.planes = block, whole, planes
        self.local, self.sends, self.recvs = sems
        self.tp, self.dp = lax.axis_index("tp"), lax.axis_index("dp")
        self.core = lax.rem(self.dp, 2)
        self.place = lax.div(self.dp, 2)

    def at(self, quarter, step):
        place = lax.rem(self.place - step + self.planes, self.planes)
        cols = self.block.shape[1]
        return self.whole.at[place, self.core, :, pl.ds(quarter * cols, cols)]

    def along(self, step):
        count = 2 * self.planes
        dp = lax.rem(self.dp + 2 * step, count)
        return remote(
            self.block, self.at(0, 0), self.sends.at[step], self.recvs.at[step], self.tp, dp
        )

    def across(self, step):
        place = self.planes + step
        src = self.block if step == 0 else self.at(0, step)
        return remote(
            src,
            self.at(1, step),
            self.sends.at[place],
            self.recvs.at[place],
            y_neighbour(self.tp),
            self.dp,
        )

    def over(self, quarter, step):
        place = (2 + quarter) * self.planes + step
        src = self.block if quarter == 0 and step == 0 else self.at(quarter, step)
        return remote(
            src,
            self.at(quarter, step),
            self.sends.at[place],
            self.recvs.at[place],
            self.tp,
            other_core(self.dp),
        )

    def own(self):
        return pltpu.make_async_copy(self.block, self.at(0, 0), self.local)

    def start(self, steps):
        self.own().start()
        self.across(0).start()
        self.over(0, 0).start()
        for step in range(1, 1 + steps):
            self.along(step).start()

    def start_rest(self, steps):
        for step in range(1 + steps, self.planes):
            self.along(step).start()

    def relay_along(self, first, last):
        for step in range(first, last):
            self.along(step).wait_recv()
            self.across(step).start()
            self.over(0, step).start()

    def relay_across(self):
        for step in range(self.planes):
            self.across(step).wait_recv()
            self.over(1, step).start()

    def finish(self):
        self.own().wait()
        for step in range(self.planes):
            if step > 0:
                self.along(step).wait_send()
            self.across(step).wait_send()
            for quarter in range(2):
                self.over(quarter, step).wait_send()
                self.over(quarter, step).wait_recv()


def gather_sems(planes):
    return [
        pltpu.SemaphoreType.DMA,
        pltpu.SemaphoreType.DMA((4 * planes,)),
        pltpu.SemaphoreType.DMA((4 * planes,)),
    ]


def front_kernel(
    planes,
    marks_ref,
    freqs_ref,
    table_ref,
    ada_ref,
    attn_ref,
    mods_ref,
    marks_all_ref,
    embed_ref,
    cond_ref,
    attn_out,
    part,
    core_land,
    pair_sum,
    landed,
    core_sems,
    mark_send,
    mark_recv,
    part_send,
    part_recv,
    mod_send,
    mod_recv,
    *gather_refs,
):
    tp, dp = lax.axis_index("tp"), lax.axis_index("dp")
    count = 2 * planes
    slots = marks_ref.shape[0]
    kinds = ada_ref.shape[0]
    around = [(tp, lax.rem(dp + step, count)) for step in range(1, count)]
    others = [(lax.rem(tp + step, 4), dp) for step in range(1, 4)]
    greet(around + others)

    gather = GatherRows(attn_ref, attn_out, gather_refs, planes)
    mark_copies = [
        remote(
            marks_ref,
            marks_all_ref.at[pl.ds(pl.multiple_of(dp * slots, slots), slots)],
            mark_send.at[i],
            mark_recv.at[i],
            *peer,
        )
        for i, peer in enumerate(around)
    ]
    for copy in mark_copies:
        copy.start()
    gather.start(1)
    marks_all_ref[pl.ds(pl.multiple_of(dp * slots, slots), slots)] = marks_ref[...]
    for copy in mark_copies:
        copy.wait()

    labels = marks_all_ref[:, 0:1]
    stamps = marks_all_ref[:, 64:65].astype(F32) / 1000.0
    angles = stamps * freqs_ref[0:1]
    stamp_embed = jnp.where(freqs_ref[1:2] > 0.0, jnp.cos(angles), jnp.sin(angles))
    classes = lax.broadcasted_iota(jnp.int32, (count * slots, table_ref.shape[1]), 1)
    onehot = jnp.where(classes == labels, 1.0, 0.0).astype(BF16)
    embed = dot32(onehot, table_ref[...], ((1,), (1,))) + stamp_embed
    embed_ref[...] = embed
    cond = (embed / (1.0 + jnp.exp(-embed))).astype(BF16)
    cond_ref[...] = cond
    for kind in range(kinds):
        rows = dot32(cond, ada_ref[kind], ((1,), (0,)))
        part[:, :, kind * slots : (kind + 1) * slots, :] = rows.reshape(
            planes, 2, slots, rows.shape[1]
        )
    core, place = lax.rem(dp, 2), lax.div(dp, 2)
    core_copy = remote(
        part.at[:, 1 - core], core_land, core_sems.at[0], core_sems.at[1], tp, other_core(dp)
    )
    core_copy.start()
    core_copy.wait()
    pair_sum[...] = part[:, core] + core_land[...]
    part_copies = [
        remote(
            pair_sum.at[lax.rem(place + step, planes)],
            landed.at[step - 1],
            part_send.at[step - 1],
            part_recv.at[step - 1],
            tp,
            lax.rem(dp + 2 * step, count),
        )
        for step in range(1, planes)
    ]
    for copy in part_copies:
        copy.start()
    gather.start_rest(1)
    gather.relay_along(1, 2)
    for copy in part_copies:
        copy.wait_recv()
    total = pair_sum[place]
    for i in range(planes - 1):
        total = total + landed[i]
    mods_ref[tp] = total
    mod_copies = [
        remote(mods_ref.at[tp], mods_ref.at[tp], mod_send.at[i], mod_recv.at[i], *peer)
        for i, peer in enumerate(others)
    ]
    for copy in mod_copies:
        copy.start()
    gather.relay_along(2, planes)
    gather.relay_across()
    for copy in part_copies:
        copy.wait_send()
    for copy in mod_copies:
        copy.wait()
    gather.finish()


def front(marks, freqs, table, ada, attn, planes):
    slots = marks.shape[0]
    count = 2 * planes
    kinds, rows, cols = ada.shape
    vmem = pl.BlockSpec(memory_space=pltpu.VMEM)
    whole = pl.BlockSpec(memory_space=pl.ANY)
    dma = pltpu.SemaphoreType.DMA
    return pl.pallas_call(
        functools.partial(front_kernel, planes),
        in_specs=[vmem, vmem, vmem, vmem, whole],
        out_specs=[vmem, vmem, vmem, vmem, whole],
        out_shape=[
            jax.ShapeDtypeStruct((4, kinds * slots, cols), F32),
            jax.ShapeDtypeStruct((count * slots, 128), jnp.int32),
            jax.ShapeDtypeStruct((count * slots, rows), F32),
            jax.ShapeDtypeStruct((count * slots, rows), BF16),
            jax.ShapeDtypeStruct((planes, 2, attn.shape[0], 2 * attn.shape[1]), BF16),
        ],
        scratch_shapes=[
            pltpu.VMEM((planes, 2, kinds * slots, cols), F32),
            pltpu.VMEM((planes, kinds * slots, cols), F32),
            pltpu.VMEM((planes, kinds * slots, cols), F32),
            pltpu.VMEM((planes - 1, kinds * slots, cols), F32),
            dma((2,)),
            dma((count - 1,)),
            dma((count - 1,)),
            dma((planes - 1,)),
            dma((planes - 1,)),
            dma((3,)),
            dma((3,)),
            *gather_sems(planes),
        ],
        compiler_params=pltpu.CompilerParams(
            collective_id=1, has_side_effects=True, vmem_limit_bytes=32 << 20
        ),
    )(marks, freqs, table, ada, attn)

def middle_kernel(
    planes,
    small_len,
    ids_ref,
    qkv_ref,
    proj_ref,
    tokens_ref,
    mods_ref,
    up_ref,
    down_ref,
    out_ref,
    log_ref,
    branch_ref,
    second_ref,
    up_out,
    down_out,
    branch_send,
    branch_land,
    branch_sends,
    branch_recvs,
    second_sends,
    second_recvs,
    *gather_refs,
):
    tp, dp = lax.axis_index("tp"), lax.axis_index("dp")
    count = 2 * planes
    own_len = tokens_ref.shape[0]
    chunks = own_len // small_len
    beside = x_neighbour(tp)
    pair = qkv_ref.shape[0]
    greet(
        [(tp, lax.rem(dp + 2 * step, count)) for step in range(1, planes)]
        + [(beside, dp), (y_neighbour(tp), dp), (tp, other_core(dp))]
    )
    ups = GatherRows(up_ref, up_out, gather_refs[:3], planes)
    downs = GatherRows(down_ref, down_out, gather_refs[3:], planes)
    ups.start(planes - 1)
    downs.start(planes - 1)

    def chunk(index):
        return pl.ds(index * small_len, small_len)

    def attend(quarters):
        @pl.loop(0, pair)
        def _(index):
            attend_quarters(ids_ref, qkv_ref, out_ref, log_ref, index, quarters, small_len)

    def project(quarter):
        return sum(
            dot32(out_ref[i, :, chunk(quarter)], proj_ref[i], ((0,), (0,))) for i in range(pair)
        )

    branch_copies = [
        remote(
            branch_send.at[chunk(i)],
            branch_land.at[chunk(i)],
            branch_sends.at[i],
            branch_recvs.at[i],
            beside,
            dp,
        )
        for i in range(chunks)
    ]
    second_copies = [
        remote(
            second_ref.at[chunk(i)],
            second_ref.at[chunk(chunks + i)],
            second_sends.at[i],
            second_recvs.at[i],
            beside,
            dp,
        )
        for i in range(chunks)
    ]
    attend(range(chunks, 2 * chunks))
    for i in range(chunks):
        branch_send[chunk(i)] = project(chunks + i).astype(BF16)
        branch_copies[i].start()
    attend(range(chunks))
    ups.relay_along(1, planes)
    for i in range(chunks):
        branch = project(i)
        branch_copies[i].wait_recv()
        branch = branch + branch_land[chunk(i)].astype(F32)
        branch_ref[chunk(i)] = branch
        middle = tokens_ref[chunk(i)].astype(F32) + mods_ref[0, i : i + 1] * branch
        hat, _ = norm_parts(middle)
        second = hat * (1.0 + mods_ref[2, i : i + 1]) + mods_ref[1, i : i + 1]
        second_ref[chunk(i)] = second.astype(BF16)
        second_copies[i].start()
    ups.relay_across()
    downs.relay_along(1, planes)
    for copy in second_copies:
        copy.wait()
    for copy in branch_copies:
        copy.wait_send()
    downs.relay_across()
    ups.finish()
    downs.finish()


def middle(ids, qkv, proj, tokens, mods, up, down, planes, small_len):
    pair, _, heads, head_width, length = qkv.shape
    own_len, width = tokens.shape
    chunks = own_len // small_len
    vmem = pl.BlockSpec(memory_space=pltpu.VMEM)
    whole = pl.BlockSpec(memory_space=pl.ANY)
    dma = pltpu.SemaphoreType.DMA
    return pl.pallas_call(
        functools.partial(middle_kernel, planes, small_len),
        in_specs=[pl.BlockSpec(memory_space=pltpu.SMEM), vmem, vmem, vmem, vmem, whole, whole],
        out_specs=[vmem, vmem, vmem, vmem, whole, whole],
        out_shape=[
            jax.ShapeDtypeStruct((pair, heads * head_width, length), BF16),
            jax.ShapeDtypeStruct((pair * heads, 1, length), F32),
            jax.ShapeDtypeStruct((own_len, width), F32),
            jax.ShapeDtypeStruct((2 * own_len, width), BF16),
            *[
                jax.ShapeDtypeStruct((planes, 2, block.shape[0], 2 * block.shape[1]), BF16)
                for block in (up, down)
            ],
        ],
        scratch_shapes=[
            pltpu.VMEM((own_len, width), BF16),
            pltpu.VMEM((own_len, width), BF16),
            dma((chunks,)),
            dma((chunks,)),
            dma((chunks,)),
            dma((chunks,)),
            *(gather_sems(planes) * 2),
        ],
        compiler_params=pltpu.CompilerParams(
            collective_id=3, has_side_effects=True, vmem_limit_bytes=48 << 20
        ),
    )(ids, qkv, proj, tokens, mods, up, down)


GELU_A = math.sqrt(2.0 / math.pi)
GELU_B = 0.044715


def gelu_pair(values):
    square = values * values
    bend = jnp.tanh(values * (GELU_A + GELU_A * GELU_B * square))
    half = 0.5 + 0.5 * bend
    slope = (0.5 * GELU_A + 1.5 * GELU_A * GELU_B * square) * (1.0 - bend * bend)
    return values * half, half + values * slope


def mlp_kernel(
    planes,
    second_ref,
    mixed_grad_ref,
    up_ref,
    down_ref,
    mixed_out,
    far_mixed_out,
    second_out,
    up_grad_out,
    down_grad_out,
    active,
    hidden_grad,
    mixed_total,
    second_total,
    mixed_send,
    second_send,
    second_land,
    weight_grads,
    weight_lands,
    sends,
    recvs,
    locals_,
):
    tp, dp = lax.axis_index("tp"), lax.axis_index("dp")
    beside, core = x_neighbour(tp), lax.rem(dp, 2)
    phase, tile = pl.program_id(0), pl.program_id(1)
    tiles, _, rows, block = weight_lands.shape[1:]
    own_len, width = mixed_total.shape
    grad_outs = (up_grad_out, down_grad_out)
    second_copy = remote(second_send, second_land, sends.at[0], recvs.at[0], beside, dp)
    keep_far = pltpu.make_async_copy(mixed_send, far_mixed_out, locals_.at[0])
    keep_mixed = pltpu.make_async_copy(mixed_total, mixed_out, locals_.at[1])
    keep_second = pltpu.make_async_copy(second_total, second_out, locals_.at[2])

    def weight_copy(which, index):
        sem = 1 + which * tiles + index
        return remote(
            weight_grads.at[which, index, :, 1 - core],
            weight_lands.at[which, index],
            sends.at[sem],
            recvs.at[sem],
            tp,
            other_core(dp),
        )

    def keep_weight(which, index):
        return pltpu.make_async_copy(
            weight_lands.at[which, index],
            grad_outs[which].at[:, :, pl.ds(index * block, block)],
            locals_.at[3 + which * tiles + index],
        )

    @pl.when((phase == 0) & (tile == 0))
    def _():
        greet([(beside, dp), (tp, other_core(dp))])

    @pl.when(phase < 2)
    def _():
        rows_here = pl.ds(pl.multiple_of((1 - phase) * own_len, own_len), own_len)
        up, down = up_ref[...], down_ref[...]
        hidden = dot32(second_ref[rows_here], up, ((1,), (0,)))
        grad = dot32(mixed_grad_ref[rows_here], down, ((1,), (0,)))
        value, slope = gelu_pair(hidden)
        value = value.astype(BF16)
        back = (grad * slope).astype(BF16)
        active[tile, rows_here] = value
        hidden_grad[tile, rows_here] = back
        mixed = dot32(value, down, ((1,), (1,)))
        second = dot32(back, up, ((1,), (1,)))

        @pl.when(tile == 0)
        def _():
            mixed_total[...] = mixed
            second_total[...] = second

        @pl.when(tile > 0)
        def _():
            mixed_total[...] += mixed
            second_total[...] += second

    @pl.when((phase == 0) & (tile == tiles - 1))
    def _():
        second_send[...] = second_total[...].astype(BF16)
        second_copy.start()
        mixed_send[...] = mixed_total[...].astype(BF16)
        keep_far.start()

    @pl.when((phase == 1) & (tile == tiles - 1))
    def _():
        keep_mixed.start()

    for index in range(tiles):

        @pl.when((phase == 2) & (tile == index))
        def _():
            grads = (
                dot32(second_ref[...], hidden_grad[index], ((0,), (0,))),
                dot32(mixed_grad_ref[...], active[index], ((0,), (0,))),
            )
            for which in range(2):
                low = grads[which].astype(BF16).reshape(planes, 2, rows, block)
                weight_grads[which, index] = low
                weight_copy(which, index).start()

    @pl.when((phase == 2) & (tile == tiles - 1))
    def _():
        second_copy.wait()
        second_total[...] += second_land[...].astype(F32)
        keep_second.start()
        for index in range(tiles):
            for which in range(2):
                weight_copy(which, index).wait()
                mine = weight_grads[which, index, :, core].astype(F32)
                landed = weight_lands[which, index].astype(F32)
                weight_lands[which, index] = (mine + landed).astype(BF16)
                keep_weight(which, index).start()
        for index in range(tiles):
            for which in range(2):
                keep_weight(which, index).wait()
        keep_far.wait()
        keep_mixed.wait()
        keep_second.wait()


def mlp(second, mixed_grad, up, down, planes):
    length, width = second.shape
    hidden = up.shape[1]
    block = 768
    tiles = hidden // block
    shard_rows = width // (2 * planes)
    own_len = length // 2
    single = pl.Buffered(buffer_count=1)
    rows = pl.BlockSpec((length, width), lambda p, t: (0, 0), pipeline_mode=single)
    weight = pl.BlockSpec((width, block), lambda p, t: (0, jnp.where(p < 2, t, tiles - 1)))
    whole = pl.BlockSpec(memory_space=pl.ANY)
    dma = pltpu.SemaphoreType.DMA
    return pl.pallas_call(
        functools.partial(mlp_kernel, planes),
        grid=(3, tiles),
        in_specs=[rows, rows, weight, weight],
        out_specs=[whole] * 5,
        out_shape=[
            jax.ShapeDtypeStruct((own_len, width), F32),
            jax.ShapeDtypeStruct((own_len, width), BF16),
            jax.ShapeDtypeStruct((own_len, width), F32),
            jax.ShapeDtypeStruct((planes, shard_rows, hidden), BF16),
            jax.ShapeDtypeStruct((planes, shard_rows, hidden), BF16),
        ],
        scratch_shapes=[
            pltpu.VMEM((tiles, length, block), BF16),
            pltpu.VMEM((tiles, length, block), BF16),
            pltpu.VMEM((own_len, width), F32),
            pltpu.VMEM((own_len, width), F32),
            pltpu.VMEM((own_len, width), BF16),
            pltpu.VMEM((own_len, width), BF16),
            pltpu.VMEM((own_len, width), BF16),
            pltpu.VMEM((2, tiles, planes, 2, shard_rows, block), BF16),
            pltpu.VMEM((2, tiles, planes, shard_rows, block), BF16),
            dma((1 + 2 * tiles,)),
            dma((1 + 2 * tiles,)),
            dma((3 + 2 * tiles,)),
        ],
        compiler_params=pltpu.CompilerParams(
            collective_id=4,
            has_side_effects=True,
            vmem_limit_bytes=62 << 20,
            dimension_semantics=("arbitrary", "arbitrary"),
        ),
    )(second, mixed_grad, up, down)


class ScatterRows:
    def __init__(self, grad, refs, planes):
        self.grad, self.planes = grad, planes
        self.cross_land, self.along_send, self.along_land, self.sends, self.recvs = refs
        self.cols = grad.shape[2] // 2
        self.tp, self.dp = lax.axis_index("tp"), lax.axis_index("dp")
        self.place = lax.div(self.dp, 2)

    def plane(self, step):
        return lax.rem(self.place + step, self.planes)

    def across(self, step):
        return remote(
            self.grad.at[self.plane(step), :, pl.ds(self.cols, self.cols)],
            self.cross_land.at[step],
            self.sends.at[step],
            self.recvs.at[step],
            y_neighbour(self.tp),
            self.dp,
        )

    def along(self, step):
        sem = self.planes + step
        return remote(
            self.along_send.at[step],
            self.along_land.at[step],
            self.sends.at[sem],
            self.recvs.at[sem],
            self.tp,
            lax.rem(self.dp + 2 * step, 2 * self.planes),
        )

    def order(self):
        return [*range(1, self.planes), 0]

    def start(self):
        for step in self.order():
            self.across(step).start()

    def send(self, step):
        self.across(step).wait_recv()
        mine = self.grad[self.plane(step), :, : self.cols].astype(F32)
        total = mine + self.cross_land[step].astype(F32)
        if step == 0:
            return total
        self.along_send[step] = total.astype(BF16)
        self.along(step).start()

    def collect(self, total):
        for step in range(1, self.planes):
            self.along(step).wait_recv()
            total = total + self.along_land[step].astype(F32)
        return total

    def finish(self):
        for step in range(self.planes):
            self.across(step).wait_send()
            if step > 0:
                self.along(step).wait_send()


def scatter_scratch(planes, rows, cols):
    return [
        pltpu.VMEM((planes, rows, cols), BF16),
        pltpu.VMEM((planes, rows, cols), BF16),
        pltpu.VMEM((planes, rows, cols), BF16),
        pltpu.SemaphoreType.DMA((2 * planes,)),
        pltpu.SemaphoreType.DMA((2 * planes,)),
    ]


def back_kernel(
    planes,
    small_len,
    ids_ref,
    qkv_ref,
    out_ref,
    log_ref,
    proj_ref,
    branch_ref,
    far_ref,
    up_ref,
    down_ref,
    gqkv_ref,
    branch_all,
    far_land,
    up_out,
    down_out,
    go,
    grad_k,
    grad_v,
    branch_sends,
    branch_recvs,
    far_sems,
    *scatter_refs,
):
    tp, dp = lax.axis_index("tp"), lax.axis_index("dp")
    count = 2 * planes
    own_len = branch_ref.shape[0]
    chunks = own_len // small_len
    pair = qkv_ref.shape[0]
    rows = out_ref.shape[0] // pair * HD
    beside = x_neighbour(tp)
    greet(
        [(tp, lax.rem(dp + 2 * step, count)) for step in range(1, planes)]
        + [(beside, dp), (y_neighbour(tp), dp)]
    )

    def chunk(index):
        return pl.ds(index * small_len, small_len)

    branch_copies = [
        remote(
            branch_ref.at[chunk(i)],
            branch_all.at[chunk(chunks + i)],
            branch_sends.at[i],
            branch_recvs.at[i],
            beside,
            dp,
        )
        for i in range(chunks)
    ]
    far_copy = remote(far_ref, far_land, far_sems.at[0], far_sems.at[1], beside, dp)
    for copy in branch_copies:
        copy.start()
    far_copy.start()
    ups = ScatterRows(up_ref, scatter_refs[:5], planes)
    downs = ScatterRows(down_ref, scatter_refs[5:], planes)
    ups.start()
    downs.start()
    branch_all[pl.ds(0, own_len)] = branch_ref[...]

    def heads_grad(quarter):
        for i in range(pair):
            go[i, :, chunk(quarter)] = dot32(proj_ref[i], branch_all[chunk(quarter)], ((1,), (1,)))

    def attend(quarters, add):
        @pl.loop(0, pair)
        def _(index):
            back_quarters(
                ids_ref,
                qkv_ref,
                out_ref,
                log_ref,
                go,
                gqkv_ref,
                grad_k,
                grad_v,
                index,
                quarters,
                small_len,
                add,
            )

    for i in range(chunks):
        heads_grad(i)
    attend(range(chunks), False)
    for step in ups.order()[:-1]:
        ups.send(step)
    for i in range(chunks):
        branch_copies[i].wait()
        heads_grad(chunks + i)
    attend(range(chunks, 2 * chunks), True)
    for i in range(pair):
        gqkv_ref[i, pl.ds(rows, rows)] = (grad_k[i] * HEAD_SCALE).astype(BF16)
        gqkv_ref[i, pl.ds(2 * rows, rows)] = grad_v[i].astype(BF16)
        gqkv_ref[i, pl.ds(3 * rows, rows)] = jnp.zeros((rows, gqkv_ref.shape[2]), BF16)
    up_total = ups.send(0)
    for step in downs.order()[:-1]:
        downs.send(step)
    up_out[...] = ups.collect(up_total)
    down_total = downs.send(0)
    down_out[...] = downs.collect(down_total)
    far_copy.wait()
    ups.finish()
    downs.finish()


def back(ids, qkv, out, log, proj, branch, far, up, down, planes, small_len):
    pair, kinds, heads, head_width, length = qkv.shape
    own_len, width = branch.shape
    chunks = own_len // small_len
    rows = heads * head_width
    shard_rows, cols = up.shape[1], up.shape[2] // 2
    vmem = pl.BlockSpec(memory_space=pltpu.VMEM)
    whole = pl.BlockSpec(memory_space=pl.ANY)
    dma = pltpu.SemaphoreType.DMA
    return pl.pallas_call(
        functools.partial(back_kernel, planes, small_len),
        in_specs=[pl.BlockSpec(memory_space=pltpu.SMEM)]
        + [vmem, vmem, vmem, vmem, vmem, whole, vmem, vmem],
        out_specs=[vmem, vmem, whole, vmem, vmem],
        out_shape=[
            jax.ShapeDtypeStruct((pair, kinds * rows, length), BF16),
            jax.ShapeDtypeStruct((2 * own_len, width), BF16),
            jax.ShapeDtypeStruct((own_len, width), BF16),
            jax.ShapeDtypeStruct((shard_rows, cols), F32),
            jax.ShapeDtypeStruct((shard_rows, cols), F32),
        ],
        scratch_shapes=[
            pltpu.VMEM((pair, rows, length), F32),
            pltpu.VMEM((pair, rows, length), F32),
            pltpu.VMEM((pair, rows, length), F32),
            dma((chunks,)),
            dma((chunks,)),
            dma((2,)),
            *(scatter_scratch(planes, shard_rows, cols) * 2),
        ],
        compiler_params=pltpu.CompilerParams(
            collective_id=5, has_side_effects=True, vmem_limit_bytes=58 << 20
        ),
    )(ids, qkv, out, log, proj, branch, far, up, down)


def tail_kernel(
    planes,
    small_len,
    tokens_ref,
    scale_ref,
    own_ref,
    other_ref,
    middle_ref,
    grad_ref,
    rest_ref,
    choose_ref,
    ada_ref,
    cond_ref,
    embed_ref,
    marks_ref,
    squares_ref,
    token_out,
    reduced_ref,
    ada_grad_ref,
    embed_grad_ref,
    norm_ref,
    first_land,
    own_token,
    first_rows,
    row_land,
    mod_all,
    cond_part,
    cond_land,
    norm_send,
    norm_land,
    first_send,
    first_recv,
    token_sems,
    token_recvs,
    row_sends,
    row_recvs,
    mod_sends,
    mod_recvs,
    cond_sends,
    cond_recvs,
    norm_sends,
    norm_recvs,
    core_land,
    core_sends,
    core_recvs,
    *scatter_refs,
):
    tp, dp = lax.axis_index("tp"), lax.axis_index("dp")
    count = 2 * planes
    core = lax.rem(dp, 2)
    kinds, shard_rows, cols = ada_ref.shape
    slots = mod_all.shape[1] // kinds
    chunks = own_ref.shape[0] // small_len
    beside, across = x_neighbour(tp), y_neighbour(tp)
    around = [(tp, lax.rem(dp + step, count)) for step in range(1, count)]
    others = [(lax.rem(tp + step, 4), dp) for step in range(1, 4)]
    greet(around + others)

    def chunk(index):
        return pl.ds(index * small_len, small_len)

    first_copies = [
        remote(
            other_ref.at[chunk(i)],
            first_land.at[chunk(i)],
            first_send.at[i],
            first_recv.at[i],
            beside,
            dp,
        )
        for i in range(chunks)
    ]
    for copy in first_copies:
        copy.start()
    scatter = ScatterRows(core_land, scatter_refs, planes)

    def core_copy(step):
        place = scatter.plane(step)
        return remote(
            grad_ref.at[place, 1 - core],
            core_land.at[place],
            core_sends.at[step],
            core_recvs.at[step],
            tp,
            other_core(dp),
        )

    for step in scatter.order():
        core_copy(step).start()

    def row_copy(part, step):
        peer = lax.rem(tp + step, 4)
        src = (rest_ref, first_rows)[part].at[peer]
        sem = part * 4 + step
        return remote(
            src, row_land.at[part, tp], row_sends.at[sem], row_recvs.at[sem], peer, dp
        )

    for step in range(1, 4):
        row_copy(0, step).start()
    row_land[0, tp] = rest_ref[tp]
    for step in scatter.order():
        core_copy(step).wait_recv()
        place = scatter.plane(step)
        landed = core_land[place].astype(F32)
        core_land[place] = (landed + grad_ref[place, core].astype(F32)).astype(BF16)
        scatter.across(step).start()

    def token_copy(kind, i):
        if kind == 2:
            owner, target = ((across, beside), (beside, across))[i % 2]
        else:
            owner, target = tp, (beside, across)[kind]
        place = token_out.at[owner, chunk(i)]
        src = own_token.at[chunk(i)] if kind < 2 else place
        sem = kind * chunks + i
        return remote(src, place, token_sems.at[sem], token_recvs.at[sem], target, dp)

    def keep_token(i):
        return pltpu.make_async_copy(
            own_token.at[chunk(i)], token_out.at[tp, chunk(i)], token_sems.at[3 * chunks + i]
        )

    sums = []
    total = None
    for i in range(chunks):
        rows = tokens_ref[chunk(i)].astype(F32)
        hat, rstd = norm_parts(rows)
        first_copies[i].wait_recv()
        grad = own_ref[chunk(i)] + first_land[chunk(i)].astype(F32)
        sums.append(jnp.sum(grad, axis=0, keepdims=True))
        sums.append(jnp.sum(grad * hat, axis=0, keepdims=True))
        back = norm_back(hat, rstd, grad * (1.0 + scale_ref[i : i + 1]))
        own_token[chunk(i)] = (back + middle_ref[chunk(i)]).astype(BF16)
        token_copy(0, i).start()
        token_copy(1, i).start()
        keep_token(i).start()
        if i == 0:
            scatter.send(1)
    quarter_rows = [sums[2 * i + kind] for kind in range(2) for i in range(chunks)]
    quarter_rows.append(jnp.zeros((8 - 2 * chunks, quarter_rows[0].shape[1]), F32))
    quarter_rows = jnp.concatenate(quarter_rows, axis=0)
    for part in range(4):
        first_rows[part] = quarter_rows[:, part * cols : (part + 1) * cols]
    row_land[1, tp] = first_rows[tp]
    for step in range(1, 4):
        row_copy(1, step).start()
    for step in scatter.order()[1:-1]:
        scatter.send(step)
    for step in range(1, 4):
        row_copy(0, step).wait_recv()
        row_copy(1, step).wait_recv()
    landed = row_land[...].reshape(2 * 4 * 8, cols)
    grad_mod = lax.dot_general(
        choose_ref[...],
        landed,
        (((1,), (0,)), ((), ())),
        precision=HIGHEST,
        preferred_element_type=F32,
    ).astype(BF16)
    mod_all[dp] = grad_mod
    mod_copies = [
        remote(mod_all.at[dp], mod_all.at[dp], mod_sends.at[i], mod_recvs.at[i], *peer)
        for i, peer in enumerate(around)
    ]
    for copy in mod_copies:
        copy.start()
    for i in range(0, chunks, 2):
        token_copy(1, i).wait_recv()
        token_copy(2, i).start()
    for copy in mod_copies:
        copy.wait()
    mods = mod_all[...].astype(F32)
    cond_grad = jnp.zeros(cond_part.shape, F32)
    squares = jnp.full((1, 1), squares_ref[0, 0], F32)
    for kind in range(kinds):
        rows = mods[:, kind * slots : (kind + 1) * slots].reshape(count * slots, cols)
        rows = rows.astype(BF16)
        ada_grad = dot32(cond_ref[...], rows, ((0,), (0,)))
        ada_grad_ref[kind] = ada_grad
        squares = squares + jnp.sum(ada_grad * ada_grad).reshape(1, 1)
        cond_grad = cond_grad + dot32(rows, ada_ref[kind], ((1,), (1,)))
    cond_part[...] = cond_grad
    cond_copies = [
        remote(cond_part, cond_land.at[i], cond_sends.at[i], cond_recvs.at[i], *peer)
        for i, peer in enumerate(others)
    ]
    for copy in cond_copies:
        copy.start()
    total = scatter.send(0)
    for copy in cond_copies:
        copy.wait()
    for i in range(3):
        cond_grad = cond_grad + cond_land[i]
    embed = embed_ref[...]
    gate = 1.0 / (1.0 + jnp.exp(-embed))
    embed_grad = cond_grad * (gate * (1.0 + embed * (1.0 - gate)))
    embed_grad_ref[...] = embed_grad
    labels = marks_ref[:, 0:1].astype(F32)
    across_labels = lax.dot_general(
        jnp.ones(labels.shape, F32),
        labels,
        (((1,), (1,)), ((), ())),
        precision=HIGHEST,
        preferred_element_type=F32,
    )
    same = jnp.where(jnp.abs(across_labels - labels) < 0.5, 1.0, 0.0)
    table_rows = lax.dot_general(
        same,
        embed_grad,
        (((1,), (0,)), ((), ())),
        precision=HIGHEST,
        preferred_element_type=F32,
    )
    squares = squares + jnp.sum(table_rows * embed_grad).reshape(1, 1) * 0.25
    total = scatter.collect(total)
    reduced_ref[...] = total
    squares = squares + jnp.sum(total * total).reshape(1, 1)

    norm_send[0] = jnp.broadcast_to(squares, norm_send.shape[1:])
    norm_copies = [
        remote(norm_send.at[0], norm_land.at[i], norm_sends.at[i], norm_recvs.at[i], *peer)
        for i, peer in enumerate(others)
    ]
    for copy in norm_copies:
        copy.start()
    for i in range(1, chunks, 2):
        token_copy(0, i).wait_recv()
        token_copy(2, i).start()
    for copy in norm_copies:
        copy.wait()
    norm = norm_send[0]
    for i in range(3):
        norm = norm + norm_land[i]
    norm_send[1] = norm
    norm_copies = [
        remote(
            norm_send.at[1],
            norm_land.at[3 + i],
            norm_sends.at[3 + i],
            norm_recvs.at[3 + i],
            *peer,
        )
        for i, peer in enumerate(around)
    ]
    for copy in norm_copies:
        copy.start()
    for copy in norm_copies:
        copy.wait()
    for i in range(count - 1):
        norm = norm + norm_land[3 + i]
    norm_ref[...] = jnp.sqrt(norm)

    for copy in first_copies:
        copy.wait_send()
    scatter.finish()
    for step in range(planes):
        core_copy(step).wait_send()
    for step in range(1, 4):
        row_copy(0, step).wait_send()
        row_copy(1, step).wait_send()
    for i in range(chunks):
        keep_token(i).wait()
        for kind in range(3):
            token_copy(kind, i).wait_send()
        if i % 2 == 0:
            token_copy(0, i).wait_recv()
        else:
            token_copy(1, i).wait_recv()
        token_copy(2, i).wait_recv()


def tail(tokens, scale, own, other, middle, grad, rest, choose, ada, cond, embed, marks, squares, small_len):
    planes, _, shard_rows, _ = grad.shape
    width = own.shape[1]
    kinds, _, cols = ada.shape
    count = 2 * planes
    slots = marks.shape[0] // count
    own_len = own.shape[0]
    chunks = own_len // small_len
    vmem = pl.BlockSpec(memory_space=pltpu.VMEM)
    whole = pl.BlockSpec(memory_space=pl.ANY)
    dma = pltpu.SemaphoreType.DMA
    args = (tokens, scale, own, other, middle, grad, rest, choose, ada, cond, embed, marks)
    return pl.pallas_call(
        functools.partial(tail_kernel, planes, small_len),
        in_specs=[vmem] * len(args) + [pl.BlockSpec(memory_space=pltpu.SMEM)],
        out_specs=[whole, vmem, vmem, vmem, vmem],
        out_shape=[
            jax.ShapeDtypeStruct((4, own_len, width), BF16),
            jax.ShapeDtypeStruct((shard_rows, width), F32),
            jax.ShapeDtypeStruct((kinds, shard_rows, cols), F32),
            jax.ShapeDtypeStruct((count * slots, shard_rows), F32),
            jax.ShapeDtypeStruct((8, 128), F32),
        ],
        scratch_shapes=[
            pltpu.VMEM((own_len, width), BF16),
            pltpu.VMEM((own_len, width), BF16),
            pltpu.VMEM((4, 8, cols), F32),
            pltpu.VMEM((2, 4, 8, cols), F32),
            pltpu.VMEM((count, kinds * slots, cols), BF16),
            pltpu.VMEM((count * slots, shard_rows), F32),
            pltpu.VMEM((3, count * slots, shard_rows), F32),
            pltpu.VMEM((2, 8, 128), F32),
            pltpu.VMEM((3 + count - 1, 8, 128), F32),
            dma((chunks,)),
            dma((chunks,)),
            dma((4 * chunks,)),
            dma((3 * chunks,)),
            dma((8,)),
            dma((8,)),
            dma((count - 1,)),
            dma((count - 1,)),
            dma((3,)),
            dma((3,)),
            dma((count + 2,)),
            dma((count + 2,)),
            pltpu.VMEM((planes, shard_rows, 2 * width), BF16),
            dma((planes,)),
            dma((planes,)),
            *scatter_scratch(planes, shard_rows, width),
        ],
        compiler_params=pltpu.CompilerParams(
            collective_id=2, has_side_effects=True, vmem_limit_bytes=48 << 20
        ),
    )(*args, squares)


def weight_grad_kernel(first_ref, grad_ref, branch_ref, out_ref, result_ref):
    cols = grad_ref.shape[1]
    result = dot32(first_ref[...], grad_ref[0], ((0,), (1,)))
    result_ref[:, :cols] = result.astype(BF16)
    result = dot32(branch_ref[...], out_ref[0], ((0,), (1,)))
    result_ref[:, cols:] = result.astype(BF16)


def weight_grad(first, grad, branch, out):
    pair, _, length = grad.shape
    more = out.shape[1]
    cols = 3 * more
    width = first.shape[1]
    block = 384
    rows = pl.BlockSpec((length, block), lambda y, i: (0, i))
    return pl.pallas_call(
        weight_grad_kernel,
        grid=(pair, width // block),
        in_specs=[
            rows,
            pl.BlockSpec((1, cols, length), lambda y, i: (y, 0, 0)),
            rows,
            pl.BlockSpec((1, more, length), lambda y, i: (y, 0, 0)),
        ],
        out_specs=pl.BlockSpec((block, cols + more), lambda y, i: (i, y)),
        out_shape=jax.ShapeDtypeStruct((width, pair * (cols + more)), BF16),
        compiler_params=pltpu.CompilerParams(vmem_limit_bytes=40 << 20),
    )(first, grad, branch, out)


def adam_step(weight, moment, second, average, gradient, rate):
    moment = 0.5 * moment + 0.5 * gradient
    second = 0.5 * second + 0.5 * gradient * gradient
    correct = 1.0 - 0.5**STEP
    weight = weight - rate * (
        moment / correct / (jnp.sqrt(second / correct) + 1e-08) + 0.1 * weight
    )
    keep_rate = min(0.9999, (1.0 + STEP) / (10.0 + STEP))
    average = keep_rate * average + (1.0 - keep_rate) * weight
    return (moment, second, weight, average)


def swap(value, axis, bit):
    count = lax.axis_size(axis)
    return lax.ppermute(value, axis, [(i, i ^ bit) for i in range(count)])


def spread_rows(own):
    place = lax.axis_index("tp")
    rows = own.shape[0]
    half = rows // 2
    beside = swap(own, "tp", 1)
    across = swap(own, "tp", 2)
    far = jnp.concatenate([swap(across[:half], "tp", 1), swap(beside[half:], "tp", 2)])
    whole = jnp.zeros((4 * rows, own.shape[1]), own.dtype)
    for bits, part in ((0, own), (1, beside), (2, across), (3, far)):
        whole = lax.dynamic_update_slice(whole, part, ((place ^ bits) * rows, 0))
    return whole


def per_device(
    tokens,
    cotangent,
    quarter_ids,
    labels,
    timesteps,
    qkv_weight,
    qkv_moment,
    qkv_second,
    qkv_average,
    proj_weight,
    proj_moment,
    proj_second,
    proj_average,
    up_weight,
    up_moment,
    up_second,
    up_average,
    down_weight,
    down_moment,
    down_second,
    down_average,
    ada_weight,
    ada_moment,
    ada_second,
    ada_average,
    table_weight,
    table_moment,
    table_second,
    table_average,
):
    row_count, width = tokens.shape
    slot_count = quarter_ids.shape[0]
    small_len = row_count // slot_count
    span_len = row_count // 2
    own_len = row_count // 4
    shard_rows, _, quarter_width = qkv_weight.shape
    heads = quarter_width // HD
    tp_place = lax.axis_index("tp")
    dp_place = lax.axis_index("dp")
    span = tp_place // 2
    side = tp_place % 2

    attn_block = jnp.concatenate(
        [qkv_weight[:, 0], qkv_weight[:, 1], qkv_weight[:, 2], proj_weight.T], axis=1
    ).astype(BF16)
    planes = lax.axis_size("dp") // 2
    marks = jnp.concatenate(
        [
            jnp.broadcast_to(labels[:, None], (slot_count, 64)),
            jnp.broadcast_to(timesteps[:, None], (slot_count, 64)),
        ],
        axis=1,
    )
    column = dp_place * shard_rows + jnp.arange(shard_rows, dtype=jnp.int32)
    half_width = width // 2
    freqs = jnp.stack(
        [
            jnp.exp(-math.log(10000.0) * (column % half_width).astype(F32) / half_width),
            (column < half_width).astype(F32),
        ]
    )
    w_ada = ada_weight.transpose(1, 0, 2).astype(BF16)
    classes = table_weight.shape[0]
    table_low = jnp.pad(table_weight.T.astype(BF16), ((0, 0), (0, -classes % 128)))
    mod_parts, marks, embed, cond_low, w_attn = front(
        marks, freqs, table_low, w_ada, attn_block, planes
    )
    w_attn = w_attn.reshape(width, 8 * quarter_width)
    w_proj = jnp.stack(
        [w_attn[:, (4 * i + 3) * quarter_width : (4 * i + 4) * quarter_width].T for i in range(2)]
    )
    class_onehot = marks[:, 0:1] == jnp.arange(classes, dtype=jnp.int32)[None, :]
    modulation = mod_parts.reshape(4, 6, slot_count, quarter_width)
    modulation = modulation.transpose(2, 1, 0, 3).reshape(slot_count, 6, width)
    slot_base = dp_place * slot_count
    choose = (
        quarter_ids[:, None] - slot_base == jnp.arange(slot_count, dtype=jnp.int32)[None, :]
    ).astype(F32)
    quarter_mod = jnp.einsum("ps,ske->pke", choose, modulation, precision=HIGHEST)

    def own_first(array, size):
        mine = lax.dynamic_slice_in_dim(array, (span * 2 + side) * size, size, 0)
        other = lax.dynamic_slice_in_dim(array, (span * 2 + 1 - side) * size, size, 0)
        return jnp.concatenate([mine, other], axis=0)

    quarters = slot_count // 4
    mods = own_first(quarter_mod, quarters)
    ids = own_first(quarter_ids, quarters)
    rows = own_first(tokens, own_len)
    grad_rows = own_first(cotangent, own_len)

    def per_token(index, count):
        return mods[:count, index][:, None, :]

    def blocks(array):
        return array.reshape(-1, small_len, width)

    rows_in = blocks(rows.astype(F32))
    hat, rstd = norm_parts(rows_in)
    first_in = (hat * (1.0 + per_token(1, None)) + per_token(0, None)).astype(BF16)
    first_in = first_in.reshape(span_len, width)
    qkv = jnp.einsum("nd,dc->cn", first_in, w_attn, preferred_element_type=F32).astype(BF16)
    qkv = qkv.reshape(2, 4, heads, HD, span_len)
    attended, log_total, branch, second_in, w_up, w_down = middle(
        ids,
        qkv,
        w_proj,
        rows[:own_len],
        jnp.stack([mods[:quarters, index] for index in (2, 3, 4)]),
        up_weight.astype(BF16),
        down_weight.T.astype(BF16),
        planes,
        small_len,
    )
    w_up = w_up.reshape(width, 8 * quarter_width)
    w_down = w_down.reshape(width, 8 * quarter_width)
    head_out = attended.reshape(2 * heads, HD, span_len)
    branch = blocks(branch)

    own_grad = blocks(grad_rows[:own_len].astype(F32))
    middle_rows = blocks(rows[:own_len].astype(F32)) + per_token(2, quarters) * branch
    hat_two, rstd_two = norm_parts(middle_rows)
    grad_mixed = (blocks(grad_rows.astype(F32)) * per_token(5, None)).astype(BF16)
    grad_mixed = grad_mixed.reshape(span_len, width)
    mixed, far_mixed, grad_second, grad_up, grad_down = mlp(
        second_in, grad_mixed, w_up, w_down, planes
    )
    grad_second = blocks(grad_second)
    grad_shift_two = jnp.sum(grad_second, axis=1)
    grad_scale_two = jnp.sum(grad_second * hat_two, axis=1)
    grad_middle = own_grad + norm_back(
        hat_two, rstd_two, grad_second * (1.0 + per_token(4, quarters))
    )
    grad_gate_one = jnp.sum(grad_middle * branch, axis=1)

    own_branch = (grad_middle * per_token(2, quarters)).astype(BF16).reshape(own_len, width)
    grad_qkv, grad_branch, far_mixed, up_reduced, down_reduced = back(
        ids,
        qkv,
        head_out,
        log_total,
        w_proj,
        own_branch,
        far_mixed,
        grad_up,
        grad_down,
        planes,
        small_len,
    )
    mixed = blocks(mixed + far_mixed.astype(F32))
    block_out = (middle_rows + per_token(5, quarters) * mixed).astype(BF16).reshape(own_len, width)
    block_out = spread_rows(block_out)
    grad_gate_two = jnp.sum(own_grad * mixed, axis=1)
    first_part = jnp.einsum(
        "cn,dc->nd",
        grad_qkv.reshape(8 * quarter_width, span_len),
        w_attn,
        preferred_element_type=F32,
    )
    grad_attn = weight_grad(first_in, grad_qkv, grad_branch, attended)
    squares = jnp.sum(up_reduced * up_reduced) + jnp.sum(down_reduced * down_reduced)

    rest = jnp.stack([grad_gate_one, grad_shift_two, grad_scale_two, grad_gate_two])
    rest = rest.reshape(4 * quarters, 4, quarter_width).transpose(1, 0, 2)
    chosen = choose.reshape(4, quarters, slot_count).transpose(2, 0, 1)
    pick_rest = (
        jnp.eye(4, dtype=F32)[:, None, None, :, None] * chosen[None, :, :, None, :]
    ).reshape(4 * slot_count, 16 * quarters)
    pick_first = (
        jnp.eye(2, 4, dtype=F32)[:, None, None, :, None] * chosen[None, :, :, None, :]
    ).reshape(2 * slot_count, 16 * quarters)
    pick = jnp.concatenate(
        [jnp.pad(pick_first, ((0, 0), (32, 0))), jnp.pad(pick_rest, ((0, 0), (0, 32)))]
    )
    token_grad, attn_reduced, grad_ada, grad_embed, grad_norm = tail(
        rows[:own_len],
        mods[:quarters, 1],
        first_part[:own_len],
        first_part[own_len:].astype(BF16),
        grad_middle.reshape(own_len, width),
        grad_attn.reshape(planes, 2, shard_rows, 2 * width),
        rest,
        pick,
        w_ada,
        cond_low,
        embed,
        marks,
        squares.reshape(1, 1),
        small_len,
    )
    token_grad = token_grad.reshape(row_count, width)
    grad_ada = grad_ada.transpose(1, 0, 2)
    grad_norm = grad_norm[0, 0]
    grad_table = jnp.einsum("qc,qd->cd", class_onehot.astype(F32), grad_embed, precision=HIGHEST)
    down_reduced = down_reduced.T
    qkv_reduced = attn_reduced[:, : 3 * quarter_width].reshape(shard_rows, 3, quarter_width)
    proj_reduced = attn_reduced[:, 3 * quarter_width :].T
    factor = jnp.minimum(1.0, clip_limit / (grad_norm + 1e-06))
    qkv_new = adam_step(
        qkv_weight, qkv_moment, qkv_second, qkv_average, qkv_reduced * factor, 0.5 * D ** (-0.5)
    )
    proj_new = adam_step(
        proj_weight,
        proj_moment,
        proj_second,
        proj_average,
        proj_reduced * factor,
        4.0 * D ** (-0.5),
    )
    up_new = adam_step(
        up_weight, up_moment, up_second, up_average, up_reduced * factor, 0.5 * D ** (-0.5)
    )
    down_new = adam_step(
        down_weight,
        down_moment,
        down_second,
        down_average,
        down_reduced * factor,
        0.5 * FF ** (-0.5),
    )
    ada_new = adam_step(
        ada_weight, ada_moment, ada_second, ada_average, grad_ada * factor, 0.5 * D ** (-0.5)
    )
    table_new = adam_step(
        table_weight, table_moment, table_second, table_average, grad_table * factor, 0.5
    )
    return (
        block_out,
        token_grad,
        grad_norm,
        *qkv_new,
        *proj_new,
        *up_new,
        *down_new,
        *ada_new,
        *table_new,
    )


def solution(mesh):
    rows = P("dp", None)
    marks = P("dp")
    cubes = (P("dp", None, "tp"),) * 4
    across = (P("tp", "dp"),) * 4
    along = (P("dp", "tp"),) * 4
    table = (P(None, "dp"),) * 4
    states = (*cubes, *across, *along, *across, *cubes, *table)
    return jax.shard_map(
        per_device,
        mesh=mesh,
        in_specs=(rows, rows, marks, marks, marks, *states),
        out_specs=(rows, rows, P(), *states),
        check_vma=False,
    )
```

time: 831 us -> 524 us (0.63)
  Pallas kernels: 186 us -> 389 us
  blocking collectives: 158 us -> 0 us
  waiting for transfers between devices: 143 us -> 5.78 us
  matrix products: 99.9 us -> 16.9 us
  local copies, waits for them, and re-layouts: 86.6 us -> 40 us
  starting transfers between devices: 48.9 us -> 4.34 us
  other arithmetic: 92.5 us -> 58.4 us
    pallas_call x2 -> x5, Pallas kernels: 51.2 us -> 335 us  [the longest x1 102 us: tail(): pl.pallas_call(functools.partial(tail_kernel, planes, small_len), in_spec...]
    ppermute x16 -> x4, waiting for transfers between devices: 121 us -> 5.78 us  [swap(): return lax.ppermute(value, axis, [(i, i ^ bit) for i in range(count)])]
    psum x2 -> x0, blocking collectives: 91.3 us -> none  [the longest x1 75.1 us: per_device(): grad_norm = jnp.sqrt(lax.psum(local_squares, ('tp', 'dp')))]
    dot_general x15 -> x2, matrix products: 97.7 us -> 14.3 us  [the longest x1 7.96 us: per_device(): jnp.einsum('nd,dc->cn', first_in, w_attn, preferred_element_type=F32)]
    pallas_call x1, Pallas kernels: 135 us -> 54 us  [front(): pl.pallas_call(functools.partial(front_kernel, planes), in_specs=[vmem, v...]
    all_gather x2 -> x0, blocking collectives: 67.1 us -> none  [the longest x1 50.4 us: per_device(): grad_quarter = lax.all_gather(grad_quarter, 'tp', axis=0, tiled=True)]
    ppermute x9 -> x0, starting transfers between devices: 34.2 us -> none  [shift(): lax.ppermute(value, 'dp', [(i, (i + 2 * steps) % count) for i in range(co...]
    ppermute x9 -> x0, waiting for transfers between devices: 21.4 us -> none  [shift(): lax.ppermute(value, 'dp', [(i, (i + 2 * steps) % count) for i in range(co...]
  transfers between devices with their start and end apart: 25 -> 4, of which waited for: 11 -> 2; matrix products, arithmetic and copies ran while one was open for 22% -> 8% of each run, Pallas kernels for 3% -> 22%
where the time goes in v3:
time: 524 us; the launch traced here: 518 us
  Pallas kernels  389 us (74%)
  other arithmetic  58.4 us (11%)
  local copies, waits for them, and re-layouts  40 us (8%)
  matrix products  16.9 us (3%)
  waiting for transfers between devices  5.78 us (1%)
    pallas_call x1, Pallas kernels, tail(): pl.pallas_call(functools.partial(tail_kernel, planes, small_len), in_spec...  102 us
    pallas_call x1, Pallas kernels, back(): pl.pallas_call(functools.partial(back_kernel, planes, small_len), in_spec...  88.4 us
    pallas_call x1, Pallas kernels, middle(): pl.pallas_call(functools.partial(middle_kernel, planes, small_len), in_sp...  82.9 us
    pallas_call x1, Pallas kernels, front(): pl.pallas_call(functools.partial(front_kernel, planes), in_specs=[vmem, v...  54 us
    pallas_call x1, Pallas kernels, mlp(): pl.pallas_call(functools.partial(mlp_kernel, planes), grid=(3, tiles), in...  50.2 us
    unnamed x141, local copies, waits for them, and re-layouts  23.4 us
    add x5, other arithmetic, adam_step(): average = keep_rate * average + (1.0 - keep_rate) * weight  12.9 us
    pallas_call x1, Pallas kernels, weight_grad(): pl.pallas_call(weight_grad_kernel, grid=(pair, width // block), in_specs=...  11.2 us
  transfers between devices with their start and end apart: 4, of which 2 were waited for; matrix products, arithmetic and copies ran while one was open for 8% of the time, Pallas kernels for 22%

profile of v3, /device:TPU:0, one launch (start us, length us, event | category | flops | bytes accessed | tf_op | source)
XLA Modules:
  0.0 518.0 jit_solution(10161441363344706297)
XLA Ops:
  0.8 4.6 constant_dynamic-slice_fusion.5
  5.8 2.5 fusion.26
  12.4 54.0 %shard_map.484 = (f32[4,48,288]{2,1,0:T(8,128)S(1)}, s32[64,128]{1,0:T(8,128)S(1)}, f32[64,144]{1,0:T(8,128)S(1)}, bf16[64,144]{1,0:T(8,128)(2,1)S(1)}, bf16[4,2,144,2304]{3,2,1,0:T(8,128)(2,1)S(1)}) custom-call(s32[8,128]{1,0:T(8,128)S(1)} %pad_add_fusion.marks_ref, f32[2,144]{1,0:T(2,128)S(1)} %pad_maximum_fusion.5.freqs_ref, ...), custom_call_target="tpu_custom_call" | custom-call | tf_op jit(solution)/shard_map/pallas_call | solution.py:389
  69.5 3.4 fusion.36
  72.9 4.5 add_convert_fusion
  77.5 8.0 %convolution_convert_fusion = bf16[2304,1024]{1,0:T(8,128)(2,1)} fusion(bf16[1152,2304]{1,0:T(8,128)(2,1)S(1)} %bitcast.149, bf16[1024,1152]{1,0:T(8,128)(2,1)S(1)} %bitcast.164), kind=kOutput, calls=%fused_computation | convolution fusion | flops 5438177280 | bytes 12386304 | tf_op jit(solution)/shard_map/nd,dc->cn/dot_general | solution.py:1444
  92.2 82.9 %shard_map.485 = (bf16[2,288,1024]{2,1,0:T(8,128)(2,1)S(1)}, f32[8,1,1024]{2,1,0:T(1,128)S(1)}, f32[512,1152]{1,0:T(8,128)}, bf16[1024,1152]{1,0:T(8,128)(2,1)},...) custom-call(s32[4]{0:T(128)S(1)} %pad_add_fusion.1.ids_ref, bf16[2,4,4,72,1024]{4,3,2,1,0:T(8,128)(2,1)} %bitcast.157, ...), custom_call_target="tpu_custom_call" | custom-call | tf_op jit(solution)/shard_map/pallas_call | solution.py:527
  175.2 2.5 fusion.34
  182.1 50.2 %shard_map.486 = (f32[512,1152]{1,0:T(8,128)}, bf16[512,1152]{1,0:T(8,128)(2,1)}, f32[512,1152]{1,0:T(8,128)}, bf16[4,144,2304]{2,1,0:T(8,128)(2,1)}, bf16[4,144,2304]{2,1,0:T(8,128)(2,1)}) custom-call(bf16[1024,1152]{1,0:T(8,128)(2,1)} %get-tuple-element.56.second_ref, bf16[1024,1152]{1,0:T(8,128)(2,1)} %fusion.1.mixed_grad_ref, ...), custom_call_target="tpu_custom_call" | custom-call | tf_op jit(solution)/shard_map/pallas_call | solution.py:705
  232.4 3.2 fusion.7
  235.6 5.4 %fusion.3 = (bf16[512,1152]{1,0:T(8,128)(2,1)}, f32[512,1152]{1,0:T(8,128)}) fusion(f32[2,1152]{1,0:T(2,128)S(1)} %copy-done.52, f32[512]{0:T(512)S(1)} %broadcast_multiply_fusion.3, f32[512,1152]{1,0:T(8,128)} %copy-done.13, f32[512]{0:T(512)S(1)} %copy-done.55, f32[512]{0:T(512)S(1)} %broadcast_multiply_fusion.4, f32[512,1152]{1,0:T(8,128)} %get-tuple-element.62, ...), kind=kLoop, calls=%fused_computation.12 | loop fusion | flops 6488064 | bytes 9463808 | tf_op jit(solution)/shard_map/convert_element_type | solution.py:1478
  241.1 88.4 %shard_map.487 = (bf16[2,1152,1024]{2,1,0:T(8,128)(2,1)}, bf16[1024,1152]{1,0:T(8,128)(2,1)}, bf16[512,1152]{1,0:T(8,128)(2,1)}, f32[144,1152]{1,0:T(8,128)}, f32[144,1152]{1,0:T(8,128)}) custom-call(s32[4]{0:T(128)} %copy-done.12, bf16[2,4,4,72,1024]{4,3,2,1,0:T(8,128)(2,1)} %bitcast.158, bf16[8,72,1024]{2,1,0:T(8,128)(2,1)} %bitcast.147, ...), custom_call_target="tpu_custom_call" | custom-call | tf_op jit(solution)/shard_map/pallas_call | solution.py:927
  329.5 4.5 multiply_reduce_fusion.2
  337.8 3.1 fusion.first_ref
  341.2 6.3 %fusion.38 = f32[1024,1152]{1,0:T(8,128)S(1)} fusion(bf16[2304,1024]{1,0:T(8,128)(2,1)S(1)} %bitcast.146, bf16[1152,2304]{1,0:T(8,128)(2,1)S(1)} %bitcast.152), kind=kOutput, calls=%fused_computation.136 | convolution fusion | flops 5435817984 | bytes 14745600 | tf_op jit(solution)/shard_map/cn,dc->nd/dot_general | solution.py:1496
  362.1 11.2 %shard_map.488 = bf16[1152,2304]{1,0:T(8,128)(2,1)} custom-call(bf16[1024,1152]{1,0:T(8,128)(2,1)S(1)} %copy-done.1, bf16[2,1152,1024]{2,1,0:T(8,128)(2,1)S(1)} %copy-done.2, bf16[1024,1152]{1,0:T(8,128)(2,1)S(1)} %copy-done.5, bf16[2,288,1024]{2,1,0:T(8,128)(2,1)S(1)} %copy-done.4), custom_call_target="tpu_custom_call" | custom-call | tf_op jit(solution)/shard_map/pallas_call | solution.py:1297
  373.4 101.9 %shard_map.489 = (bf16[4,512,1152]{2,1,0:T(8,128)(2,1)}, f32[144,1152]{1,0:T(8,128)S(1)}, f32[6,144,288]{2,1,0:T(8,128)S(1)}, f32[64,144]{1,0:T(8,128)S(1)}, f32[8,128]{1,0:T(8,128)S(1)}) custom-call(bf16[512,1152]{1,0:T(8,128)(2,1)S(1)} %get-tuple-element.146.tokens_ref, f32[2,1152]{1,0:T(2,128)S(1)} %get-tuple-element.151.scale_ref, ...), custom_call_target="tpu_custom_call" | custom-call | tf_op jit(solution)/shard_map/pallas_call | solution.py:1238
  480.0 3.6 multiply_add_fusion.7
  486.0 2.4 multiply_add_fusion.10
  489.1 3.3 multiply_add_fusion.2
  501.2 2.4 constant_dynamic-update-slice_fusion.1
  503.6 2.4 constant_dynamic-update-slice_fusion
  506.0 3.8 collective-permute-done.2
  512.8 4.9 copy.96
  (221 shorter events, 54.8 us)
Async XLA Ops:
  10.9 58.2 %copy-start.60 = (s32[8]{0:T(128)S(1)}, s32[8]{0:T(128)}, u32[]{:S(2)}) copy-start(s32[8]{0:T(128)} %param.31) | copy-start | bytes 100
  69.1 8.4 %copy-start.61 = (s32[8]{0:T(128)}, s32[8]{0:T(128)S(1)}, u32[]{:S(2)}) copy-start(s32[8]{0:T(128)S(1)} %broadcast_subtract_fusion) | copy-start | bytes 100
  72.9 4.5 copy-start.10
  91.3 83.8 %copy-start.12 = (s32[4]{0:T(128)}, s32[4]{0:T(128)S(1)}, u32[]{:S(2)}) copy-start(s32[4]{0:T(128)S(1)} %pad_add_fusion.1.ids_ref) | copy-start | bytes 52
  91.4 83.7 %copy-start = (bf16[2,288,1152]{2,1,0:T(8,128)(2,1)}, bf16[2,288,1152]{2,1,0:T(8,128)(2,1)S(1)}, u32[]{:S(2)}) copy-start(bf16[2,288,1152]{2,1,0:T(8,128)(2,1)S(1)} %pad_maximum_fusion.1.proj_ref) | copy-start | bytes 3981316
  92.2 83.0 %copy-start.51 = (f32[2,1152]{1,0:T(2,128)}, f32[2,1152]{1,0:T(2,128)S(1)}, u32[]{:S(2)}) copy-start(f32[2,1152]{1,0:T(2,128)S(1)} %get-tuple-element.157) | copy-start | bytes 27652
  241.1 88.4 %copy-start.17 = (f32[512,1152]{1,0:T(8,128)S(1)}, f32[512,1152]{1,0:T(8,128)}, u32[]{:S(2)}) copy-start(f32[512,1152]{1,0:T(8,128)} %get-tuple-element.62) | copy-start | bytes 7077892
  329.5 4.9 copy-start.14
  329.5 4.9 copy-start.56
  334.0 6.9 %slice-start = ((s8[4718592]{0:T(1024)(128)(4,1)}), s8[4194304]{0:T(1024)(128)(4,1)S(1)}, s32[]{:S(2)}) async-start(s8[4718592]{0:T(1024)(128)(4,1)} %bitcast.144), calls=%async_computation | async-start | bytes 8388608
  334.0 6.9 %slice-start.2 = ((s8[5308416]{0:T(1024)(128)(4,1)}), s8[4194304]{0:T(1024)(128)(4,1)S(1)}, s32[]{:S(2)}) async-start(s8[5308416]{0:T(1024)(128)(4,1)} %bitcast.150), calls=%async_computation.2 | async-start | bytes 8388608
  334.4 6.5 %slice-start.1 = ((s8[4718592]{0:T(1024)(128)(4,1)}), s8[524288]{0:T(1024)(128)(4,1)S(1)}, s32[]{:S(2)}) async-start(s8[4718592]{0:T(1024)(128)(4,1)} %bitcast.144), calls=%async_computation.1 | async-start | bytes 1048576
  334.4 6.7 %slice-start.3 = ((s8[5308416]{0:T(1024)(128)(4,1)}), s8[1114112]{0:T(1024)(128)(4,1)S(1)}, s32[]{:S(2)}) async-start(s8[5308416]{0:T(1024)(128)(4,1)} %bitcast.150), calls=%async_computation.3 | async-start | bytes 2228224
  335.8 5.1 copy-start.23
  335.8 161.3 %collective-permute-start = (bf16[512,1152]{1,0:T(8,128)(2,1)}, bf16[512,1152]{1,0:T(8,128)(2,1)}, u32[]{:S(2)}, u32[]{:S(2)}) collective-permute-start(bf16[512,1152]{1,0:T(8,128)(2,1)} %get-tuple-element.166), channel_id=1, source_target_pairs={{0,8},{8,0},{16,24},{24,16},{1,9},{9,1},{17,25},{25,17},{2,10},{10... | collective-permute-start | bytes 3538952 | tf_op jit(solution)/shard_map/ppermute | solution.py:1326
  336.1 158.4 %collective-permute-start.1 = (bf16[512,1152]{1,0:T(8,128)(2,1)}, bf16[512,1152]{1,0:T(8,128)(2,1)}, u32[]{:S(2)}, u32[]{:S(2)}) collective-permute-start(bf16[512,1152]{1,0:T(8,128)(2,1)} %get-tuple-element.166), channel_id=1, source_target_pairs={{0,16},{8,24},{16,0},{24,8},{1,17},{9,25},{17,1},{25,9},{2,18},{10... | collective-permute-start | bytes 3538952 | tf_op jit(solution)/shard_map/ppermute | solution.py:1326
  483.7 4.7 copy-start.35
  483.7 4.7 copy-start.36
  494.4 4.7 copy-start.38
  494.4 4.7 copy-start.48
  494.4 4.7 copy-start.49
  494.4 4.7 copy-start.50
  495.7 14.1 %collective-permute-start.2 = (bf16[256,1152]{1,0:T(8,128)(2,1)S(1)}, bf16[256,1152]{1,0:T(8,128)(2,1)S(1)}, u32[]{:S(2)}, u32[]{:S(2)}) collective-permute-start(bf16[256,1152]{1,0:T(8,128)(2,1)S(1)} %slice.96), channel_id=1, source_target_pairs={{0,8},{8,0},{16,24},{24,16},{1,9},{9,1},{17,25},{25,17},{2,10},{10... | collective-permute-start | bytes 1769480 | tf_op jit(solution)/shard_map/ppermute | solution.py:1326
  498.2 13.5 %collective-permute-start.3 = (bf16[256,1152]{1,0:T(8,128)(2,1)S(1)}, bf16[256,1152]{1,0:T(8,128)(2,1)S(1)}, u32[]{:S(2)}, u32[]{:S(2)}) collective-permute-start(bf16[256,1152]{1,0:T(8,128)(2,1)S(1)} %slice.97), channel_id=1, source_target_pairs={{0,16},{8,24},{16,0},{24,8},{1,17},{9,25},{17,1},{25,9},{2,18},{10... | collective-permute-start | bytes 1769480 | tf_op jit(solution)/shard_map/ppermute | solution.py:1326
  (49 other events, 125.5 us)

commit v4 on v3

v4 whole, which is shorter than its diff:
```python
import functools
import math

import jax
import jax.numpy as jnp
from jax import lax
from jax.experimental import pallas as pl
from jax.experimental.pallas import tpu as pltpu
from jax.sharding import PartitionSpec as P

D = 1152
HD = 72
FF = 4608
STEP = 5

HIGHEST = lax.Precision.HIGHEST
F32 = jnp.float32
BF16 = jnp.bfloat16
clip_limit = 1.0
HEAD_SCALE = HD**-0.5
LOG2_SCALE = HEAD_SCALE * math.log2(math.e)


def dot32(a, b, dims):
    return lax.dot_general(a, b, (dims, ((), ())), preferred_element_type=F32)


def norm_parts(values):
    centre = values - jnp.mean(values, axis=-1, keepdims=True)
    spread = jnp.mean(centre * centre, axis=-1, keepdims=True)
    rstd = lax.rsqrt(spread + 1e-06)
    return centre * rstd, rstd


def norm_back(hat, rstd, grad_hat):
    first = jnp.mean(grad_hat, axis=-1, keepdims=True)
    second = jnp.mean(grad_hat * hat, axis=-1, keepdims=True)
    return rstd * (grad_hat - first - hat * second)


def time_embed(stamps, width):
    half_width = width // 2
    freqs = jnp.exp(-math.log(10000.0) * jnp.arange(half_width, dtype=jnp.float32) / half_width)
    angles = (stamps.astype(jnp.float32) / 1000.0)[:, None] * freqs[None, :]
    return jnp.concatenate([jnp.cos(angles), jnp.sin(angles)], axis=-1)


def attend_softmax(scores, same, small_len):
    count = len(same)
    blocks = [scores[kb * small_len : (kb + 1) * small_len] for kb in range(count)]
    top = jnp.full((1, small_len), -jnp.inf, F32)
    for kb in range(count):
        block_top = jnp.max(blocks[kb], axis=0, keepdims=True)
        top = jnp.maximum(top, jnp.where(same[kb], block_top, -jnp.inf))
    top = top * LOG2_SCALE
    total = jnp.zeros((1, small_len), F32)
    probs = []
    for kb in range(count):
        base = top + jnp.where(same[kb], 0.0, 1e9)
        expo = jnp.exp2(blocks[kb] * LOG2_SCALE - base)
        total = total + jnp.sum(expo, axis=0, keepdims=True)
        probs.append(expo.astype(BF16))
    return jnp.concatenate(probs, axis=0), total, top


def attend_quarters(ids_ref, qkv_ref, out_ref, log_ref, pair, quarters, small_len):
    heads = qkv_ref.shape[2]
    count = qkv_ref.shape[-1] // small_len
    units = [(qb, h) for qb in quarters for h in range(heads)]
    scores, probs, outs = {}, {}, []
    for i in range(len(units) + 2):
        if i < len(units):
            qb, h = units[i]
            queries = qkv_ref[pair, 0, h, :, pl.ds(qb * small_len, small_len)]
            scores[i] = dot32(qkv_ref[pair, 1, h], queries, ((0,), (0,)))
        if i >= 2:
            qb, h = units[i - 2]
            cols = pl.ds(qb * small_len, small_len)
            low, total, top = probs.pop(i - 2)
            mixed = dot32(qkv_ref[pair, 2, h], low, ((1,), (0,)))
            outs.append(mixed / total)
            log_ref[pair * heads + h, :, cols] = top + jnp.log2(total)
            if h == heads - 1:
                out_ref[pair, :, cols] = jnp.concatenate(outs, axis=0).astype(BF16)
                outs = []
        if 1 <= i <= len(units):
            qb, h = units[i - 1]
            same = [ids_ref[kb] == ids_ref[qb] for kb in range(count)]
            probs[i - 1] = attend_softmax(scores.pop(i - 1), same, small_len)


def back_quarters(
    ids_ref, qkv_ref, out_ref, log_ref, go_ref, gq_ref, gk_ref, gv_ref, pair, quarters, small_len, add
):
    heads = qkv_ref.shape[2]
    count = qkv_ref.shape[-1] // small_len
    units = [(qb, h) for qb in quarters for h in range(heads)]
    firsts, seconds, deltas, outs = {}, {}, {}, []
    for i in range(len(units) + 2):
        if i < len(units):
            qb, h = units[i]
            cols = pl.ds(qb * small_len, small_len)
            rows = pl.ds(h * HD, HD)
            grad_out = go_ref[pair, rows, cols]
            firsts[i] = (
                dot32(qkv_ref[pair, 1, h], qkv_ref[pair, 0, h, :, cols], ((0,), (0,))),
                dot32(qkv_ref[pair, 2, h], grad_out.astype(BF16), ((0,), (0,))),
            )
        if i >= 2:
            qb, h = units[i - 2]
            cols = pl.ds(qb * small_len, small_len)
            rows = pl.ds(h * HD, HD)
            probs, scores = seconds.pop(i - 2)
            grad_q = dot32(qkv_ref[pair, 1, h], scores, ((1,), (0,)))
            outs.append(grad_q * HEAD_SCALE)
            grad_k = dot32(qkv_ref[pair, 0, h, :, cols], scores, ((1,), (1,)))
            grad_v = dot32(go_ref[pair, rows, cols].astype(BF16), probs, ((1,), (1,)))
            if add or qb != quarters[0]:
                gk_ref[pair, rows] += grad_k
                gv_ref[pair, rows] += grad_v
            else:
                gk_ref[pair, rows] = grad_k
                gv_ref[pair, rows] = grad_v
            if h == heads - 1:
                place = pl.ds(0, heads * HD)
                gq_ref[pair, place, cols] = jnp.concatenate(outs, axis=0).astype(BF16)
                outs = []
        if 1 <= i <= len(units):
            qb, h = units[i - 1]
            cols = pl.ds(qb * small_len, small_len)
            scores, grad_prob = firsts.pop(i - 1)
            if qb not in deltas:
                deltas[qb] = go_ref[pair, :, cols] * out_ref[pair, :, cols].astype(F32)
            delta = jnp.sum(deltas[qb][h * HD : (h + 1) * HD], axis=0, keepdims=True)
            probs_low, score_low = [], []
            for kb in range(count):
                part = slice(kb * small_len, (kb + 1) * small_len)
                base = log_ref[pair * heads + h, :, cols] + jnp.where(
                    ids_ref[kb] == ids_ref[qb], 0.0, 1e9
                )
                probs = jnp.exp2(scores[part] * LOG2_SCALE - base)
                probs_low.append(probs.astype(BF16))
                score_low.append((probs * (grad_prob[part] - delta)).astype(BF16))
            seconds[i - 1] = (
                jnp.concatenate(probs_low, axis=0),
                jnp.concatenate(score_low, axis=0),
            )


MESH = pl.DeviceIdType.MESH


def remote(src, dst, send_sem, recv_sem, tp, dp):
    return pltpu.make_async_remote_copy(
        src_ref=src,
        dst_ref=dst,
        send_sem=send_sem,
        recv_sem=recv_sem,
        device_id=(tp, dp),
        device_id_type=MESH,
    )


def greet(peers):
    barrier = pltpu.get_barrier_semaphore()
    for tp, dp in peers:
        pl.semaphore_signal(barrier, inc=1, device_id=(tp, dp), device_id_type=MESH)
    pl.semaphore_wait(barrier, len(peers))


def other_core(dp):
    return dp + 1 - 2 * lax.rem(dp, 2)


def x_neighbour(tp):
    return tp + 1 - 2 * lax.rem(tp, 2)


def y_neighbour(tp):
    return lax.rem(tp + 2, 4)


class GatherRows:
    def __init__(self, block, whole, sems, planes):
        self.block, self.whole, self.planes = block, whole, planes
        self.local, self.sends, self.recvs = sems
        self.tp, self.dp = lax.axis_index("tp"), lax.axis_index("dp")
        self.core = lax.rem(self.dp, 2)
        self.place = lax.div(self.dp, 2)

    def at(self, quarter, plane):
        cols = self.block.shape[1]
        return self.whole.at[plane, self.core, :, pl.ds(quarter * cols, cols)]

    def along(self, way, plane, own=False):
        return remote(
            self.block if own else self.at(0, plane),
            self.at(0, plane),
            self.sends.at[plane + (self.planes if way < 0 else 0)],
            self.recvs.at[plane],
            self.tp,
            self.dp + 2 * way,
        )

    def across(self, plane, own=False):
        return remote(
            self.block if own else self.at(0, plane),
            self.at(1, plane),
            self.sends.at[2 * self.planes + plane],
            self.recvs.at[self.planes + plane],
            y_neighbour(self.tp),
            self.dp,
        )

    def over(self, quarter, plane, own=False):
        return remote(
            self.block if own else self.at(quarter, plane),
            self.at(quarter, plane),
            self.sends.at[(3 + quarter) * self.planes + plane],
            self.recvs.at[(2 + quarter) * self.planes + plane],
            self.tp,
            other_core(self.dp),
        )

    def own(self):
        return pltpu.make_async_copy(self.block, self.at(0, self.place), self.local)

    def has_next(self, way):
        return self.place < self.planes - 1 if way > 0 else self.place > 0

    def start_own(self):
        self.own().start()
        self.across(self.place, True).start()
        self.over(0, self.place, True).start()

    def start_along(self):
        for way in (1, -1):

            @pl.when(self.has_next(way))
            def _():
                self.along(way, self.place, True).start()

    def relay(self, step):
        for way in (1, -1):
            plane = self.place - way * (step + 1)

            @pl.when((plane >= 0) & (plane < self.planes))
            def _():
                self.along(way, plane).wait_recv()

                @pl.when(self.has_next(way))
                def _():
                    self.along(way, plane).start()

                self.across(plane).start()
                self.over(0, plane).start()

    def relay_across(self, step):
        if step == 0:
            self.across(self.place).wait_recv()
            self.over(1, self.place).start()
            return
        for way in (1, -1):
            plane = self.place - way * step

            @pl.when((plane >= 0) & (plane < self.planes))
            def _():
                self.across(plane).wait_recv()
                self.over(1, plane).start()

    def finish(self):
        self.own().wait()
        for plane in range(self.planes):
            for way in (1, -1):

                @pl.when(self.has_next(way) & (way * plane <= way * self.place))
                def _():
                    self.along(way, plane).wait_send()

            self.across(plane).wait_send()
            for quarter in range(2):
                self.over(quarter, plane).wait_send()
                self.over(quarter, plane).wait_recv()


def gather_sems(planes):
    return [
        pltpu.SemaphoreType.DMA,
        pltpu.SemaphoreType.DMA((5 * planes,)),
        pltpu.SemaphoreType.DMA((4 * planes,)),
    ]


def front_kernel(
    planes,
    small_len,
    ids_ref,
    tokens_ref,
    cotangent_ref,
    attn_ref,
    up_ref,
    down_ref,
    marks_ref,
    freqs_ref,
    table_ref,
    ada_ref,
    pick_ref,
    marks_all_ref,
    embed_ref,
    cond_ref,
    mods_ref,
    first_ref,
    qkv_ref,
    proj_ref,
    out_ref,
    log_ref,
    branch_ref,
    second_ref,
    mixed_grad_ref,
    attn_out,
    up_out,
    down_out,
    rows,
    grads,
    hats,
    attn_all,
    attn_turned,
    branch_send,
    branch_land,
    part,
    core_land,
    pair_sum,
    landed,
    mods_all,
    load_sems,
    core_sems,
    mark_send,
    mark_recv,
    part_send,
    part_recv,
    mod_send,
    mod_recv,
    branch_sends,
    branch_recvs,
    second_sends,
    second_recvs,
    *gather_refs,
):
    tp, dp = lax.axis_index("tp"), lax.axis_index("dp")
    core, place = lax.rem(dp, 2), lax.div(dp, 2)
    count = 2 * planes
    slots = marks_ref.shape[0]
    kinds, _, cols = ada_ref.shape
    own_len, width = branch_ref.shape
    chunks = own_len // small_len
    pair, _, heads, _, length = qkv_ref.shape
    beside = x_neighbour(tp)
    around = [(tp, lax.rem(dp + step, count)) for step in range(1, count)]
    others = [(lax.rem(tp + step, 4), dp) for step in range(1, 4)]

    def chunk(index):
        return pl.ds(index * small_len, small_len)

    loads = []
    for i, (src, dst) in enumerate(((tokens_ref, rows), (cotangent_ref, grads))):
        for j, owner in enumerate((tp, beside)):
            start = pl.multiple_of(owner * own_len, own_len)
            loads.append(
                pltpu.make_async_copy(
                    src.at[pl.ds(start, own_len)],
                    dst.at[pl.ds(j * own_len, own_len)],
                    load_sems.at[2 * i + j],
                )
            )
    for load in loads:
        load.start()
    greet(around + others)
    attns = GatherRows(attn_ref, attn_all, gather_refs[:3], planes)
    ups = GatherRows(up_ref, up_out, gather_refs[3:6], planes)
    downs = GatherRows(down_ref, down_out, gather_refs[6:], planes)
    mark_copies = [
        remote(
            marks_ref,
            marks_all_ref.at[pl.ds(pl.multiple_of(dp * slots, slots), slots)],
            mark_send.at[i],
            mark_recv.at[i],
            *peer,
        )
        for i, peer in enumerate(around)
    ]
    for copy in mark_copies:
        copy.start()
    attns.start_along()
    attns.start_own()
    marks_all_ref[pl.ds(pl.multiple_of(dp * slots, slots), slots)] = marks_ref[...]
    for copy in mark_copies:
        copy.wait()

    labels = marks_all_ref[:, 0:1]
    stamps = marks_all_ref[:, 64:65].astype(F32) / 1000.0
    angles = stamps * freqs_ref[0:1]
    stamp_embed = jnp.where(freqs_ref[1:2] > 0.0, jnp.cos(angles), jnp.sin(angles))
    classes = lax.broadcasted_iota(jnp.int32, (count * slots, table_ref.shape[1]), 1)
    onehot = jnp.where(classes == labels, 1.0, 0.0).astype(BF16)
    embed = dot32(onehot, table_ref[...], ((1,), (1,))) + stamp_embed
    embed_ref[...] = embed
    cond = (embed / (1.0 + jnp.exp(-embed))).astype(BF16)
    cond_ref[...] = cond
    for kind in range(kinds):
        sums = dot32(cond, ada_ref[kind], ((1,), (0,)))
        part[:, :, kind * slots : (kind + 1) * slots, :] = sums.reshape(planes, 2, slots, cols)
    core_copy = remote(
        part.at[:, 1 - core], core_land, core_sems.at[0], core_sems.at[1], tp, other_core(dp)
    )
    core_copy.start()
    core_copy.wait()
    pair_sum[...] = part[:, core] + core_land[...]
    part_copies = [
        remote(
            pair_sum.at[lax.rem(place + step, planes)],
            landed.at[step - 1],
            part_send.at[step - 1],
            part_recv.at[step - 1],
            tp,
            lax.rem(dp + 2 * step, count),
        )
        for step in range(1, planes)
    ]
    for copy in part_copies:
        copy.start()
    attns.relay(0)
    ups.start_along()
    for copy in part_copies:
        copy.wait_recv()
    total = pair_sum[place]
    for i in range(planes - 1):
        total = total + landed[i]
    mods_all[tp] = total
    mod_copies = [
        remote(mods_all.at[tp], mods_all.at[tp], mod_send.at[i], mod_recv.at[i], *peer)
        for i, peer in enumerate(others)
    ]
    for copy in mod_copies:
        copy.start()
    attns.relay(1)
    ups.start_own()
    for load in loads:
        load.wait()
    for i in range(2 * chunks):
        hats[chunk(i)] = norm_parts(rows[chunk(i)].astype(F32))[0]
    for step in range(2, planes - 1):
        attns.relay(step)
    downs.start_along()
    downs.start_own()
    for copy in mod_copies:
        copy.wait()
    for owner in range(4):
        mods_ref[:, owner * cols : (owner + 1) * cols] = lax.dot_general(
            pick_ref[...],
            mods_all[owner],
            (((1,), (0,)), ((), ())),
            precision=HIGHEST,
            preferred_element_type=F32,
        )

    def mod(kind, quarter):
        row = kind * 2 * chunks + quarter
        return mods_ref[row : row + 1]

    for i in range(2 * chunks):
        first = hats[chunk(i)] * (1.0 + mod(1, i)) + mod(0, i)
        first_ref[chunk(i)] = first.astype(BF16)
        mixed_grad_ref[chunk(i)] = (grads[chunk(i)].astype(F32) * mod(5, i)).astype(BF16)
    for step in range(planes):
        attns.relay_across(step)
    ups.relay(0)
    attns.finish()

    keep_attn = pltpu.make_async_copy(attn_all, attn_out, load_sems.at[4])
    keep_attn.start()
    whole = attn_all[...].reshape(width, attn_turned.shape[0])
    for i in range(attn_turned.shape[0] // 128):
        attn_turned[i * 128 : (i + 1) * 128] = whole[:, i * 128 : (i + 1) * 128].T
    span = heads * HD
    for i in range(pair):
        proj_ref[i] = attn_turned[(4 * i + 3) * span : 4 * (i + 1) * span]
        for kind in range(3):
            place_rows = slice((4 * i + kind) * span, (4 * i + kind + 1) * span)
            values = dot32(attn_turned[place_rows], first_ref[...], ((1,), (1,)))
            for h in range(heads):
                qkv_ref[i, kind, h] = values[h * HD : (h + 1) * HD].astype(BF16)
    ups.relay(1)
    downs.relay(0)

    def attend(quarters):
        @pl.loop(0, pair)
        def _(index):
            attend_quarters(ids_ref, qkv_ref, out_ref, log_ref, index, quarters, small_len)

    def project(quarter):
        return sum(
            dot32(out_ref[i, :, chunk(quarter)], proj_ref[i], ((0,), (0,))) for i in range(pair)
        )

    branch_copies = [
        remote(
            branch_send.at[chunk(i)],
            branch_land.at[chunk(i)],
            branch_sends.at[i],
            branch_recvs.at[i],
            beside,
            dp,
        )
        for i in range(chunks)
    ]
    second_copies = [
        remote(
            second_ref.at[chunk(i)],
            second_ref.at[chunk(chunks + i)],
            second_sends.at[i],
            second_recvs.at[i],
            beside,
            dp,
        )
        for i in range(chunks)
    ]
    for i in range(chunks):
        attend([chunks + i])
        branch_send[chunk(i)] = project(chunks + i).astype(BF16)
        branch_copies[i].start()
        if i == 0:
            for step in range(2, planes - 1):
                ups.relay(step)
        else:
            downs.relay(1)
    attend(range(chunks))
    for step in range(2, planes - 1):
        downs.relay(step)
    for i in range(chunks):
        branch = project(i)
        branch_copies[i].wait_recv()
        branch = branch + branch_land[chunk(i)].astype(F32)
        branch_ref[chunk(i)] = branch
        middle = rows[chunk(i)].astype(F32) + mod(2, i) * branch
        hat, _ = norm_parts(middle)
        second_ref[chunk(i)] = (hat * (1.0 + mod(4, i)) + mod(3, i)).astype(BF16)
        second_copies[i].start()
    for step in range(planes):
        ups.relay_across(step)
    for copy in second_copies:
        copy.wait()
    for step in range(planes):
        downs.relay_across(step)
    for copy in branch_copies + part_copies:
        copy.wait_send()
    keep_attn.wait()
    ups.finish()
    downs.finish()


def front(ids, whole_args, vmem_args, planes, heads):
    tokens, _, attn, up, down = whole_args
    marks, _, _, ada, pick = vmem_args
    slots = marks.shape[0]
    count = 2 * planes
    kinds, shard_rows, cols = ada.shape
    small_len = tokens.shape[0] // slots
    own_len, width = tokens.shape[0] // 4, tokens.shape[1]
    length = 2 * own_len
    chunks = own_len // small_len
    vmem = pl.BlockSpec(memory_space=pltpu.VMEM)
    whole = pl.BlockSpec(memory_space=pl.ANY)
    dma = pltpu.SemaphoreType.DMA
    gathered = [
        jax.ShapeDtypeStruct((planes, 2, block.shape[0], 2 * block.shape[1]), BF16)
        for block in (attn, up, down)
    ]
    return pl.pallas_call(
        functools.partial(front_kernel, planes, small_len),
        in_specs=[pl.BlockSpec(memory_space=pltpu.SMEM)]
        + [whole] * len(whole_args)
        + [vmem] * len(vmem_args),
        out_specs=[vmem] * 12 + [whole] * 3,
        out_shape=[
            jax.ShapeDtypeStruct((count * slots, 128), jnp.int32),
            jax.ShapeDtypeStruct((count * slots, shard_rows), F32),
            jax.ShapeDtypeStruct((count * slots, shard_rows), BF16),
            jax.ShapeDtypeStruct((pick.shape[0], width), F32),
            jax.ShapeDtypeStruct((length, width), BF16),
            jax.ShapeDtypeStruct((2, 3, heads, HD, length), BF16),
            jax.ShapeDtypeStruct((2, heads * HD, width), BF16),
            jax.ShapeDtypeStruct((2, heads * HD, length), BF16),
            jax.ShapeDtypeStruct((2 * heads, 1, length), F32),
            jax.ShapeDtypeStruct((own_len, width), F32),
            jax.ShapeDtypeStruct((length, width), BF16),
            jax.ShapeDtypeStruct((length, width), BF16),
            *gathered,
        ],
        scratch_shapes=[
            pltpu.VMEM((length, width), BF16),
            pltpu.VMEM((length, width), BF16),
            pltpu.VMEM((length, width), F32),
            pltpu.VMEM(gathered[0].shape, BF16),
            pltpu.VMEM((gathered[0].shape[3], width), BF16),
            pltpu.VMEM((own_len, width), BF16),
            pltpu.VMEM((own_len, width), BF16),
            pltpu.VMEM((planes, 2, kinds * slots, cols), F32),
            pltpu.VMEM((planes, kinds * slots, cols), F32),
            pltpu.VMEM((planes, kinds * slots, cols), F32),
            pltpu.VMEM((planes - 1, kinds * slots, cols), F32),
            pltpu.VMEM((4, kinds * slots, cols), F32),
            dma((5,)),
            dma((2,)),
            dma((count - 1,)),
            dma((count - 1,)),
            dma((planes - 1,)),
            dma((planes - 1,)),
            dma((3,)),
            dma((3,)),
            *([dma((chunks,))] * 4),
            *(gather_sems(planes) * 3),
        ],
        compiler_params=pltpu.CompilerParams(
            collective_id=1, has_side_effects=True, vmem_limit_bytes=62 << 20
        ),
    )(ids, *whole_args, *vmem_args)


GELU_A = math.sqrt(2.0 / math.pi)
GELU_B = 0.044715


def gelu_pair(values):
    square = values * values
    bend = jnp.tanh(values * (GELU_A + GELU_A * GELU_B * square))
    half = 0.5 + 0.5 * bend
    slope = (0.5 * GELU_A + 1.5 * GELU_A * GELU_B * square) * (1.0 - bend * bend)
    return values * half, half + values * slope


def mlp_kernel(
    planes,
    small_len,
    second_ref,
    mixed_grad_ref,
    up_ref,
    down_ref,
    tokens_ref,
    cotangent_ref,
    branch_ref,
    mods_ref,
    base_out,
    far_mixed_out,
    middle_out,
    branch_grad_out,
    up_grad_out,
    down_grad_out,
    sums_ref,
    tokens,
    cotangent,
    branch,
    active,
    hidden_grad,
    mixed_total,
    second_total,
    mixed_send,
    second_send,
    second_land,
    weight_grads,
    weight_lands,
    sends,
    recvs,
    locals_,
):
    tp, dp = lax.axis_index("tp"), lax.axis_index("dp")
    beside, core = x_neighbour(tp), lax.rem(dp, 2)
    phase, tile = pl.program_id(0), pl.program_id(1)
    tiles, _, rows, block = weight_lands.shape[1:]
    own_len, width = mixed_total.shape
    grad_outs = (up_grad_out, down_grad_out)
    second_copy = remote(second_send, second_land, sends.at[0], recvs.at[0], beside, dp)
    keep_far = pltpu.make_async_copy(mixed_send, far_mixed_out, locals_.at[0])
    keeps = [
        pltpu.make_async_copy(src, dst, locals_.at[1 + i])
        for i, (src, dst) in enumerate(
            ((mixed_total, base_out), (second_total, middle_out), (second_send, branch_grad_out))
        )
    ]
    place = pl.ds(pl.multiple_of(tp * own_len, own_len), own_len)
    loads = [
        pltpu.make_async_copy(src, dst, locals_.at[4 + i])
        for i, (src, dst) in enumerate(
            ((tokens_ref.at[place], tokens), (cotangent_ref.at[place], cotangent), (branch_ref, branch))
        )
    ]

    def weight_copy(which, index):
        sem = 1 + which * tiles + index
        return remote(
            weight_grads.at[which, index, :, 1 - core],
            weight_lands.at[which, index],
            sends.at[sem],
            recvs.at[sem],
            tp,
            other_core(dp),
        )

    def keep_weight(which, index):
        return pltpu.make_async_copy(
            weight_lands.at[which, index],
            grad_outs[which].at[:, :, pl.ds(index * block, block)],
            locals_.at[7 + which * tiles + index],
        )

    @pl.when((phase == 0) & (tile == 0))
    def _():
        for load in loads:
            load.start()
        greet([(beside, dp), (tp, other_core(dp))])

    @pl.when(phase < 2)
    def _():
        rows_here = pl.ds(pl.multiple_of((1 - phase) * own_len, own_len), own_len)
        up, down = up_ref[...], down_ref[...]
        hidden = dot32(second_ref[rows_here], up, ((1,), (0,)))
        grad = dot32(mixed_grad_ref[rows_here], down, ((1,), (0,)))
        value, slope = gelu_pair(hidden)
        value = value.astype(BF16)
        back = (grad * slope).astype(BF16)
        active[tile, rows_here] = value
        hidden_grad[tile, rows_here] = back
        mixed = dot32(value, down, ((1,), (1,)))
        second = dot32(back, up, ((1,), (1,)))

        @pl.when(tile == 0)
        def _():
            mixed_total[...] = mixed
            second_total[...] = second

        @pl.when(tile > 0)
        def _():
            mixed_total[...] += mixed
            second_total[...] += second

    @pl.when((phase == 0) & (tile == tiles - 1))
    def _():
        second_send[...] = second_total[...].astype(BF16)
        second_copy.start()
        mixed_send[...] = mixed_total[...].astype(BF16)
        keep_far.start()

    for index in range(tiles):

        @pl.when((phase == 2) & (tile == index))
        def _():
            grads = (
                dot32(second_ref[...], hidden_grad[index], ((0,), (0,))),
                dot32(mixed_grad_ref[...], active[index], ((0,), (0,))),
            )
            for which in range(2):
                low = grads[which].astype(BF16).reshape(planes, 2, rows, block)
                weight_grads[which, index] = low
                weight_copy(which, index).start()

    @pl.when((phase == 2) & (tile == tiles - 1))
    def _():
        for load in loads:
            load.wait()
        second_copy.wait()
        chunks = own_len // small_len
        sums = {}
        for i in range(chunks):
            here = pl.ds(i * small_len, small_len)
            gate_one, _, scale_two, gate_two = (
                mods_ref[kind * 2 * chunks + i : kind * 2 * chunks + i + 1] for kind in (2, 3, 4, 5)
            )
            attended = branch[here]
            rest = cotangent[here].astype(F32)
            middle = tokens[here].astype(F32) + gate_one * attended
            hat, rstd = norm_parts(middle)
            grad = second_total[here] + second_land[here].astype(F32)
            sums[1, i] = jnp.sum(grad, axis=0, keepdims=True)
            sums[2, i] = jnp.sum(grad * hat, axis=0, keepdims=True)
            grad = rest + norm_back(hat, rstd, grad * (1.0 + scale_two))
            sums[0, i] = jnp.sum(grad * attended, axis=0, keepdims=True)
            second_total[here] = grad
            second_send[here] = (grad * gate_one).astype(BF16)
            mixed = mixed_total[here]
            sums[3, i] = jnp.sum(rest * mixed, axis=0, keepdims=True)
            mixed_total[here] = middle + gate_two * mixed
        for keep in keeps:
            keep.start()
        sums_ref[...] = jnp.concatenate(
            [sums[kind, i] for kind in range(4) for i in range(chunks)], axis=0
        )
        for index in range(tiles):
            for which in range(2):
                weight_copy(which, index).wait()
                mine = weight_grads[which, index, :, core].astype(F32)
                landed = weight_lands[which, index].astype(F32)
                weight_lands[which, index] = (mine + landed).astype(BF16)
                keep_weight(which, index).start()
        for index in range(tiles):
            for which in range(2):
                keep_weight(which, index).wait()
        keep_far.wait()
        for keep in keeps:
            keep.wait()


def mlp(second, mixed_grad, up, down, tokens, cotangent, branch, mods, planes, small_len):
    length, width = second.shape
    hidden = up.shape[1]
    block = 768
    tiles = hidden // block
    shard_rows = width // (2 * planes)
    own_len = length // 2
    single = pl.Buffered(buffer_count=1)
    rows = pl.BlockSpec((length, width), lambda p, t: (0, 0), pipeline_mode=single)
    weight = pl.BlockSpec((width, block), lambda p, t: (0, jnp.where(p < 2, t, tiles - 1)))
    whole = pl.BlockSpec(memory_space=pl.ANY)
    dma = pltpu.SemaphoreType.DMA
    return pl.pallas_call(
        functools.partial(mlp_kernel, planes, small_len),
        grid=(3, tiles),
        in_specs=[rows, rows, weight, weight, whole, whole, whole]
        + [pl.BlockSpec(mods.shape, lambda p, t: (0, 0))],
        out_specs=[whole] * 6 + [pl.BlockSpec((8, width), lambda p, t: (0, 0))],
        out_shape=[
            jax.ShapeDtypeStruct((own_len, width), F32),
            jax.ShapeDtypeStruct((own_len, width), BF16),
            jax.ShapeDtypeStruct((own_len, width), F32),
            jax.ShapeDtypeStruct((own_len, width), BF16),
            jax.ShapeDtypeStruct((planes, shard_rows, hidden), BF16),
            jax.ShapeDtypeStruct((planes, shard_rows, hidden), BF16),
            jax.ShapeDtypeStruct((8, width), F32),
        ],
        scratch_shapes=[
            pltpu.VMEM((own_len, width), BF16),
            pltpu.VMEM((own_len, width), BF16),
            pltpu.VMEM((own_len, width), F32),
            pltpu.VMEM((tiles, length, block), BF16),
            pltpu.VMEM((tiles, length, block), BF16),
            pltpu.VMEM((own_len, width), F32),
            pltpu.VMEM((own_len, width), F32),
            pltpu.VMEM((own_len, width), BF16),
            pltpu.VMEM((own_len, width), BF16),
            pltpu.VMEM((own_len, width), BF16),
            pltpu.VMEM((2, tiles, planes, 2, shard_rows, block), BF16),
            pltpu.VMEM((2, tiles, planes, shard_rows, block), BF16),
            dma((1 + 2 * tiles,)),
            dma((1 + 2 * tiles,)),
            dma((7 + 2 * tiles,)),
        ],
        compiler_params=pltpu.CompilerParams(
            collective_id=4,
            has_side_effects=True,
            vmem_limit_bytes=62 << 20,
            dimension_semantics=("arbitrary", "arbitrary"),
        ),
    )(second, mixed_grad, up, down, tokens, cotangent, branch, mods)


class ScatterRows:
    def __init__(self, grad, refs, planes):
        self.grad, self.planes = grad, planes
        self.mine, self.cross_land, self.along_land, self.local, self.sends, self.recvs = refs
        self.cols = grad.shape[2] // 2
        self.tp, self.dp = lax.axis_index("tp"), lax.axis_index("dp")
        self.place = lax.div(self.dp, 2)

    def plane(self, step):
        return lax.rem(self.place + step, self.planes)

    def own(self):
        return pltpu.make_async_copy(
            self.grad.at[:, :, pl.ds(0, self.cols)], self.mine, self.local.at[0]
        )

    def across(self, step):
        return remote(
            self.grad.at[self.plane(step), :, pl.ds(self.cols, self.cols)],
            self.cross_land.at[step],
            self.sends.at[step],
            self.recvs.at[step],
            y_neighbour(self.tp),
            self.dp,
        )

    def along(self, step):
        sem = self.planes + step
        return remote(
            self.mine.at[self.plane(step)],
            self.along_land.at[step - 1],
            self.sends.at[sem],
            self.recvs.at[sem],
            self.tp,
            lax.rem(self.dp + 2 * step, 2 * self.planes),
        )

    def order(self):
        return [*range(1, self.planes), 0]

    def start(self):
        self.own().start()
        for step in self.order():
            self.across(step).start()

    def send(self, step):
        self.across(step).wait_recv()
        mine = self.mine[self.plane(step)].astype(F32)
        total = mine + self.cross_land[step].astype(F32)
        if step == 0:
            return total
        self.mine[self.plane(step)] = total.astype(BF16)
        self.along(step).start()

    def collect(self, total):
        for step in range(1, self.planes):
            self.along(step).wait_recv()
            total = total + self.along_land[step - 1].astype(F32)
        return total

    def finish(self):
        for step in range(self.planes):
            self.across(step).wait_send()
            if step > 0:
                self.along(step).wait_send()


def scatter_scratch(planes, rows, cols):
    return [
        pltpu.VMEM((planes, rows, cols), BF16),
        pltpu.VMEM((planes, rows, cols), BF16),
        pltpu.VMEM((planes - 1, rows, cols), BF16),
        pltpu.SemaphoreType.DMA((1,)),
        pltpu.SemaphoreType.DMA((2 * planes,)),
        pltpu.SemaphoreType.DMA((2 * planes,)),
    ]


def back_kernel(
    planes,
    small_len,
    ids_ref,
    qkv_ref,
    branch_ref,
    far_ref,
    up_ref,
    down_ref,
    attn_ref,
    first_ref,
    tokens_ref,
    middle_ref,
    base_ref,
    cotangent_ref,
    out_ref,
    log_ref,
    proj_ref,
    scale_ref,
    gate_ref,
    gate_grad_ref,
    rest_ref,
    choose_ref,
    ada_ref,
    cond_ref,
    embed_ref,
    marks_ref,
    token_out,
    block_out,
    up_out,
    down_out,
    attn_out,
    ada_grad_ref,
    embed_grad_ref,
    norm_ref,
    grad_qkv,
    branch_all,
    far_land,
    first_send,
    first_land,
    first_own,
    core_land,
    first_rows,
    row_land,
    mod_all,
    cond_part,
    cond_land,
    norm_send,
    norm_land,
    load_sems,
    store_sems,
    branch_sends,
    branch_recvs,
    far_sends,
    far_recvs,
    first_sends,
    first_recvs,
    core_sends,
    core_recvs,
    row_sends,
    row_recvs,
    mod_sends,
    mod_recvs,
    cond_sends,
    cond_recvs,
    norm_sends,
    norm_recvs,
    *scatter_refs,
):
    tp, dp = lax.axis_index("tp"), lax.axis_index("dp")
    count = 2 * planes
    core = lax.rem(dp, 2)
    kinds, shard_rows, cols = ada_ref.shape
    slots = mod_all.shape[1] // kinds
    own_len, width = first_own.shape
    chunks = own_len // small_len
    pair, rows, length = out_ref.shape
    heads = qkv_ref.shape[2]
    beside = x_neighbour(tp)
    around = [(tp, lax.rem(dp + step, count)) for step in range(1, count)]
    others = [(lax.rem(tp + step, 4), dp) for step in range(1, 4)]
    greet(around + others)

    def chunk(index):
        return pl.ds(index * small_len, small_len)

    def beside_copies(src, dst, first, sends, recvs):
        return [
            remote(src.at[chunk(i)], dst.at[chunk(first + i)], sends.at[i], recvs.at[i], beside, dp)
            for i in range(chunks)
        ]

    branch_copies = beside_copies(branch_ref, branch_all, chunks, branch_sends, branch_recvs)
    far_copies = beside_copies(far_ref, far_land, 0, far_sends, far_recvs)
    first_copies = beside_copies(first_send, first_land, 0, first_sends, first_recvs)
    for copy in branch_copies + far_copies:
        copy.start()
    row_land[0, tp] = rest_ref[tp]
    ups = ScatterRows(up_ref, scatter_refs[:6], planes)
    downs = ScatterRows(down_ref, scatter_refs[6:12], planes)
    attns = ScatterRows(core_land, scatter_refs[12:], planes)
    ups.start()
    downs.start()

    def row_copy(part, step):
        peer = lax.rem(tp + step, 4)
        src = (rest_ref, first_rows)[part].at[peer]
        sem = part * 4 + step
        return remote(src, row_land.at[part, tp], row_sends.at[sem], row_recvs.at[sem], peer, dp)

    for step in range(1, 4):
        row_copy(0, step).start()

    def attention(qkv, go, grad_k, grad_v):
        load = pltpu.make_async_copy(qkv_ref, qkv, load_sems.at[0])
        keep = pltpu.make_async_copy(
            branch_ref, branch_all.at[pl.ds(0, own_len)], load_sems.at[1]
        )
        load.start()
        keep.start()
        keep.wait()

        def heads_grad(quarter):
            for i in range(pair):
                go[i, :, chunk(quarter)] = dot32(
                    proj_ref[i], branch_all[chunk(quarter)], ((1,), (1,))
                )

        def attend(quarters, add):
            @pl.loop(0, pair)
            def _(index):
                back_quarters(
                    ids_ref,
                    qkv,
                    out_ref,
                    log_ref,
                    go,
                    grad_qkv,
                    grad_k,
                    grad_v,
                    index,
                    quarters,
                    small_len,
                    add,
                )

        for i in range(chunks):
            heads_grad(i)
        load.wait()
        attend(range(chunks), False)
        ups.own().wait()
        downs.own().wait()
        for step in ups.order()[:2]:
            ups.send(step)
        for i in range(chunks):
            branch_copies[i].wait()
            heads_grad(chunks + i)
        ups.send(ups.order()[2])
        attend(range(chunks, 2 * chunks), True)
        up_out[...] = ups.send(0)
        downs.send(downs.order()[0])
        for i in range(pair):
            grad_qkv[i, pl.ds(rows, rows)] = (grad_k[i] * HEAD_SCALE).astype(BF16)
            grad_qkv[i, pl.ds(2 * rows, rows)] = grad_v[i].astype(BF16)
            grad_qkv[i, pl.ds(3 * rows, rows)] = jnp.zeros((rows, length), BF16)

    pl.run_scoped(
        attention,
        pltpu.VMEM((pair, 3, heads, HD, length), BF16),
        pltpu.VMEM((pair, rows, length), F32),
        pltpu.VMEM((pair, rows, length), F32),
        pltpu.VMEM((pair, rows, length), F32),
    )

    def weights(attn, first, grads):
        load_attn = pltpu.make_async_copy(attn_ref, attn, load_sems.at[0])
        load_first = pltpu.make_async_copy(first_ref, first, load_sems.at[1])
        load_attn.start()
        load_first.start()
        load_attn.wait()

        def input_grad(quarter):
            return sum(
                dot32(
                    grad_qkv[i, :, chunk(quarter)],
                    attn[:, i * 4 * rows : (i + 1) * 4 * rows],
                    ((0,), (1,)),
                )
                for i in range(pair)
            )

        for i in range(chunks):
            first_send[chunk(i)] = input_grad(chunks + i).astype(BF16)
            first_copies[i].start()
        load_first.wait()
        downs.send(downs.order()[1])
        shape = (planes, 2, shard_rows)
        for i in range(pair):
            split, end = (i * 4 + 3) * rows, (i + 1) * 4 * rows
            grad = dot32(first[...], grad_qkv[i, : 3 * rows], ((0,), (1,))).astype(BF16)
            grads[:, :, :, i * 4 * rows : split] = grad.reshape(*shape, 3 * rows)
            grad = dot32(branch_all[...], out_ref[i], ((0,), (1,))).astype(BF16)
            grads[:, :, :, split:end] = grad.reshape(*shape, rows)

        def core_copy(step):
            place = attns.plane(step)
            return remote(
                grads.at[place, 1 - core],
                core_land.at[place],
                core_sends.at[step],
                core_recvs.at[step],
                tp,
                other_core(dp),
            )

        for step in attns.order():
            core_copy(step).start()
        downs.send(downs.order()[2])
        for i in range(chunks):
            first_own[chunk(i)] = input_grad(i)
        for step in attns.order():
            core_copy(step).wait_recv()
            place = attns.plane(step)
            total = core_land[place].astype(F32) + grads[place, core].astype(F32)
            core_land[place] = total.astype(BF16)
            attns.mine[place] = total[:, :width].astype(BF16)
            attns.across(step).start()
        for step in range(planes):
            core_copy(step).wait_send()

    pl.run_scoped(
        weights,
        pltpu.VMEM((width, 8 * rows), BF16),
        pltpu.VMEM((length, width), BF16),
        pltpu.VMEM((planes, 2, shard_rows, 8 * rows), BF16),
    )
    down_out[...] = downs.send(0)
    up_total = ups.collect(up_out[...])
    up_out[...] = up_total
    squares = jnp.sum(up_total * up_total).reshape(1, 1)

    own_place = pl.ds(pl.multiple_of(tp * own_len, own_len), own_len)

    def ends(tokens, middle, base, cotangent, token, block):
        loads = [
            pltpu.make_async_copy(src, dst, load_sems.at[i])
            for i, (src, dst) in enumerate(
                (
                    (base_ref, base),
                    (cotangent_ref.at[own_place], cotangent),
                    (tokens_ref.at[own_place], tokens),
                    (middle_ref, middle),
                )
            )
        ]
        keeps = [
            pltpu.make_async_copy(token, token_out, store_sems.at[0]),
            pltpu.make_async_copy(block, block_out, store_sems.at[1]),
        ]
        for load in loads:
            load.start()
        for load in loads:
            load.wait()
        sums = {}
        for i in range(chunks):
            far_copies[i].wait_recv()
            far = far_land[chunk(i)].astype(F32)
            block[chunk(i)] = (base[chunk(i)] + gate_ref[i : i + 1] * far).astype(BF16)
            gate_grad = jnp.sum(far * cotangent[chunk(i)].astype(F32), axis=0, keepdims=True)
            sums[2, i] = gate_grad + gate_grad_ref[i : i + 1]
        keeps[1].start()
        attns.send(attns.order()[0])
        for i in range(chunks):
            hat, rstd = norm_parts(tokens[chunk(i)].astype(F32))
            first_copies[i].wait_recv()
            grad = first_own[chunk(i)] + first_land[chunk(i)].astype(F32)
            sums[0, i] = jnp.sum(grad, axis=0, keepdims=True)
            sums[1, i] = jnp.sum(grad * hat, axis=0, keepdims=True)
            back = norm_back(hat, rstd, grad * (1.0 + scale_ref[i : i + 1]))
            token[chunk(i)] = (back + middle[chunk(i)]).astype(BF16)
        keeps[0].start()
        quarter_rows = [sums[kind, i] for kind in range(3) for i in range(chunks)]
        quarter_rows.append(jnp.zeros((8 - 3 * chunks, width), F32))
        quarter_rows = jnp.concatenate(quarter_rows, axis=0)
        for part in range(4):
            first_rows[part] = quarter_rows[:, part * cols : (part + 1) * cols]
        for keep in keeps:
            keep.wait()

    pl.run_scoped(
        ends,
        pltpu.VMEM((own_len, width), BF16),
        pltpu.VMEM((own_len, width), F32),
        pltpu.VMEM((own_len, width), F32),
        pltpu.VMEM((own_len, width), BF16),
        pltpu.VMEM((own_len, width), BF16),
        pltpu.VMEM((own_len, width), BF16),
    )

    row_land[1, tp] = first_rows[tp]
    for step in range(1, 4):
        row_copy(1, step).start()
    for step in attns.order()[1:-1]:
        attns.send(step)
    down_total = downs.collect(down_out[...])
    down_out[...] = down_total
    squares = squares + jnp.sum(down_total * down_total).reshape(1, 1)
    for step in range(1, 4):
        row_copy(0, step).wait_recv()
        row_copy(1, step).wait_recv()
    grad_mod = lax.dot_general(
        choose_ref[...],
        row_land[...].reshape(2 * 4 * 8, cols),
        (((1,), (0,)), ((), ())),
        precision=HIGHEST,
        preferred_element_type=F32,
    ).astype(BF16)
    mod_all[dp] = grad_mod
    mod_copies = [
        remote(mod_all.at[dp], mod_all.at[dp], mod_sends.at[i], mod_recvs.at[i], *peer)
        for i, peer in enumerate(around)
    ]
    for copy in mod_copies:
        copy.start()
    attn_total = attns.send(0)
    for copy in mod_copies:
        copy.wait()
    mods = mod_all[...].astype(F32)
    cond_grad = jnp.zeros(cond_part.shape, F32)
    kind_rows = []
    for kind in range(kinds):
        part = mods[:, kind * slots : (kind + 1) * slots].reshape(count * slots, cols)
        kind_rows.append(part.astype(BF16))
        cond_grad = cond_grad + dot32(kind_rows[kind], ada_ref[kind], ((1,), (1,)))
    cond_part[...] = cond_grad
    cond_copies = [
        remote(cond_part, cond_land.at[i], cond_sends.at[i], cond_recvs.at[i], *peer)
        for i, peer in enumerate(others)
    ]
    for copy in cond_copies:
        copy.start()
    for kind in range(kinds):
        ada_grad = dot32(cond_ref[...], kind_rows[kind], ((0,), (0,)))
        ada_grad_ref[kind] = ada_grad
        squares = squares + jnp.sum(ada_grad * ada_grad).reshape(1, 1)
    for copy in cond_copies:
        copy.wait()
    for i in range(3):
        cond_grad = cond_grad + cond_land[i]
    embed = embed_ref[...]
    gate = 1.0 / (1.0 + jnp.exp(-embed))
    embed_grad = cond_grad * (gate * (1.0 + embed * (1.0 - gate)))
    embed_grad_ref[...] = embed_grad
    labels = marks_ref[:, 0:1].astype(F32)
    across_labels = lax.dot_general(
        jnp.ones(labels.shape, F32),
        labels,
        (((1,), (1,)), ((), ())),
        precision=HIGHEST,
        preferred_element_type=F32,
    )
    same = jnp.where(jnp.abs(across_labels - labels) < 0.5, 1.0, 0.0)
    table_rows = lax.dot_general(
        same,
        embed_grad,
        (((1,), (0,)), ((), ())),
        precision=HIGHEST,
        preferred_element_type=F32,
    )
    squares = squares + jnp.sum(table_rows * embed_grad).reshape(1, 1) * 0.25
    attn_total = attns.collect(attn_total)
    attn_out[...] = attn_total
    squares = squares + jnp.sum(attn_total * attn_total).reshape(1, 1)

    norm_send[0] = jnp.broadcast_to(squares, norm_send.shape[1:])
    norm_copies = [
        remote(norm_send.at[0], norm_land.at[i], norm_sends.at[i], norm_recvs.at[i], *peer)
        for i, peer in enumerate(others)
    ]
    for copy in norm_copies:
        copy.start()
    for copy in norm_copies:
        copy.wait()
    norm = norm_send[0]
    for i in range(3):
        norm = norm + norm_land[i]
    norm_send[1] = norm
    norm_copies = [
        remote(
            norm_send.at[1],
            norm_land.at[3 + i],
            norm_sends.at[3 + i],
            norm_recvs.at[3 + i],
            *peer,
        )
        for i, peer in enumerate(around)
    ]
    for copy in norm_copies:
        copy.start()
    for copy in norm_copies:
        copy.wait()
    for i in range(count - 1):
        norm = norm + norm_land[3 + i]
    norm_ref[...] = jnp.sqrt(norm)

    for copy in far_copies + first_copies:
        copy.wait_send()
    ups.finish()
    downs.finish()
    attns.finish()
    for step in range(1, 4):
        row_copy(0, step).wait_send()
        row_copy(1, step).wait_send()


def back(ids, whole_args, vmem_args, planes, small_len):
    qkv, branch = whole_args[0], whole_args[1]
    out, ada, marks = vmem_args[0], vmem_args[8], vmem_args[11]
    own_len, width = branch.shape
    chunks = own_len // small_len
    pair, rows, length = out.shape
    kinds, shard_rows, cols = ada.shape
    count = 2 * planes
    slots = marks.shape[0] // count
    vmem = pl.BlockSpec(memory_space=pltpu.VMEM)
    whole = pl.BlockSpec(memory_space=pl.ANY)
    dma = pltpu.SemaphoreType.DMA
    shard = jax.ShapeDtypeStruct((shard_rows, width), F32)
    return pl.pallas_call(
        functools.partial(back_kernel, planes, small_len),
        in_specs=[pl.BlockSpec(memory_space=pltpu.SMEM)]
        + [whole] * len(whole_args)
        + [vmem] * len(vmem_args),
        out_specs=[whole, whole, vmem, vmem, vmem, vmem, vmem, vmem],
        out_shape=[
            jax.ShapeDtypeStruct((own_len, width), BF16),
            jax.ShapeDtypeStruct((own_len, width), BF16),
            shard,
            shard,
            shard,
            jax.ShapeDtypeStruct((kinds, shard_rows, cols), F32),
            jax.ShapeDtypeStruct((count * slots, shard_rows), F32),
            jax.ShapeDtypeStruct((8, 128), F32),
        ],
        scratch_shapes=[
            pltpu.VMEM((pair, 4 * rows, length), BF16),
            pltpu.VMEM((2 * own_len, width), BF16),
            pltpu.VMEM((own_len, width), BF16),
            pltpu.VMEM((own_len, width), BF16),
            pltpu.VMEM((own_len, width), BF16),
            pltpu.VMEM((own_len, width), F32),
            pltpu.VMEM((planes, shard_rows, 2 * width), BF16),
            pltpu.VMEM((4, 8, cols), F32),
            pltpu.VMEM((2, 4, 8, cols), F32),
            pltpu.VMEM((count, kinds * slots, cols), BF16),
            pltpu.VMEM((count * slots, shard_rows), F32),
            pltpu.VMEM((3, count * slots, shard_rows), F32),
            pltpu.VMEM((2, 8, 128), F32),
            pltpu.VMEM((3 + count - 1, 8, 128), F32),
            dma((4,)),
            dma((2,)),
            *([dma((chunks,))] * 6),
            *([dma((planes,))] * 2),
            *([dma((8,))] * 2),
            *([dma((count - 1,))] * 2),
            *([dma((3,))] * 2),
            *([dma((count + 2,))] * 2),
            *(scatter_scratch(planes, shard_rows, width) * 3),
        ],
        compiler_params=pltpu.CompilerParams(
            collective_id=5, has_side_effects=True, vmem_limit_bytes=62 << 20
        ),
    )(ids, *whole_args, *vmem_args)


def swap(value, bit):
    return lax.ppermute(value, "tp", [(i, i ^ bit) for i in range(4)])


def assemble_kernel(*refs):
    tp = lax.axis_index("tp")
    beside, across = x_neighbour(tp), y_neighbour(tp)
    far = y_neighbour(beside)
    sems = refs[-1]
    copies = []
    for i in range(2):
        own, near, over = refs[3 * i : 3 * i + 3]
        halves = refs[6:8]
        whole = refs[8 + i]
        half = own.shape[0] // 2
        places = [
            (own, whole.at[tp]),
            (near, whole.at[beside]),
            (over, whole.at[across]),
            (halves[0].at[i], whole.at[far, pl.ds(0, half)]),
            (halves[1].at[i], whole.at[far, pl.ds(half, half)]),
        ]
        for j, (src, dst) in enumerate(places):
            copies.append(pltpu.make_async_copy(src, dst, sems.at[5 * i + j]))
    for copy in copies:
        copy.start()
    for copy in copies:
        copy.wait()


def assemble(parts):
    whole = pl.BlockSpec(memory_space=pl.ANY)
    vmem = pl.BlockSpec(memory_space=pltpu.VMEM)
    rows = jax.ShapeDtypeStruct((4, *parts[0].shape), BF16)
    return pl.pallas_call(
        assemble_kernel,
        in_specs=[vmem] * len(parts),
        out_specs=[whole] * 2,
        out_shape=[rows] * 2,
        scratch_shapes=[pltpu.SemaphoreType.DMA((10,))],
        cost_estimate=pl.CostEstimate(flops=0, bytes_accessed=20 << 20, transcendentals=0),
    )(*parts)


def spread(own):
    beside = [swap(array, 1) for array in own]
    across = [swap(array, 2) for array in own]
    half = own[0].shape[0] // 2
    far = (
        swap(jnp.stack([array[:half] for array in across]), 1),
        swap(jnp.stack([array[half:] for array in beside]), 2),
    )
    return (own[0], beside[0], across[0], own[1], beside[1], across[1], *far)


def update_kernel(
    rates, norm_ref, attn_ref, up_ref, down_ref, ada_ref, embed_ref, marks_ref, *refs
):
    sources, outs, states = refs[:24], refs[24:48], refs[48:72]
    load_sems, store_sems = refs[72:74]
    loads = [
        pltpu.make_async_copy(src, dst, load_sems.at[i])
        for i, (src, dst) in enumerate(zip(sources, states))
    ]
    stores = [
        pltpu.make_async_copy(src, dst, store_sems.at[i])
        for i, (src, dst) in enumerate(zip(states, outs))
    ]
    for load in loads:
        load.start()
    factor = jnp.minimum(1.0, clip_limit / (norm_ref[0:1, 0:1] + 1e-06))

    def update(which, grad, at):
        values = [ref[at] for ref in states[4 * which : 4 * which + 4]]
        fresh = adam_step(*values, grad * factor, rates[which])
        for ref, value in zip(states[4 * which : 4 * which + 4], fresh):
            ref[at] = value

    def ready(which):
        for load in loads[4 * which : 4 * which + 4]:
            load.wait()

    def leave(which):
        for store in stores[4 * which : 4 * which + 4]:
            store.start()

    cols = attn_ref.shape[1] // 4
    ready(0)
    for kind in range(3):
        update(0, attn_ref[:, kind * cols : (kind + 1) * cols], kind)
    leave(0)
    for which, grad in ((1, attn_ref[:, 3 * cols :]), (2, up_ref[...]), (3, down_ref[...])):
        ready(which)
        update(which, grad, ...)
        leave(which)
    ready(4)
    for kind in range(ada_ref.shape[0]):
        update(4, ada_ref[kind], kind)
    leave(4)
    classes = states[20].shape[1]
    slots = marks_ref.shape[0]
    places = lax.broadcasted_iota(jnp.int32, (slots, classes + -classes % 128), 1)
    onehot = jnp.where(places == marks_ref[:, 0:1], 1.0, 0.0)
    table = lax.dot_general(
        embed_ref[...],
        onehot,
        (((0,), (0,)), ((), ())),
        precision=HIGHEST,
        preferred_element_type=F32,
    )
    ready(5)
    update(5, table[:, :classes], ...)
    leave(5)
    for store in stores:
        store.wait()


def update(grads, states, rates):
    vmem = pl.BlockSpec(memory_space=pltpu.VMEM)
    whole = pl.BlockSpec(memory_space=pl.ANY)
    dma = pltpu.SemaphoreType.DMA
    return pl.pallas_call(
        functools.partial(update_kernel, rates),
        in_specs=[vmem] * len(grads) + [whole] * len(states),
        out_specs=[whole] * len(states),
        out_shape=[jax.ShapeDtypeStruct(state.shape, F32) for state in states],
        scratch_shapes=[
            *[pltpu.VMEM(state.shape, F32) for state in states],
            dma((len(states),)),
            dma((len(states),)),
        ],
        compiler_params=pltpu.CompilerParams(vmem_limit_bytes=48 << 20),
        cost_estimate=pl.CostEstimate(
            flops=40 << 20, bytes_accessed=40 << 20, transcendentals=1 << 20
        ),
    )(*grads, *states)


def adam_step(weight, moment, second, average, gradient, rate):
    moment = 0.5 * moment + 0.5 * gradient
    second = 0.5 * second + 0.5 * gradient * gradient
    correct = 1.0 - 0.5**STEP
    weight = weight - rate * (
        moment / correct / (jnp.sqrt(second / correct) + 1e-08) + 0.1 * weight
    )
    keep_rate = min(0.9999, (1.0 + STEP) / (10.0 + STEP))
    average = keep_rate * average + (1.0 - keep_rate) * weight
    return (moment, second, weight, average)


def per_device(
    tokens,
    cotangent,
    quarter_ids,
    labels,
    timesteps,
    qkv_weight,
    qkv_moment,
    qkv_second,
    qkv_average,
    proj_weight,
    proj_moment,
    proj_second,
    proj_average,
    up_weight,
    up_moment,
    up_second,
    up_average,
    down_weight,
    down_moment,
    down_second,
    down_average,
    ada_weight,
    ada_moment,
    ada_second,
    ada_average,
    table_weight,
    table_moment,
    table_second,
    table_average,
):
    row_count, width = tokens.shape
    slot_count = quarter_ids.shape[0]
    small_len = row_count // slot_count
    span_len = row_count // 2
    own_len = row_count // 4
    shard_rows, _, quarter_width = qkv_weight.shape
    heads = quarter_width // HD
    tp_place = lax.axis_index("tp")
    dp_place = lax.axis_index("dp")
    span = tp_place // 2
    side = tp_place % 2

    attn_block = jnp.concatenate(
        [qkv_weight[:, 0], qkv_weight[:, 1], qkv_weight[:, 2], proj_weight.T], axis=1
    ).astype(BF16)
    planes = lax.axis_size("dp") // 2
    marks = jnp.concatenate(
        [
            jnp.broadcast_to(labels[:, None], (slot_count, 64)),
            jnp.broadcast_to(timesteps[:, None], (slot_count, 64)),
        ],
        axis=1,
    )
    column = dp_place * shard_rows + jnp.arange(shard_rows, dtype=jnp.int32)
    half_width = width // 2
    freqs = jnp.stack(
        [
            jnp.exp(-math.log(10000.0) * (column % half_width).astype(F32) / half_width),
            (column < half_width).astype(F32),
        ]
    )
    w_ada = ada_weight.transpose(1, 0, 2).astype(BF16)
    classes = table_weight.shape[0]
    table_low = jnp.pad(table_weight.T.astype(BF16), ((0, 0), (0, -classes % 128)))
    slot_base = dp_place * slot_count
    choose = (
        quarter_ids[:, None] - slot_base == jnp.arange(slot_count, dtype=jnp.int32)[None, :]
    ).astype(F32)
    quarters = slot_count // 4

    def own_first(array, size):
        mine = lax.dynamic_slice_in_dim(array, (span * 2 + side) * size, size, 0)
        other = lax.dynamic_slice_in_dim(array, (span * 2 + 1 - side) * size, size, 0)
        return jnp.concatenate([mine, other], axis=0)

    ids = own_first(quarter_ids, quarters)
    pick = jnp.eye(6, dtype=F32)[:, None, :, None] * own_first(choose, quarters)[None, :, None, :]
    (
        marks,
        embed,
        cond_low,
        mods,
        first_in,
        qkv,
        w_proj,
        attended,
        log_total,
        branch,
        second_in,
        grad_mixed,
        w_attn,
        w_up,
        w_down,
    ) = front(
        ids,
        (
            tokens,
            cotangent,
            attn_block,
            up_weight.astype(BF16),
            down_weight.T.astype(BF16),
        ),
        (marks, freqs, table_low, w_ada, pick.reshape(12 * quarters, 6 * slot_count)),
        planes,
        heads,
    )
    w_attn = w_attn.reshape(width, 8 * quarter_width)
    w_up = w_up.reshape(width, 8 * quarter_width)
    w_down = w_down.reshape(width, 8 * quarter_width)

    base, far_mixed, grad_middle, own_branch, grad_up, grad_down, sums = mlp(
        second_in, grad_mixed, w_up, w_down, tokens, cotangent, branch, mods, planes, small_len
    )

    rest = sums.reshape(8, 4, quarter_width).transpose(1, 0, 2)
    chosen = choose.reshape(4, quarters, slot_count).transpose(2, 0, 1)
    kinds = jnp.arange(6, dtype=jnp.int32)[:, None]
    known = (kinds - 2 == jnp.arange(4, dtype=jnp.int32)[None, :]) & (kinds < 5)
    later = jnp.where(kinds == 5, 2, kinds) == jnp.arange(4, dtype=jnp.int32)[None, :]
    later = later & ((kinds < 2) | (kinds == 5))
    pick = jnp.stack([known, later], axis=1).astype(F32)
    pick = (pick[:, None, :, None, :, None] * chosen[None, :, None, :, None, :]).reshape(
        6 * slot_count, 32 * quarters
    )
    token_grad, block_out, up_reduced, down_reduced, attn_reduced, grad_ada, grad_embed, norm = back(
        ids,
        (
            qkv,
            own_branch,
            far_mixed,
            grad_up,
            grad_down,
            w_attn,
            first_in,
            tokens,
            grad_middle,
            base,
            cotangent,
        ),
        (
            attended,
            log_total,
            w_proj,
            mods[2 * quarters : 3 * quarters],
            mods[10 * quarters : 11 * quarters],
            sums[3 * quarters :],
            rest,
            pick,
            w_ada,
            cond_low,
            embed,
            marks,
        ),
        planes,
        small_len,
    )

    cube = lambda states: [state.transpose(1, 0, 2) for state in states]
    turned = lambda states: [state.T for state in states]
    states = (
        *cube((qkv_weight, qkv_moment, qkv_second, qkv_average)),
        *turned((proj_weight, proj_moment, proj_second, proj_average)),
        *(up_weight, up_moment, up_second, up_average),
        *turned((down_weight, down_moment, down_second, down_average)),
        *cube((ada_weight, ada_moment, ada_second, ada_average)),
        *turned((table_weight, table_moment, table_second, table_average)),
    )
    wide = 0.5 * D ** (-0.5)
    rates = (wide, 4.0 * D ** (-0.5), wide, 0.5 * FF ** (-0.5), wide, 0.5)
    parts = spread((token_grad, block_out))
    fresh = update(
        (norm, attn_reduced, up_reduced, down_reduced, grad_ada, grad_embed, marks), states, rates
    )
    token_grad, block_out = assemble(parts)
    return (
        block_out.reshape(row_count, width),
        token_grad.reshape(row_count, width),
        norm[0, 0],
        *cube(fresh[:4]),
        *turned(fresh[4:8]),
        *fresh[8:12],
        *turned(fresh[12:16]),
        *cube(fresh[16:20]),
        *turned(fresh[20:24]),
    )


def solution(mesh):
    rows = P("dp", None)
    marks = P("dp")
    cubes = (P("dp", None, "tp"),) * 4
    across = (P("tp", "dp"),) * 4
    along = (P("dp", "tp"),) * 4
    table = (P(None, "dp"),) * 4
    states = (*cubes, *across, *along, *across, *cubes, *table)
    return jax.shard_map(
        per_device,
        mesh=mesh,
        in_specs=(rows, rows, marks, marks, marks, *states),
        out_specs=(rows, rows, P(), *states),
        check_vma=False,
    )
```

time: 524 us -> 440 us (0.84)
  waiting for transfers between devices: 5.78 us -> 58.2 us
  other arithmetic: 58.4 us -> 6.84 us
  Pallas kernels: 389 us -> 345 us
  local copies, waits for them, and re-layouts: 40 us -> 12.7 us
  matrix products: 16.9 us -> 0 us
    pallas_call x5 -> x4, Pallas kernels: 300 us -> 216 us  [the longest x1 127 us: front(): pl.pallas_call(functools.partial(front_kernel, planes, small_len), in_spe...]
    ppermute x4 -> x6, waiting for transfers between devices: 5.78 us -> 58.2 us  [swap(): return lax.ppermute(value, 'tp', [(i, i ^ bit) for i in range(4)])]
    pallas_call x1, Pallas kernels: 88.4 us -> 129 us  [back(): pl.pallas_call(functools.partial(back_kernel, planes, small_len), in_spec...]
    unnamed x141 -> x50, local copies, waits for them, and re-layouts: 23.4 us -> 3.5 us
    convert_element_type x7 -> x2, other arithmetic: 17.4 us -> 0.01 us  [the longest x1 0.01 us: per_device(): pick = jnp.stack([known, later], axis=1).astype(F32)]
    dot_general x4 -> x0, matrix products: 16.9 us -> none  [the longest x1 7.96 us: per_device(): jnp.einsum('nd,dc->cn', first_in, w_attn, preferred_element_type=F32)]
    reduce_sum x8 -> x0, other arithmetic: 15.4 us -> none  [the longest x1 4.51 us: per_device(): grad_gate_one = jnp.sum(grad_middle * branch, axis=1)]
    add x5 -> x0, other arithmetic: 12.9 us -> none  [adam_step(): average = keep_rate * average + (1.0 - keep_rate) * weight]
  transfers between devices with their start and end apart: 4 -> 6, of which waited for: 2 -> 4; matrix products, arithmetic and copies ran while one was open for 8% -> 0% of each run, Pallas kernels for 22% -> 4%
where the time goes in v4:
time: 440 us; the launch traced here: 431 us
  Pallas kernels  345 us (78%)
  waiting for transfers between devices  58.2 us (13%)
  local copies, waits for them, and re-layouts  12.7 us (3%)
  other arithmetic  6.84 us (2%)
  starting transfers between devices  6.23 us (1%)
    pallas_call x1, Pallas kernels, back(): pl.pallas_call(functools.partial(back_kernel, planes, small_len), in_spec...  129 us
    pallas_call x1, Pallas kernels, front(): pl.pallas_call(functools.partial(front_kernel, planes, small_len), in_spe...  127 us
    pallas_call x1, Pallas kernels, mlp(): pl.pallas_call(functools.partial(mlp_kernel, planes, small_len), grid=(3,...  65.4 us
    ppermute x6, waiting for transfers between devices, swap(): return lax.ppermute(value, 'tp', [(i, i ^ bit) for i in range(4)])  58.2 us
    pallas_call x1, Pallas kernels, update(): pl.pallas_call(functools.partial(update_kernel, rates), in_specs=[vmem] *...  16 us
  transfers between devices with their start and end apart: 6, of which 4 were waited for; matrix products, arithmetic and copies ran while one was open for 0% of the time, Pallas kernels for 4%

profile of v4, /device:TPU:0, one launch (start us, length us, event | category | flops | bytes accessed | tf_op | source)
XLA Modules:
  0.0 430.9 jit_solution(16678444757631588254)
XLA Ops:
  0.8 0.8 broadcast_subtract_fusion
  1.6 0.8 fusion.8
  3.2 1.1 convert.14
  4.4 0.9 bitcast_convert_fusion.ada_ref
  5.9 0.8 bitcast_convert_fusion.2.down_ref
  6.7 0.8 convert_element_type.56.up_ref
  10.2 0.9 concatenate.18.attn_ref
  11.1 127.3 %shard_map.484 = (s32[64,128]{1,0:T(8,128)}, f32[64,144]{1,0:T(8,128)}, bf16[64,144]{1,0:T(8,128)(2,1)}, f32[24,1152]{1,0:T(8,128)}, bf16[1024,1152]{1,0:T(8,128...) custom-call(s32[4]{0:T(128)} %pad_add_fusion.1.ids_ref, ...), custom_call_target="tpu_custom_call" | custom-call | tf_op jit(solution)/shard_map/pallas_call | solution.py:578
  138.4 65.4 %shard_map.485 = (f32[512,1152]{1,0:T(8,128)}, bf16[512,1152]{1,0:T(8,128)(2,1)}, f32[512,1152]{1,0:T(8,128)}, bf16[512,1152]{1,0:T(8,128)(2,1)}, bf16[4,144,230...) custom-call(bf16[1024,1152]{1,0:T(8,128)(2,1)} %get-tuple-element.84.second_ref, ...), custom_call_target="tpu_custom_call" | custom-call | tf_op jit(solution)/shard_map/pallas_call | solution.py:823
  203.8 0.9 reshape.289
  204.6 1.4 slice.41.gate_grad_ref
  206.0 1.4 fusion.7
  209.1 129.4 %shard_map.486 = (bf16[512,1152]{1,0:T(8,128)(2,1)}, bf16[512,1152]{1,0:T(8,128)(2,1)}, f32[144,1152]{1,0:T(8,128)}, f32[144,1152]{1,0:T(8,128)}, f32[144,1152]{...) custom-call(s32[4]{0:T(128)} %pad_add_fusion.1.ids_ref, ...), custom_call_target="tpu_custom_call" | custom-call | tf_op jit(solution)/shard_map/pallas_call | solution.py:1370
  339.2 1.4 collective-permute-start
  341.2 1.4 collective-permute-start.1
  342.6 25.0 %collective-permute-done.2.refs_4_ = bf16[512,1152]{1,0:T(8,128)(2,1)S(1)} collective-permute-done((bf16[512,1152]{1,0:T(8,128)(2,1)}, bf16[512,1152]{1,0:T(8,128)(2,1)S(1)}, u32[]{:S(2)}, u32[]{:S(2)}) %collective-permute-start.2) | collective-permute-done | bytes 1179680 | tf_op jit(solution)/shard_map/ppermute | solution.py:1418
  367.6 24.4 %collective-permute-done.refs_1_ = bf16[512,1152]{1,0:T(8,128)(2,1)S(1)} collective-permute-done((bf16[512,1152]{1,0:T(8,128)(2,1)}, bf16[512,1152]{1,0:T(8,128)(2,1)S(1)}, u32[]{:S(2)}, u32[]{:S(2)}) %collective-permute-start) | collective-permute-done | bytes 1179680 | tf_op jit(solution)/shard_map/ppermute | solution.py:1418
  392.3 0.8 copy-done.19
  395.1 1.5 collective-permute-start.4
  397.2 16.0 %shard_map.488 = (f32[3,144,288]{2,1,0:T(8,128)}, f32[3,144,288]{2,1,0:T(8,128)}, f32[3,144,288]{2,1,0:T(8,128)}, f32[3,144,288]{2,1,0:T(8,128)}, f32[144,288]{1...) custom-call(f32[8,128]{1,0:T(8,128)S(1)} %copy-done.14, ...), custom_call_target="tpu_custom_call" | custom-call | flops 41943040 | bytes 41943040 | tf_op jit(solution)/shard_map/pallas_call | solution.py:1538
  413.2 7.2 %collective-permute-done.5.refs_7_ = bf16[2,256,1152]{2,1,0:T(8,128)(2,1)} collective-permute-done((bf16[2,256,1152]{2,1,0:T(8,128)(2,1)S(1)}, bf16[2,256,1152]{2,1,0:T(8,128)(2,1)}, u32[]{:S(2)}, u32[]{:S(2)}) %collective-permute-start.5) | collective-permute-done | bytes 1179680 | tf_op jit(solution)/shard_map/ppermute | solution.py:1418
  420.3 1.6 collective-permute-done.4.refs_6_
  422.0 1.0 copy-done.22
  423.0 7.4 %shard_map.487 = (bf16[4,512,1152]{2,1,0:T(8,128)(2,1)}, bf16[4,512,1152]{2,1,0:T(8,128)(2,1)}) custom-call(bf16[512,1152]{1,0:T(8,128)(2,1)} %get-tuple-element.105.refs_0_, bf16[512,1152]{1,0:T(8,128)(2,1)} %copy-done.19, bf16[512,1152]{1,0:T(8,128)(2,1)} %copy-done.21, bf16[512,1152]{1,0:T(8,128)(2,1)} %get-tuple-element.106.refs_3_, ...), custom_call_target="tpu_custom_call" | custom-call | bytes 20971520 | tf_op jit(solution)/shard_map/pallas_call | solution.py:1451
  (89 shorter events, 9.9 us)
Async XLA Ops:
  0.7 3.7 copy-start.2
  0.7 3.7 copy-start.15
  5.9 3.4 copy-start.23
  5.9 3.5 copy-start.24
  338.5 29.1 %collective-permute-start.2 = (bf16[512,1152]{1,0:T(8,128)(2,1)}, bf16[512,1152]{1,0:T(8,128)(2,1)S(1)}, u32[]{:S(2)}, u32[]{:S(2)}) collective-permute-start(bf16[512,1152]{1,0:T(8,128)(2,1)} %get-tuple-element.106.refs_3_), channel_id=1, source_target_pairs={{0,8},{8,0},{16,24},{24,16},{1,9},{9,1},{17,25},{25,17},{2,10},{10... | collective-permute-start | bytes 3538952 | tf_op jit(solution)/shard_map/ppermute | solution.py:1418
  339.2 52.9 %collective-permute-start = (bf16[512,1152]{1,0:T(8,128)(2,1)}, bf16[512,1152]{1,0:T(8,128)(2,1)S(1)}, u32[]{:S(2)}, u32[]{:S(2)}) collective-permute-start(bf16[512,1152]{1,0:T(8,128)(2,1)} %get-tuple-element.105.refs_0_), channel_id=1, source_target_pairs={{0,8},{8,0},{16,24},{24,16},{1,9},{9,1},{17,25},{25,17},{2,10},{10... | collective-permute-start | bytes 3538952 | tf_op jit(solution)/shard_map/ppermute | solution.py:1418
  340.6 53.1 %collective-permute-start.3 = (bf16[512,1152]{1,0:T(8,128)(2,1)}, bf16[512,1152]{1,0:T(8,128)(2,1)S(1)}, u32[]{:S(2)}, u32[]{:S(2)}) collective-permute-start(bf16[512,1152]{1,0:T(8,128)(2,1)} %get-tuple-element.106.refs_3_), channel_id=1, source_target_pairs={{0,16},{8,24},{16,0},{24,8},{1,17},{9,25},{17,1},{25,9},{2,18},{10... | collective-permute-start | bytes 3538952 | tf_op jit(solution)/shard_map/ppermute | solution.py:1418
  341.2 52.6 %collective-permute-start.1 = (bf16[512,1152]{1,0:T(8,128)(2,1)}, bf16[512,1152]{1,0:T(8,128)(2,1)S(1)}, u32[]{:S(2)}, u32[]{:S(2)}) collective-permute-start(bf16[512,1152]{1,0:T(8,128)(2,1)} %get-tuple-element.105.refs_0_), channel_id=1, source_target_pairs={{0,16},{8,24},{16,0},{24,8},{1,17},{9,25},{17,1},{25,9},{2,18},{10... | collective-permute-start | bytes 3538952 | tf_op jit(solution)/shard_map/ppermute | solution.py:1418
  367.6 24.7 %copy-start.18 = (bf16[512,1152]{1,0:T(8,128)(2,1)}, bf16[512,1152]{1,0:T(8,128)(2,1)S(1)}, u32[]{:S(2)}) copy-start(bf16[512,1152]{1,0:T(8,128)(2,1)S(1)} %collective-permute-done.2.refs_4_) | copy-start | bytes 3538948
  392.1 5.0 %copy-start.10 = (f32[288,144]{0,1:T(8,128)S(1)}, f32[288,144]{0,1:T(8,128)}, u32[]{:S(2)}) copy-start(f32[288,144]{0,1:T(8,128)} %param.40) | copy-start | bytes 497668
  392.1 5.0 %copy-start.11 = (f32[288,144]{0,1:T(8,128)S(1)}, f32[288,144]{0,1:T(8,128)}, u32[]{:S(2)}) copy-start(f32[288,144]{0,1:T(8,128)} %param.41) | copy-start | bytes 497668
  393.1 27.3 %collective-permute-start.5 = (bf16[2,256,1152]{2,1,0:T(8,128)(2,1)S(1)}, bf16[2,256,1152]{2,1,0:T(8,128)(2,1)}, u32[]{:S(2)}, u32[]{:S(2)}) collective-permute-start(bf16[2,256,1152]{2,1,0:T(8,128)(2,1)S(1)} %pad_maximum_fusion.1), channel_id=1, source_target_pairs={{0,16},{8,24},{16,0},{24,8},{1,17},{9,25},{17,1},{25,9},{2,18},{10... | collective-permute-start | bytes 3538952 | tf_op jit(solution)/shard_map/ppermute | solution.py:1418
  393.7 3.4 copy-start.7
  393.7 3.4 copy-start.8
  393.8 2.8 copy-start.14
  393.8 3.3 copy-start.5
  393.8 3.3 copy-start.6
  393.9 3.3 copy-start
  393.9 3.3 copy-start.3
  393.9 3.3 copy-start.4
  393.9 3.3 copy-start.9
  393.9 3.3 copy-start.12
  393.9 3.3 copy-start.13
  395.1 26.9 %collective-permute-start.4 = (bf16[2,256,1152]{2,1,0:T(8,128)(2,1)S(1)}, bf16[2,256,1152]{2,1,0:T(8,128)(2,1)S(1)}, u32[]{:S(2)}, u32[]{:S(2)}) collective-permute-start(bf16[2,256,1152]{2,1,0:T(8,128)(2,1)S(1)} %pad_maximum_fusion), channel_id=1, source_target_pairs={{0,8},{8,0},{16,24},{24,16},{1,9},{9,1},{17,25},{25,17},{2,10},{10... | collective-permute-start | bytes 3538952 | tf_op jit(solution)/shard_map/ppermute | solution.py:1418
  (7 other events, 8.2 us)

commit v5 on v4

--- a/solution.py
+++ b/solution.py
@@ -63,7 +63,7 @@
     return jnp.concatenate(probs, axis=0), total, top
 
 
-def attend_quarters(ids_ref, qkv_ref, out_ref, log_ref, pair, quarters, small_len):
+def attend_quarters(ids, qkv_ref, out_ref, log_ref, pair, quarters, small_len):
     heads = qkv_ref.shape[2]
     count = qkv_ref.shape[-1] // small_len
     units = [(qb, h) for qb in quarters for h in range(heads)]
@@ -85,12 +85,12 @@
                 outs = []
         if 1 <= i <= len(units):
             qb, h = units[i - 1]
-            same = [ids_ref[kb] == ids_ref[qb] for kb in range(count)]
+            same = [ids[kb] == ids[qb] for kb in range(count)]
             probs[i - 1] = attend_softmax(scores.pop(i - 1), same, small_len)
 
 
 def back_quarters(
-    ids_ref, qkv_ref, out_ref, log_ref, go_ref, gq_ref, gk_ref, gv_ref, pair, quarters, small_len, add
+    ids, qkv_ref, out_ref, log_ref, go_ref, gq_ref, gk_ref, gv_ref, pair, quarters, small_len, add
 ):
     heads = qkv_ref.shape[2]
     count = qkv_ref.shape[-1] // small_len
@@ -136,7 +136,7 @@
             for kb in range(count):
                 part = slice(kb * small_len, (kb + 1) * small_len)
                 base = log_ref[pair * heads + h, :, cols] + jnp.where(
-                    ids_ref[kb] == ids_ref[qb], 0.0, 1e9
+                    ids[kb] == ids[qb], 0.0, 1e9
                 )
                 probs = jnp.exp2(scores[part] * LOG2_SCALE - base)
                 probs_low.append(probs.astype(BF16))
@@ -161,10 +161,12 @@
     )
 
 
-def greet(peers):
+def greet(peers, meanwhile=None):
     barrier = pltpu.get_barrier_semaphore()
     for tp, dp in peers:
         pl.semaphore_signal(barrier, inc=1, device_id=(tp, dp), device_id_type=MESH)
+    if meanwhile is not None:
+        meanwhile()
     pl.semaphore_wait(barrier, len(peers))
 
 
@@ -178,6 +180,14 @@
 
 def y_neighbour(tp):
     return lax.rem(tp + 2, 4)
+
+
+def iota(shape, axis):
+    return lax.broadcasted_iota(jnp.int32, shape, axis)
+
+
+def own_first_ids(ids_ref, tp, chunks):
+    return [ids_ref[owner * chunks + i] for owner in (tp, x_neighbour(tp)) for i in range(chunks)]
 
 
 class GatherRows:
@@ -295,20 +305,32 @@
     planes,
     small_len,
     ids_ref,
+    labels_ref,
+    stamps_ref,
     tokens_ref,
     cotangent_ref,
-    attn_ref,
-    up_ref,
-    down_ref,
-    marks_ref,
-    freqs_ref,
-    table_ref,
-    ada_ref,
-    pick_ref,
+    qkv_weight_ref,
+    proj_weight_ref,
+    up_weight_ref,
+    down_weight_ref,
+    ada_weight_ref,
+    table_weight_ref,
     marks_all_ref,
     embed_ref,
     cond_ref,
     mods_ref,
+    ada_ref,
+    first_hbm,
+    qkv_hbm,
+    proj_hbm,
+    out_hbm,
+    log_hbm,
+    branch_hbm,
+    second_hbm,
+    mixed_grad_hbm,
+    attn_out,
+    up_out,
+    down_out,
     first_ref,
     qkv_ref,
     proj_ref,
@@ -317,9 +339,12 @@
     branch_ref,
     second_ref,
     mixed_grad_ref,
-    attn_out,
-    up_out,
-    down_out,
+    keep_sems,
+    marks_ref,
+    attn_ref,
+    up_ref,
+    down_ref,
+    table_ref,
     rows,
     grads,
     hats,
@@ -350,11 +375,12 @@
     core, place = lax.rem(dp, 2), lax.div(dp, 2)
     count = 2 * planes
     slots = marks_ref.shape[0]
-    kinds, _, cols = ada_ref.shape
+    kinds, shard_rows, cols = ada_ref.shape
     own_len, width = branch_ref.shape
     chunks = own_len // small_len
     pair, _, heads, _, length = qkv_ref.shape
     beside = x_neighbour(tp)
+    ids = own_first_ids(ids_ref, tp, chunks)
     around = [(tp, lax.rem(dp + step, count)) for step in range(1, count)]
     others = [(lax.rem(tp + step, 4), dp) for step in range(1, 4)]
 
@@ -374,7 +400,32 @@
             )
     for load in loads:
         load.start()
-    greet(around + others)
+
+    keeps = []
+
+    def keep(src, dst):
+        copy = pltpu.make_async_copy(src, dst, keep_sems.at[len(keeps)])
+        copy.start()
+        keeps.append(copy)
+
+    def prepare():
+        slot_rows = iota(marks_ref.shape, 0)
+        lanes = iota(marks_ref.shape, 1)
+        marks = jnp.zeros(marks_ref.shape, jnp.int32)
+        for slot in range(slots):
+            mark = jnp.where(lanes < 64, labels_ref[slot], stamps_ref[slot])
+            marks = jnp.where(slot_rows == slot, mark, marks)
+        marks_ref[...] = marks
+        for kind in range(3):
+            attn_ref[:, kind * cols : (kind + 1) * cols] = qkv_weight_ref[kind].astype(BF16)
+        attn_ref[:, 3 * cols :] = proj_weight_ref[...].astype(BF16)
+        up_ref[...] = up_weight_ref[...].astype(BF16)
+        down_ref[...] = down_weight_ref[...].astype(BF16)
+        ada_ref[...] = ada_weight_ref[...].astype(BF16)
+        table_ref[...] = jnp.zeros(table_ref.shape, BF16)
+        table_ref[:, : table_weight_ref.shape[1]] = table_weight_ref[...].astype(BF16)
+
+    greet(around + others, prepare)
     attns = GatherRows(attn_ref, attn_all, gather_refs[:3], planes)
     ups = GatherRows(up_ref, up_out, gather_refs[3:6], planes)
     downs = GatherRows(down_ref, down_out, gather_refs[6:], planes)
@@ -398,9 +449,12 @@
 
     labels = marks_all_ref[:, 0:1]
     stamps = marks_all_ref[:, 64:65].astype(F32) / 1000.0
-    angles = stamps * freqs_ref[0:1]
-    stamp_embed = jnp.where(freqs_ref[1:2] > 0.0, jnp.cos(angles), jnp.sin(angles))
-    classes = lax.broadcasted_iota(jnp.int32, (count * slots, table_ref.shape[1]), 1)
+    column = dp * shard_rows + iota((1, shard_rows), 1)
+    half_width = width // 2
+    turn = jnp.where(column < half_width, column, column - half_width).astype(F32)
+    angles = stamps * jnp.exp(-math.log(10000.0) * turn / half_width)
+    stamp_embed = jnp.where(column < half_width, jnp.cos(angles), jnp.sin(angles))
+    classes = iota((count * slots, table_ref.shape[1]), 1)
     onehot = jnp.where(classes == labels, 1.0, 0.0).astype(BF16)
     embed = dot32(onehot, table_ref[...], ((1,), (1,))) + stamp_embed
     embed_ref[...] = embed
@@ -454,9 +508,17 @@
     downs.start_own()
     for copy in mod_copies:
         copy.wait()
+    pick_shape = (mods_ref.shape[0], kinds * slots)
+    pick_row, pick_col = iota(pick_shape, 0), iota(pick_shape, 1)
+    pick = jnp.zeros(pick_shape, F32)
+    for kind in range(kinds):
+        for quarter in range(2 * chunks):
+            slot = ids[quarter] - dp * slots + kind * slots
+            hit = (pick_row == kind * 2 * chunks + quarter) & (pick_col == slot)
+            pick = jnp.where(hit, 1.0, pick)
     for owner in range(4):
         mods_ref[:, owner * cols : (owner + 1) * cols] = lax.dot_general(
-            pick_ref[...],
+            pick,
             mods_all[owner],
             (((1,), (0,)), ((), ())),
             precision=HIGHEST,
@@ -470,14 +532,14 @@
     for i in range(2 * chunks):
         first = hats[chunk(i)] * (1.0 + mod(1, i)) + mod(0, i)
         first_ref[chunk(i)] = first.astype(BF16)
-        mixed_grad_ref[chunk(i)] = (grads[chunk(i)].astype(F32) * mod(5, i)).astype(BF16)
+    keep(first_ref, first_hbm)
+    ups.relay(0)
     for step in range(planes):
         attns.relay_across(step)
-    ups.relay(0)
     attns.finish()
-
-    keep_attn = pltpu.make_async_copy(attn_all, attn_out, load_sems.at[4])
-    keep_attn.start()
+    ups.relay(1)
+
+    keep(attn_all, attn_out)
     whole = attn_all[...].reshape(width, attn_turned.shape[0])
     for i in range(attn_turned.shape[0] // 128):
         attn_turned[i * 128 : (i + 1) * 128] = whole[:, i * 128 : (i + 1) * 128].T
@@ -489,13 +551,15 @@
             values = dot32(attn_turned[place_rows], first_ref[...], ((1,), (1,)))
             for h in range(heads):
                 qkv_ref[i, kind, h] = values[h * HD : (h + 1) * HD].astype(BF16)
-    ups.relay(1)
-    downs.relay(0)
+        if i == 0:
+            downs.relay(0)
+    keep(qkv_ref, qkv_hbm)
+    keep(proj_ref, proj_hbm)
 
     def attend(quarters):
         @pl.loop(0, pair)
         def _(index):
-            attend_quarters(ids_ref, qkv_ref, out_ref, log_ref, index, quarters, small_len)
+            attend_quarters(ids, qkv_ref, out_ref, log_ref, index, quarters, small_len)
 
     def project(quarter):
         return sum(
@@ -529,13 +593,17 @@
         branch_send[chunk(i)] = project(chunks + i).astype(BF16)
         branch_copies[i].start()
         if i == 0:
-            for step in range(2, planes - 1):
-                ups.relay(step)
-        else:
             downs.relay(1)
+    for step in range(2, planes - 1):
+        ups.relay(step)
     attend(range(chunks))
+    keep(out_ref, out_hbm)
+    keep(log_ref, log_hbm)
     for step in range(2, planes - 1):
         downs.relay(step)
+    for i in range(2 * chunks):
+        mixed_grad_ref[chunk(i)] = (grads[chunk(i)].astype(F32) * mod(5, i)).astype(BF16)
+    keep(mixed_grad_ref, mixed_grad_hbm)
     for i in range(chunks):
         branch = project(i)
         branch_copies[i].wait_recv()
@@ -545,23 +613,27 @@
         hat, _ = norm_parts(middle)
         second_ref[chunk(i)] = (hat * (1.0 + mod(4, i)) + mod(3, i)).astype(BF16)
         second_copies[i].start()
+    keep(branch_ref, branch_hbm)
+    keep(second_ref.at[pl.ds(0, own_len)], second_hbm.at[pl.ds(0, own_len)])
     for step in range(planes):
         ups.relay_across(step)
     for copy in second_copies:
         copy.wait()
+    keep(second_ref.at[pl.ds(own_len, own_len)], second_hbm.at[pl.ds(own_len, own_len)])
     for step in range(planes):
         downs.relay_across(step)
     for copy in branch_copies + part_copies:
         copy.wait_send()
-    keep_attn.wait()
     ups.finish()
     downs.finish()
-
-
-def front(ids, whole_args, vmem_args, planes, heads):
-    tokens, _, attn, up, down = whole_args
-    marks, _, _, ada, pick = vmem_args
-    slots = marks.shape[0]
+    for copy in keeps:
+        copy.wait()
+
+
+def front(marks, whole_args, vmem_args, planes, heads):
+    tokens = whole_args[0]
+    ada, table = vmem_args[4:]
+    slots = marks[0].shape[0]
     count = 2 * planes
     kinds, shard_rows, cols = ada.shape
     small_len = tokens.shape[0] // slots
@@ -571,32 +643,38 @@
     vmem = pl.BlockSpec(memory_space=pltpu.VMEM)
     whole = pl.BlockSpec(memory_space=pl.ANY)
     dma = pltpu.SemaphoreType.DMA
-    gathered = [
-        jax.ShapeDtypeStruct((planes, 2, block.shape[0], 2 * block.shape[1]), BF16)
-        for block in (attn, up, down)
+    gathered = [jax.ShapeDtypeStruct((planes, 2, shard_rows, 2 * width), BF16)] * 3
+    kept = [
+        jax.ShapeDtypeStruct((length, width), BF16),
+        jax.ShapeDtypeStruct((2, 3, heads, HD, length), BF16),
+        jax.ShapeDtypeStruct((2, heads * HD, width), BF16),
+        jax.ShapeDtypeStruct((2, heads * HD, length), BF16),
+        jax.ShapeDtypeStruct((2 * heads, 1, length), F32),
+        jax.ShapeDtypeStruct((own_len, width), F32),
+        jax.ShapeDtypeStruct((length, width), BF16),
+        jax.ShapeDtypeStruct((length, width), BF16),
     ]
     return pl.pallas_call(
         functools.partial(front_kernel, planes, small_len),
-        in_specs=[pl.BlockSpec(memory_space=pltpu.SMEM)]
+        in_specs=[pl.BlockSpec(memory_space=pltpu.SMEM)] * len(marks)
         + [whole] * len(whole_args)
         + [vmem] * len(vmem_args),
-        out_specs=[vmem] * 12 + [whole] * 3,
+        out_specs=[vmem] * 5 + [whole] * 11,
         out_shape=[
             jax.ShapeDtypeStruct((count * slots, 128), jnp.int32),
             jax.ShapeDtypeStruct((count * slots, shard_rows), F32),
             jax.ShapeDtypeStruct((count * slots, shard_rows), BF16),
-            jax.ShapeDtypeStruct((pick.shape[0], width), F32),
-            jax.ShapeDtypeStruct((length, width), BF16),
-            jax.ShapeDtypeStruct((2, 3, heads, HD, length), BF16),
-            jax.ShapeDtypeStruct((2, heads * HD, width), BF16),
-            jax.ShapeDtypeStruct((2, heads * HD, length), BF16),
-            jax.ShapeDtypeStruct((2 * heads, 1, length), F32),
-            jax.ShapeDtypeStruct((own_len, width), F32),
-            jax.ShapeDtypeStruct((length, width), BF16),
-            jax.ShapeDtypeStruct((length, width), BF16),
+            jax.ShapeDtypeStruct((2 * chunks * kinds, width), F32),
+            jax.ShapeDtypeStruct(ada.shape, BF16),
+            *kept,
             *gathered,
         ],
         scratch_shapes=[
+            *[pltpu.VMEM(array.shape, array.dtype) for array in kept],
+            dma((len(kept) + 2,)),
+            pltpu.VMEM((slots, 128), jnp.int32),
+            *([pltpu.VMEM((shard_rows, width), BF16)] * 3),
+            pltpu.VMEM((shard_rows, table.shape[1] + -table.shape[1] % 128), BF16),
             pltpu.VMEM((length, width), BF16),
             pltpu.VMEM((length, width), BF16),
             pltpu.VMEM((length, width), F32),
@@ -623,7 +701,7 @@
         compiler_params=pltpu.CompilerParams(
             collective_id=1, has_side_effects=True, vmem_limit_bytes=62 << 20
         ),
-    )(ids, *whole_args, *vmem_args)
+    )(*marks, *whole_args, *vmem_args)
 
 
 GELU_A = math.sqrt(2.0 / math.pi)
@@ -957,11 +1035,8 @@
     out_ref,
     log_ref,
     proj_ref,
-    scale_ref,
-    gate_ref,
-    gate_grad_ref,
-    rest_ref,
-    choose_ref,
+    mods_ref,
+    sums_ref,
     ada_ref,
     cond_ref,
     embed_ref,
@@ -981,6 +1056,7 @@
     first_land,
     first_own,
     core_land,
+    rest_rows,
     first_rows,
     row_land,
     mod_all,
@@ -1018,12 +1094,17 @@
     pair, rows, length = out_ref.shape
     heads = qkv_ref.shape[2]
     beside = x_neighbour(tp)
+    ids = own_first_ids(ids_ref, tp, chunks)
     around = [(tp, lax.rem(dp + step, count)) for step in range(1, count)]
     others = [(lax.rem(tp + step, 4), dp) for step in range(1, 4)]
     greet(around + others)
 
     def chunk(index):
         return pl.ds(index * small_len, small_len)
+
+    def mod(kind, quarter):
+        row = kind * 2 * chunks + quarter
+        return mods_ref[row : row + 1]
 
     def beside_copies(src, dst, first, sends, recvs):
         return [
@@ -1036,7 +1117,9 @@
     first_copies = beside_copies(first_send, first_land, 0, first_sends, first_recvs)
     for copy in branch_copies + far_copies:
         copy.start()
-    row_land[0, tp] = rest_ref[tp]
+    for part in range(4):
+        rest_rows[part] = sums_ref[:, part * cols : (part + 1) * cols]
+    row_land[0, tp] = rest_rows[tp]
     ups = ScatterRows(up_ref, scatter_refs[:6], planes)
     downs = ScatterRows(down_ref, scatter_refs[6:12], planes)
     attns = ScatterRows(core_land, scatter_refs[12:], planes)
@@ -1045,7 +1128,7 @@
 
     def row_copy(part, step):
         peer = lax.rem(tp + step, 4)
-        src = (rest_ref, first_rows)[part].at[peer]
+        src = (rest_rows, first_rows)[part].at[peer]
         sem = part * 4 + step
         return remote(src, row_land.at[part, tp], row_sends.at[sem], row_recvs.at[sem], peer, dp)
 
@@ -1071,7 +1154,7 @@
             @pl.loop(0, pair)
             def _(index):
                 back_quarters(
-                    ids_ref,
+                    ids,
                     qkv,
                     out_ref,
                     log_ref,
@@ -1206,9 +1289,9 @@
         for i in range(chunks):
             far_copies[i].wait_recv()
             far = far_land[chunk(i)].astype(F32)
-            block[chunk(i)] = (base[chunk(i)] + gate_ref[i : i + 1] * far).astype(BF16)
+            block[chunk(i)] = (base[chunk(i)] + mod(5, i) * far).astype(BF16)
             gate_grad = jnp.sum(far * cotangent[chunk(i)].astype(F32), axis=0, keepdims=True)
-            sums[2, i] = gate_grad + gate_grad_ref[i : i + 1]
+            sums[2, i] = gate_grad + sums_ref[3 * chunks + i : 3 * chunks + i + 1]
         keeps[1].start()
         attns.send(attns.order()[0])
         for i in range(chunks):
@@ -1217,7 +1300,7 @@
             grad = first_own[chunk(i)] + first_land[chunk(i)].astype(F32)
             sums[0, i] = jnp.sum(grad, axis=0, keepdims=True)
             sums[1, i] = jnp.sum(grad * hat, axis=0, keepdims=True)
-            back = norm_back(hat, rstd, grad * (1.0 + scale_ref[i : i + 1]))
+            back = norm_back(hat, rstd, grad * (1.0 + mod(1, i)))
             token[chunk(i)] = (back + middle[chunk(i)]).astype(BF16)
         keeps[0].start()
         quarter_rows = [sums[kind, i] for kind in range(3) for i in range(chunks)]
@@ -1249,8 +1332,19 @@
     for step in range(1, 4):
         row_copy(0, step).wait_recv()
         row_copy(1, step).wait_recv()
+    shape = (kinds * slots, 2 * 4 * 8)
+    pick_row, pick_col = iota(shape, 0), iota(shape, 1)
+    pick = jnp.zeros(shape, F32)
+    for part, known in enumerate(((2, 3, 4), (0, 1, 5))):
+        for source in range(4):
+            for i in range(chunks):
+                slot = ids_ref[source * chunks + i] - dp * slots
+                for j, kind in enumerate(known):
+                    col = (part * 4 + source) * 8 + j * chunks + i
+                    hit = (pick_row == kind * slots + slot) & (pick_col == col)
+                    pick = jnp.where(hit, 1.0, pick)
     grad_mod = lax.dot_general(
-        choose_ref[...],
+        pick,
         row_land[...].reshape(2 * 4 * 8, cols),
         (((1,), (0,)), ((), ())),
         precision=HIGHEST,
@@ -1356,7 +1450,7 @@
 
 def back(ids, whole_args, vmem_args, planes, small_len):
     qkv, branch = whole_args[0], whole_args[1]
-    out, ada, marks = vmem_args[0], vmem_args[8], vmem_args[11]
+    out, ada, marks = vmem_args[0], vmem_args[5], vmem_args[8]
     own_len, width = branch.shape
     chunks = own_len // small_len
     pair, rows, length = out.shape
@@ -1392,6 +1486,7 @@
             pltpu.VMEM((own_len, width), F32),
             pltpu.VMEM((planes, shard_rows, 2 * width), BF16),
             pltpu.VMEM((4, 8, cols), F32),
+            pltpu.VMEM((4, 8, cols), F32),
             pltpu.VMEM((2, 4, 8, cols), F32),
             pltpu.VMEM((count, kinds * slots, cols), BF16),
             pltpu.VMEM((count * slots, shard_rows), F32),
@@ -1596,57 +1691,15 @@
     table_average,
 ):
     row_count, width = tokens.shape
-    slot_count = quarter_ids.shape[0]
-    small_len = row_count // slot_count
-    span_len = row_count // 2
-    own_len = row_count // 4
-    shard_rows, _, quarter_width = qkv_weight.shape
-    heads = quarter_width // HD
-    tp_place = lax.axis_index("tp")
-    dp_place = lax.axis_index("dp")
-    span = tp_place // 2
-    side = tp_place % 2
-
-    attn_block = jnp.concatenate(
-        [qkv_weight[:, 0], qkv_weight[:, 1], qkv_weight[:, 2], proj_weight.T], axis=1
-    ).astype(BF16)
+    small_len = row_count // quarter_ids.shape[0]
+    heads = qkv_weight.shape[2] // HD
     planes = lax.axis_size("dp") // 2
-    marks = jnp.concatenate(
-        [
-            jnp.broadcast_to(labels[:, None], (slot_count, 64)),
-            jnp.broadcast_to(timesteps[:, None], (slot_count, 64)),
-        ],
-        axis=1,
-    )
-    column = dp_place * shard_rows + jnp.arange(shard_rows, dtype=jnp.int32)
-    half_width = width // 2
-    freqs = jnp.stack(
-        [
-            jnp.exp(-math.log(10000.0) * (column % half_width).astype(F32) / half_width),
-            (column < half_width).astype(F32),
-        ]
-    )
-    w_ada = ada_weight.transpose(1, 0, 2).astype(BF16)
-    classes = table_weight.shape[0]
-    table_low = jnp.pad(table_weight.T.astype(BF16), ((0, 0), (0, -classes % 128)))
-    slot_base = dp_place * slot_count
-    choose = (
-        quarter_ids[:, None] - slot_base == jnp.arange(slot_count, dtype=jnp.int32)[None, :]
-    ).astype(F32)
-    quarters = slot_count // 4
-
-    def own_first(array, size):
-        mine = lax.dynamic_slice_in_dim(array, (span * 2 + side) * size, size, 0)
-        other = lax.dynamic_slice_in_dim(array, (span * 2 + 1 - side) * size, size, 0)
-        return jnp.concatenate([mine, other], axis=0)
-
-    ids = own_first(quarter_ids, quarters)
-    pick = jnp.eye(6, dtype=F32)[:, None, :, None] * own_first(choose, quarters)[None, :, None, :]
     (
         marks,
         embed,
         cond_low,
         mods,
+        w_ada,
         first_in,
         qkv,
         w_proj,
@@ -1659,38 +1712,27 @@
         w_up,
         w_down,
     ) = front(
-        ids,
+        (quarter_ids, labels, timesteps),
+        (tokens, cotangent),
         (
-            tokens,
-            cotangent,
-            attn_block,
-            up_weight.astype(BF16),
-            down_weight.T.astype(BF16),
+            qkv_weight.transpose(1, 0, 2),
+            proj_weight.T,
+            up_weight,
+            down_weight.T,
+            ada_weight.transpose(1, 0, 2),
+            table_weight.T,
         ),
-        (marks, freqs, table_low, w_ada, pick.reshape(12 * quarters, 6 * slot_count)),
         planes,
         heads,
     )
-    w_attn = w_attn.reshape(width, 8 * quarter_width)
-    w_up = w_up.reshape(width, 8 * quarter_width)
-    w_down = w_down.reshape(width, 8 * quarter_width)
+    w_attn, w_up, w_down = (block.reshape(width, 2 * width) for block in (w_attn, w_up, w_down))
 
     base, far_mixed, grad_middle, own_branch, grad_up, grad_down, sums = mlp(
         second_in, grad_mixed, w_up, w_down, tokens, cotangent, branch, mods, planes, small_len
     )
 
-    rest = sums.reshape(8, 4, quarter_width).transpose(1, 0, 2)
-    chosen = choose.reshape(4, quarters, slot_count).transpose(2, 0, 1)
-    kinds = jnp.arange(6, dtype=jnp.int32)[:, None]
-    known = (kinds - 2 == jnp.arange(4, dtype=jnp.int32)[None, :]) & (kinds < 5)
-    later = jnp.where(kinds == 5, 2, kinds) == jnp.arange(4, dtype=jnp.int32)[None, :]
-    later = later & ((kinds < 2) | (kinds == 5))
-    pick = jnp.stack([known, later], axis=1).astype(F32)
-    pick = (pick[:, None, :, None, :, None] * chosen[None, :, None, :, None, :]).reshape(
-        6 * slot_count, 32 * quarters
-    )
     token_grad, block_out, up_reduced, down_reduced, attn_reduced, grad_ada, grad_embed, norm = back(
-        ids,
+        quarter_ids,
         (
             qkv,
             own_branch,
@@ -1708,11 +1750,8 @@
             attended,
             log_total,
             w_proj,
-            mods[2 * quarters : 3 * quarters],
-            mods[10 * quarters : 11 * quarters],
-            sums[3 * quarters :],
-            rest,
-            pick,
+            mods,
+            sums,
             w_ada,
             cond_low,
             embed,

time: 440 us -> 420 us (0.955)
  local copies, waits for them, and re-layouts: 12.7 us -> 3.13 us
  other arithmetic: 6.84 us -> 0.24 us
where the time goes in v5:
time: 420 us; the launch traced here: 412 us
  Pallas kernels  343 us (82%)
  waiting for transfers between devices  58.7 us (14%)
  starting transfers between devices  6.15 us (1%)
    pallas_call x1, Pallas kernels, back(): pl.pallas_call(functools.partial(back_kernel, planes, small_len), in_spec...  130 us
    pallas_call x1, Pallas kernels, front(): pl.pallas_call(functools.partial(front_kernel, planes, small_len), in_spe...  124 us
    pallas_call x1, Pallas kernels, mlp(): pl.pallas_call(functools.partial(mlp_kernel, planes, small_len), grid=(3,...  65.7 us
    ppermute x6, waiting for transfers between devices, swap(): return lax.ppermute(value, 'tp', [(i, i ^ bit) for i in range(4)])  58.7 us
    pallas_call x1, Pallas kernels, update(): pl.pallas_call(functools.partial(update_kernel, rates), in_specs=[vmem] *...  15.8 us
  transfers between devices with their start and end apart: 6, of which 4 were waited for; matrix products, arithmetic and copies ran while one was open for 0% of the time, Pallas kernels for 4%

profile of v5, /device:TPU:0, one launch (start us, length us, event | category | flops | bytes accessed | tf_op | source)
XLA Modules:
  0.0 412.4 jit_solution(8504494525573345184)
XLA Ops:
  0.7 124.3 %shard_map.484 = (s32[64,128]{1,0:T(8,128)}, f32[64,144]{1,0:T(8,128)}, bf16[64,144]{1,0:T(8,128)(2,1)}, f32[24,1152]{1,0:T(8,128)}, bf16[6,144,288]{2,1,0:T(8,1...) custom-call(s32[8]{0:T(128)} %ids_ref.3, ...), custom_call_target="tpu_custom_call" | custom-call | tf_op jit(solution)/shard_map/pallas_call | solution.py:657
  125.0 65.7 %shard_map.485 = (f32[512,1152]{1,0:T(8,128)}, bf16[512,1152]{1,0:T(8,128)(2,1)}, f32[512,1152]{1,0:T(8,128)}, bf16[512,1152]{1,0:T(8,128)(2,1)}, bf16[4,144,230...) custom-call(bf16[1024,1152]{1,0:T(8,128)(2,1)} %get-tuple-element.85.second_ref, ...), custom_call_target="tpu_custom_call" | custom-call | tf_op jit(solution)/shard_map/pallas_call | solution.py:901
  190.7 129.6 %shard_map.486 = (bf16[512,1152]{1,0:T(8,128)(2,1)}, bf16[512,1152]{1,0:T(8,128)(2,1)}, f32[144,1152]{1,0:T(8,128)}, f32[144,1152]{1,0:T(8,128)}, f32[144,1152]{...) custom-call(s32[8]{0:T(128)} %ids_ref.3, ...), custom_call_target="tpu_custom_call" | custom-call | tf_op jit(solution)/shard_map/pallas_call | solution.py:1464
  320.3 1.5 collective-permute-start.1
  321.7 0.6 collective-permute-start.3
  322.4 1.4 collective-permute-start
  323.7 0.6 collective-permute-start.2
  324.4 25.0 %collective-permute-done.1.refs_2_ = bf16[512,1152]{1,0:T(8,128)(2,1)S(1)} collective-permute-done((bf16[512,1152]{1,0:T(8,128)(2,1)}, bf16[512,1152]{1,0:T(8,128)(2,1)S(1)}, u32[]{:S(2)}, u32[]{:S(2)}) %collective-permute-start.1) | collective-permute-done | bytes 1179680 | tf_op jit(solution)/shard_map/ppermute | solution.py:1513
  349.4 24.4 %collective-permute-done.3.refs_5_ = bf16[512,1152]{1,0:T(8,128)(2,1)S(1)} collective-permute-done((bf16[512,1152]{1,0:T(8,128)(2,1)}, bf16[512,1152]{1,0:T(8,128)(2,1)S(1)}, u32[]{:S(2)}, u32[]{:S(2)}) %collective-permute-start.3) | collective-permute-done | bytes 1179680 | tf_op jit(solution)/shard_map/ppermute | solution.py:1513
  373.9 0.1 pad_maximum_fusion
  374.0 0.8 copy-done.16
  374.8 1.4 collective-permute-start.4
  376.5 0.1 pad_maximum_fusion.1
  376.6 0.7 copy-done.17
  377.2 0.3 copy-done.18
  377.6 0.6 collective-permute-start.5
  378.2 0.5 slice.19
  378.8 0.1 copy-done
  378.9 0.2 copy-done.1
  379.1 0.2 copy-done.3
  379.4 15.8 %shard_map.488 = (f32[3,144,288]{2,1,0:T(8,128)}, f32[3,144,288]{2,1,0:T(8,128)}, f32[3,144,288]{2,1,0:T(8,128)}, f32[3,144,288]{2,1,0:T(8,128)}, f32[144,288]{1...) custom-call(f32[8,128]{1,0:T(8,128)S(1)} %copy-done.14, ...), custom_call_target="tpu_custom_call" | custom-call | flops 41943040 | bytes 41943040 | tf_op jit(solution)/shard_map/pallas_call | solution.py:1633
  395.2 6.8 %collective-permute-done.4.refs_6_ = bf16[2,256,1152]{2,1,0:T(8,128)(2,1)S(1)} collective-permute-done((bf16[2,256,1152]{2,1,0:T(8,128)(2,1)S(1)}, bf16[2,256,1152]{2,1,0:T(8,128)(2,1)S(1)}, u32[]{:S(2)}, u32[]{:S(2)}) %collective-permute-start.4) | collective-permute-done | bytes 1179680 | tf_op jit(solution)/shard_map/ppermute | solution.py:1513
  402.0 2.6 collective-permute-done.5.refs_7_
  404.6 7.4 %shard_map.487 = (bf16[4,512,1152]{2,1,0:T(8,128)(2,1)}, bf16[4,512,1152]{2,1,0:T(8,128)(2,1)}) custom-call(bf16[512,1152]{1,0:T(8,128)(2,1)} %get-tuple-element.107.refs_0_, bf16[512,1152]{1,0:T(8,128)(2,1)} %copy-done.17, bf16[512,1152]{1,0:T(8,128)(2,1)} %copy-done.15, bf16[512,1152]{1,0:T(8,128)(2,1)} %get-tuple-element.108.refs_3_, ...), custom_call_target="tpu_custom_call" | custom-call | bytes 20971520 | tf_op jit(solution)/shard_map/pallas_call | solution.py:1546
  (40 shorter events, 0.3 us)
Async XLA Ops:
  320.3 29.1 %collective-permute-start.1 = (bf16[512,1152]{1,0:T(8,128)(2,1)}, bf16[512,1152]{1,0:T(8,128)(2,1)S(1)}, u32[]{:S(2)}, u32[]{:S(2)}) collective-permute-start(bf16[512,1152]{1,0:T(8,128)(2,1)} %get-tuple-element.107.refs_0_), channel_id=1, source_target_pairs={{0,16},{8,24},{16,0},{24,8},{1,17},{9,25},{17,1},{25,9},{2,18},{10... | collective-permute-start | bytes 3538952 | tf_op jit(solution)/shard_map/ppermute | solution.py:1513
  321.7 52.1 %collective-permute-start.3 = (bf16[512,1152]{1,0:T(8,128)(2,1)}, bf16[512,1152]{1,0:T(8,128)(2,1)S(1)}, u32[]{:S(2)}, u32[]{:S(2)}) collective-permute-start(bf16[512,1152]{1,0:T(8,128)(2,1)} %get-tuple-element.108.refs_3_), channel_id=1, source_target_pairs={{0,16},{8,24},{16,0},{24,8},{1,17},{9,25},{17,1},{25,9},{2,18},{10... | collective-permute-start | bytes 3538952 | tf_op jit(solution)/shard_map/ppermute | solution.py:1513
  322.4 53.9 %collective-permute-start = (bf16[512,1152]{1,0:T(8,128)(2,1)}, bf16[512,1152]{1,0:T(8,128)(2,1)S(1)}, u32[]{:S(2)}, u32[]{:S(2)}) collective-permute-start(bf16[512,1152]{1,0:T(8,128)(2,1)} %get-tuple-element.107.refs_0_), channel_id=1, source_target_pairs={{0,8},{8,0},{16,24},{24,16},{1,9},{9,1},{17,25},{25,17},{2,10},{10... | collective-permute-start | bytes 3538952 | tf_op jit(solution)/shard_map/ppermute | solution.py:1513
  323.7 52.6 %collective-permute-start.2 = (bf16[512,1152]{1,0:T(8,128)(2,1)}, bf16[512,1152]{1,0:T(8,128)(2,1)S(1)}, u32[]{:S(2)}, u32[]{:S(2)}) collective-permute-start(bf16[512,1152]{1,0:T(8,128)(2,1)} %get-tuple-element.108.refs_3_), channel_id=1, source_target_pairs={{0,8},{8,0},{16,24},{24,16},{1,9},{9,1},{17,25},{25,17},{2,10},{10... | collective-permute-start | bytes 3538952 | tf_op jit(solution)/shard_map/ppermute | solution.py:1513
  349.4 24.7 %copy-start.15 = (bf16[512,1152]{1,0:T(8,128)(2,1)}, bf16[512,1152]{1,0:T(8,128)(2,1)S(1)}, u32[]{:S(2)}) copy-start(bf16[512,1152]{1,0:T(8,128)(2,1)S(1)} %collective-permute-done.1.refs_2_) | copy-start | bytes 3538948
  373.9 4.9 %copy-start.8 = (f32[1001,144]{0,1:T(8,128)S(1)}, f32[1001,144]{0,1:T(8,128)}, u32[]{:S(2)}) copy-start(f32[1001,144]{0,1:T(8,128)} %param.57) | copy-start | bytes 1729732
  373.9 4.9 %copy-start.9 = (f32[288,144]{0,1:T(8,128)S(1)}, f32[288,144]{0,1:T(8,128)}, u32[]{:S(2)}) copy-start(f32[288,144]{0,1:T(8,128)} %param.39) | copy-start | bytes 497668
  373.9 4.9 %copy-start.10 = (f32[288,144]{0,1:T(8,128)S(1)}, f32[288,144]{0,1:T(8,128)}, u32[]{:S(2)}) copy-start(f32[288,144]{0,1:T(8,128)} %param.40) | copy-start | bytes 497668
  373.9 4.9 %copy-start.11 = (f32[288,144]{0,1:T(8,128)S(1)}, f32[288,144]{0,1:T(8,128)}, u32[]{:S(2)}) copy-start(f32[288,144]{0,1:T(8,128)} %param.41) | copy-start | bytes 497668
  374.8 27.1 %collective-permute-start.4 = (bf16[2,256,1152]{2,1,0:T(8,128)(2,1)S(1)}, bf16[2,256,1152]{2,1,0:T(8,128)(2,1)S(1)}, u32[]{:S(2)}, u32[]{:S(2)}) collective-permute-start(bf16[2,256,1152]{2,1,0:T(8,128)(2,1)S(1)} %pad_maximum_fusion), channel_id=1, source_target_pairs={{0,8},{8,0},{16,24},{24,16},{1,9},{9,1},{17,25},{25,17},{2,10},{10... | collective-permute-start | bytes 3538952 | tf_op jit(solution)/shard_map/ppermute | solution.py:1513
  376.2 2.5 copy-start.6
  376.2 2.5 copy-start.7
  376.3 1.3 copy-start.18
  376.3 1.9 copy-start.14
  376.3 2.5 copy-start.4
  376.3 2.5 copy-start.5
  376.4 2.5 copy-start
  376.4 2.7 copy-start.1
  376.4 2.7 copy-start.2
  376.4 2.9 copy-start.3
  376.4 2.9 copy-start.12
  376.4 2.9 copy-start.13
  377.6 27.0 %collective-permute-start.5 = (bf16[2,256,1152]{2,1,0:T(8,128)(2,1)S(1)}, bf16[2,256,1152]{2,1,0:T(8,128)(2,1)}, u32[]{:S(2)}, u32[]{:S(2)}) collective-permute-start(bf16[2,256,1152]{2,1,0:T(8,128)(2,1)S(1)} %pad_maximum_fusion.1), channel_id=1, source_target_pairs={{0,16},{8,24},{16,0},{24,8},{1,17},{9,25},{17,1},{25,9},{2,18},{10... | collective-permute-start | bytes 3538952 | tf_op jit(solution)/shard_map/ppermute | solution.py:1513
  402.0 2.6 copy-start.19
  (2 other events, 2.1 us)

commit v6 on v5

--- a/solution.py
+++ b/solution.py
@@ -842,6 +842,16 @@
 
     @pl.when((phase == 2) & (tile == tiles - 1))
     def _():
+        def weight_sum(index):
+            for which in range(2):
+                weight_copy(which, index).wait()
+                mine = weight_grads[which, index, :, core].astype(F32)
+                landed = weight_lands[which, index].astype(F32)
+                weight_lands[which, index] = (mine + landed).astype(BF16)
+                keep_weight(which, index).start()
+
+        for index in range(tiles - 1):
+            weight_sum(index)
         for load in loads:
             load.wait()
         second_copy.wait()
@@ -871,13 +881,7 @@
         sums_ref[...] = jnp.concatenate(
             [sums[kind, i] for kind in range(4) for i in range(chunks)], axis=0
         )
-        for index in range(tiles):
-            for which in range(2):
-                weight_copy(which, index).wait()
-                mine = weight_grads[which, index, :, core].astype(F32)
-                landed = weight_lands[which, index].astype(F32)
-                weight_lands[which, index] = (mine + landed).astype(BF16)
-                keep_weight(which, index).start()
+        weight_sum(tiles - 1)
         for index in range(tiles):
             for which in range(2):
                 keep_weight(which, index).wait()
@@ -1043,6 +1047,8 @@
     marks_ref,
     token_out,
     block_out,
+    near_out,
+    over_out,
     up_out,
     down_out,
     attn_out,
@@ -1082,6 +1088,8 @@
     cond_recvs,
     norm_sends,
     norm_recvs,
+    block_sends,
+    block_recvs,
     *scatter_refs,
 ):
     tp, dp = lax.axis_index("tp"), lax.axis_index("dp")
@@ -1134,6 +1142,20 @@
 
     for step in range(1, 4):
         row_copy(0, step).start()
+
+    def block_copy(way, piece):
+        place = pl.ds(piece * (own_len // 4), own_len // 4)
+        sem = 4 * way + piece
+        return remote(
+            block_out.at[place],
+            (near_out, over_out)[way].at[place],
+            block_sends.at[sem],
+            block_recvs.at[sem],
+            (beside, y_neighbour(tp))[way],
+            dp,
+        )
+
+    block_pieces = [(0, 0), (0, 1), (0, 2), (1, 0), (0, 3), (1, 1)]
 
     def attention(qkv, go, grad_k, grad_v):
         load = pltpu.make_async_copy(qkv_ref, qkv, load_sems.at[0])
@@ -1293,6 +1315,9 @@
             gate_grad = jnp.sum(far * cotangent[chunk(i)].astype(F32), axis=0, keepdims=True)
             sums[2, i] = gate_grad + sums_ref[3 * chunks + i : 3 * chunks + i + 1]
         keeps[1].start()
+        keeps[1].wait()
+        for piece in block_pieces[:2]:
+            block_copy(*piece).start()
         attns.send(attns.order()[0])
         for i in range(chunks):
             hat, rstd = norm_parts(tokens[chunk(i)].astype(F32))
@@ -1308,8 +1333,7 @@
         quarter_rows = jnp.concatenate(quarter_rows, axis=0)
         for part in range(4):
             first_rows[part] = quarter_rows[:, part * cols : (part + 1) * cols]
-        for keep in keeps:
-            keep.wait()
+        keeps[0].wait()
 
     pl.run_scoped(
         ends,
@@ -1324,6 +1348,8 @@
     row_land[1, tp] = first_rows[tp]
     for step in range(1, 4):
         row_copy(1, step).start()
+    for piece in block_pieces[2:4]:
+        block_copy(*piece).start()
     for step in attns.order()[1:-1]:
         attns.send(step)
     down_total = downs.collect(down_out[...])
@@ -1374,6 +1400,8 @@
     ]
     for copy in cond_copies:
         copy.start()
+    for piece in block_pieces[4:]:
+        block_copy(*piece).start()
     for kind in range(kinds):
         ada_grad = dot32(cond_ref[...], kind_rows[kind], ((0,), (0,)))
         ada_grad_ref[kind] = ada_grad
@@ -1438,6 +1466,8 @@
         norm = norm + norm_land[3 + i]
     norm_ref[...] = jnp.sqrt(norm)
 
+    for piece in block_pieces:
+        block_copy(*piece).wait()
     for copy in far_copies + first_copies:
         copy.wait_send()
     ups.finish()
@@ -1466,10 +1496,12 @@
         in_specs=[pl.BlockSpec(memory_space=pltpu.SMEM)]
         + [whole] * len(whole_args)
         + [vmem] * len(vmem_args),
-        out_specs=[whole, whole, vmem, vmem, vmem, vmem, vmem, vmem],
+        out_specs=[whole, whole, whole, whole, vmem, vmem, vmem, vmem, vmem, vmem],
         out_shape=[
             jax.ShapeDtypeStruct((own_len, width), BF16),
             jax.ShapeDtypeStruct((own_len, width), BF16),
+            jax.ShapeDtypeStruct((own_len, width), BF16),
+            jax.ShapeDtypeStruct((own_len // 2, width), BF16),
             shard,
             shard,
             shard,
@@ -1501,6 +1533,7 @@
             *([dma((count - 1,))] * 2),
             *([dma((3,))] * 2),
             *([dma((count + 2,))] * 2),
+            *([dma((8,))] * 2),
             *(scatter_scratch(planes, shard_rows, width) * 3),
         ],
         compiler_params=pltpu.CompilerParams(
@@ -1513,55 +1546,54 @@
     return lax.ppermute(value, "tp", [(i, i ^ bit) for i in range(4)])
 
 
-def assemble_kernel(*refs):
+def assemble_kernel(places, *refs):
     tp = lax.axis_index("tp")
     beside, across = x_neighbour(tp), y_neighbour(tp)
-    far = y_neighbour(beside)
-    sems = refs[-1]
-    copies = []
-    for i in range(2):
-        own, near, over = refs[3 * i : 3 * i + 3]
-        halves = refs[6:8]
-        whole = refs[8 + i]
-        half = own.shape[0] // 2
-        places = [
-            (own, whole.at[tp]),
-            (near, whole.at[beside]),
-            (over, whole.at[across]),
-            (halves[0].at[i], whole.at[far, pl.ds(0, half)]),
-            (halves[1].at[i], whole.at[far, pl.ds(half, half)]),
-        ]
-        for j, (src, dst) in enumerate(places):
-            copies.append(pltpu.make_async_copy(src, dst, sems.at[5 * i + j]))
+    owners = (tp, beside, across, y_neighbour(beside))
+    whole, sems = refs[-2:]
+    copies = [
+        pltpu.make_async_copy(src, whole.at[owners[owner], pl.ds(first, src.shape[0])], sems.at[i])
+        for i, (src, (owner, first)) in enumerate(zip(refs, places))
+    ]
     for copy in copies:
         copy.start()
     for copy in copies:
         copy.wait()
 
 
-def assemble(parts):
-    whole = pl.BlockSpec(memory_space=pl.ANY)
-    vmem = pl.BlockSpec(memory_space=pltpu.VMEM)
-    rows = jax.ShapeDtypeStruct((4, *parts[0].shape), BF16)
+def assemble(pieces):
+    parts = [piece[2] for piece in pieces]
+    rows, width = parts[0].shape
     return pl.pallas_call(
-        assemble_kernel,
-        in_specs=[vmem] * len(parts),
-        out_specs=[whole] * 2,
-        out_shape=[rows] * 2,
-        scratch_shapes=[pltpu.SemaphoreType.DMA((10,))],
-        cost_estimate=pl.CostEstimate(flops=0, bytes_accessed=20 << 20, transcendentals=0),
+        functools.partial(assemble_kernel, [piece[:2] for piece in pieces]),
+        in_specs=[pl.BlockSpec(memory_space=pltpu.VMEM)] * len(parts),
+        out_specs=pl.BlockSpec(memory_space=pl.ANY),
+        out_shape=jax.ShapeDtypeStruct((4, rows, width), BF16),
+        scratch_shapes=[pltpu.SemaphoreType.DMA((len(parts),))],
+        cost_estimate=pl.CostEstimate(flops=0, bytes_accessed=10 << 20, transcendentals=0),
     )(*parts)
 
 
-def spread(own):
-    beside = [swap(array, 1) for array in own]
-    across = [swap(array, 2) for array in own]
-    half = own[0].shape[0] // 2
-    far = (
-        swap(jnp.stack([array[:half] for array in across]), 1),
-        swap(jnp.stack([array[half:] for array in beside]), 2),
-    )
-    return (own[0], beside[0], across[0], own[1], beside[1], across[1], *far)
+def spread_token(own):
+    near, over = swap(own, 1), swap(own, 2)
+    half = own.shape[0] // 2
+    far = (swap(over[:half], 1), swap(near[half:], 2))
+    return [(0, 0, own), (1, 0, near), (2, 0, over), (3, 0, far[0]), (3, half, far[1])]
+
+
+def spread_block(own, near, over):
+    rows = own.shape[0]
+    half, rest = rows // 2, 3 * rows // 4
+    later = swap(own[half:], 2)
+    return [
+        (0, 0, own),
+        (1, 0, near),
+        (2, 0, over),
+        (2, half, later),
+        (3, 0, swap(over, 1)),
+        (3, half, swap(later[: rest - half], 1)),
+        (3, rest, swap(near[rest:], 2)),
+    ]
 
 
 def update_kernel(
@@ -1731,7 +1763,18 @@
         second_in, grad_mixed, w_up, w_down, tokens, cotangent, branch, mods, planes, small_len
     )
 
-    token_grad, block_out, up_reduced, down_reduced, attn_reduced, grad_ada, grad_embed, norm = back(
+    (
+        token_grad,
+        block_out,
+        block_near,
+        block_over,
+        up_reduced,
+        down_reduced,
+        attn_reduced,
+        grad_ada,
+        grad_embed,
+        norm,
+    ) = back(
         quarter_ids,
         (
             qkv,
@@ -1773,11 +1816,12 @@
     )
     wide = 0.5 * D ** (-0.5)
     rates = (wide, 4.0 * D ** (-0.5), wide, 0.5 * FF ** (-0.5), wide, 0.5)
-    parts = spread((token_grad, block_out))
+    token_pieces = spread_token(token_grad)
+    block_pieces = spread_block(block_out, block_near, block_over)
     fresh = update(
         (norm, attn_reduced, up_reduced, down_reduced, grad_ada, grad_embed, marks), states, rates
     )
-    token_grad, block_out = assemble(parts)
+    token_grad, block_out = assemble(token_pieces), assemble(block_pieces)
     return (
         block_out.reshape(row_count, width),
         token_grad.reshape(row_count, width),

time: 420 us -> 401 us (0.955)
  waiting for transfers between devices: 58.7 us -> 30.8 us
    ppermute x6 -> x8, waiting for transfers between devices: 58.7 us -> 30.8 us  [swap(): return lax.ppermute(value, 'tp', [(i, i ^ bit) for i in range(4)])]
    ppermute x6 -> x8, starting transfers between devices: 6.15 us -> 8.7 us  [swap(): return lax.ppermute(value, 'tp', [(i, i ^ bit) for i in range(4)])]
    pallas_call x1 -> x2, Pallas kernels: 7.41 us -> 9.05 us  [assemble(): pl.pallas_call(functools.partial(assemble_kernel, [piece[:2] for piece in...]
  transfers between devices with their start and end apart: 6 -> 8, of which waited for: 4 -> 4; matrix products, arithmetic and copies ran while one was open for 0% -> 1% of each run, Pallas kernels for 4% -> 5%
where the time goes in v6:
time: 401 us; the launch traced here: 393 us
  Pallas kernels  346 us (86%)
  waiting for transfers between devices  30.8 us (8%)
  starting transfers between devices  8.7 us (2%)
  local copies, waits for them, and re-layouts  5.7 us (1%)
    pallas_call x1, Pallas kernels, back(): pl.pallas_call(functools.partial(back_kernel, planes, small_len), in_spec...  133 us
    pallas_call x1, Pallas kernels, front(): pl.pallas_call(functools.partial(front_kernel, planes, small_len), in_spe...  124 us
    pallas_call x1, Pallas kernels, mlp(): pl.pallas_call(functools.partial(mlp_kernel, planes, small_len), grid=(3,...  64.3 us
    ppermute x8, waiting for transfers between devices, swap(): return lax.ppermute(value, 'tp', [(i, i ^ bit) for i in range(4)])  30.8 us
    pallas_call x1, Pallas kernels, update(): pl.pallas_call(functools.partial(update_kernel, rates), in_specs=[vmem] *...  16 us
    pallas_call x2, Pallas kernels, assemble(): pl.pallas_call(functools.partial(assemble_kernel, [piece[:2] for piece in...  9.05 us
    ppermute x8, starting transfers between devices, swap(): return lax.ppermute(value, 'tp', [(i, i ^ bit) for i in range(4)])  8.7 us
  transfers between devices with their start and end apart: 8, of which 4 were waited for; matrix products, arithmetic and copies ran while one was open for 1% of the time, Pallas kernels for 5%

profile of v6, /device:TPU:0, one launch (start us, length us, event | category | flops | bytes accessed | tf_op | source)
XLA Modules:
  0.0 393.0 jit_solution(18441847250745006251)
XLA Ops:
  0.7 124.3 %shard_map.484 = (s32[64,128]{1,0:T(8,128)}, f32[64,144]{1,0:T(8,128)}, bf16[64,144]{1,0:T(8,128)(2,1)}, f32[24,1152]{1,0:T(8,128)}, bf16[6,144,288]{2,1,0:T(8,1...) custom-call(s32[8]{0:T(128)} %ids_ref.3, ...), custom_call_target="tpu_custom_call" | custom-call | tf_op jit(solution)/shard_map/pallas_call | solution.py:657
  124.9 64.3 %shard_map.485 = (f32[512,1152]{1,0:T(8,128)}, bf16[512,1152]{1,0:T(8,128)(2,1)}, f32[512,1152]{1,0:T(8,128)}, bf16[512,1152]{1,0:T(8,128)(2,1)}, bf16[4,144,230...) custom-call(bf16[1024,1152]{1,0:T(8,128)(2,1)} %get-tuple-element.85.second_ref, ...), custom_call_target="tpu_custom_call" | custom-call | tf_op jit(solution)/shard_map/pallas_call | solution.py:905
  189.3 132.9 %shard_map.486 = (bf16[512,1152]{1,0:T(8,128)(2,1)}, bf16[512,1152]{1,0:T(8,128)(2,1)}, bf16[512,1152]{1,0:T(8,128)(2,1)}, bf16[256,1152]{1,0:T(8,128)(2,1)}, f3...) custom-call(s32[8]{0:T(128)} %ids_ref.3, ...), custom_call_target="tpu_custom_call" | custom-call | tf_op jit(solution)/shard_map/pallas_call | solution.py:1494
  322.2 0.7 collective-permute-start.5
  322.9 1.1 collective-permute-start.4
  324.0 1.2 slice.18
  325.2 1.5 collective-permute-start
  326.7 0.9 collective-permute-start.1
  327.6 23.7 %collective-permute-done.5.refs_2_ = bf16[512,1152]{1,0:T(8,128)(2,1)S(1)} collective-permute-done((bf16[512,1152]{1,0:T(8,128)(2,1)}, bf16[512,1152]{1,0:T(8,128)(2,1)S(1)}, u32[]{:S(2)}, u32[]{:S(2)}) %collective-permute-start.5) | collective-permute-done | bytes 1179680 | tf_op jit(solution)/shard_map/ppermute | solution.py:1546
  351.3 0.9 slice.25
  352.2 1.2 collective-permute-start.6
  353.4 0.9 slice.26
  354.3 0.6 collective-permute-start.7
  354.9 1.0 slice.20
  355.9 1.5 collective-permute-start.3
  357.4 6.5 %collective-permute-done.refs_3_ = bf16[256,1152]{1,0:T(8,128)(2,1)S(1)} collective-permute-done((bf16[256,1152]{1,0:T(8,128)(2,1)S(1)}, bf16[256,1152]{1,0:T(8,128)(2,1)S(1)}, u32[]{:S(2)}, u32[]{:S(2)}) %collective-permute-start) | collective-permute-done | bytes 589856 | tf_op jit(solution)/shard_map/ppermute | solution.py:1546
  363.9 1.2 collective-permute-start.2
  365.1 0.5 slice.23
  365.8 16.0 %shard_map.489 = (f32[3,144,288]{2,1,0:T(8,128)}, f32[3,144,288]{2,1,0:T(8,128)}, f32[3,144,288]{2,1,0:T(8,128)}, f32[3,144,288]{2,1,0:T(8,128)}, f32[144,288]{1...) custom-call(f32[8,128]{1,0:T(8,128)S(1)} %copy-done.14, ...), custom_call_target="tpu_custom_call" | custom-call | flops 41943040 | bytes 41943040 | tf_op jit(solution)/shard_map/pallas_call | solution.py:1665
  382.0 0.3 collective-permute-done.2.refs_5_
  382.4 0.4 copy-done.18
  382.7 0.7 copy-done.19
  383.5 4.5 %shard_map.487 = bf16[4,512,1152]{2,1,0:T(8,128)(2,1)} custom-call(bf16[512,1152]{1,0:T(8,128)(2,1)} %get-tuple-element.107.refs_0_, bf16[512,1152]{1,0:T(8,128)(2,1)} %get-tuple-element.108.refs_1_, bf16[256,1152]{1,0:T(8,128)(2,1)} %get-tuple-element.109.refs_2_, bf16[256,1152]{1,0:T(8,128)(2,1)} %copy-done.17, ...), custom_call_target="tpu_custom_call" | custom-call | bytes 10485760 | tf_op jit(solution)/shard_map/pallas_call | solution.py:1567
  388.0 4.5 %shard_map.488 = bf16[4,512,1152]{2,1,0:T(8,128)(2,1)} custom-call(bf16[512,1152]{1,0:T(8,128)(2,1)} %get-tuple-element.110.refs_0_, bf16[512,1152]{1,0:T(8,128)(2,1)} %copy-done.16, bf16[512,1152]{1,0:T(8,128)(2,1)} %copy-done.15, bf16[256,1152]{1,0:T(8,128)(2,1)} %collective-permute-done.6.refs_3_, bf16[256,1152]{1,0:T(8,128)(2,1)} %collective-permute-done.7.refs_4_), custom_call_target="tpu_custom_call" | custom-call | bytes 10485760 | tf_op jit(solution)/shard_map/pallas_call | solution.py:1567
  (44 shorter events, 0.4 us)
Async XLA Ops:
  189.2 176.4 %copy-start.8 = (f32[1001,144]{0,1:T(8,128)S(1)}, f32[1001,144]{0,1:T(8,128)}, u32[]{:S(2)}) copy-start(f32[1001,144]{0,1:T(8,128)} %param.57) | copy-start | bytes 1729732
  189.3 176.4 %copy-start.9 = (f32[288,144]{0,1:T(8,128)S(1)}, f32[288,144]{0,1:T(8,128)}, u32[]{:S(2)}) copy-start(f32[288,144]{0,1:T(8,128)} %param.39) | copy-start | bytes 497668
  189.3 176.4 %copy-start.10 = (f32[288,144]{0,1:T(8,128)S(1)}, f32[288,144]{0,1:T(8,128)}, u32[]{:S(2)}) copy-start(f32[288,144]{0,1:T(8,128)} %param.40) | copy-start | bytes 497668
  189.3 176.4 %copy-start.11 = (f32[288,144]{0,1:T(8,128)S(1)}, f32[288,144]{0,1:T(8,128)}, u32[]{:S(2)}) copy-start(f32[288,144]{0,1:T(8,128)} %param.41) | copy-start | bytes 497668
  322.2 29.1 %collective-permute-start.5 = (bf16[512,1152]{1,0:T(8,128)(2,1)}, bf16[512,1152]{1,0:T(8,128)(2,1)S(1)}, u32[]{:S(2)}, u32[]{:S(2)}) collective-permute-start(bf16[512,1152]{1,0:T(8,128)(2,1)} %get-tuple-element.110.refs_0_), channel_id=1, source_target_pairs={{0,16},{8,24},{16,0},{24,8},{1,17},{9,25},{17,1},{25,9},{2,18},{10... | collective-permute-start | bytes 3538952 | tf_op jit(solution)/shard_map/ppermute | solution.py:1546
  322.9 30.5 %collective-permute-start.4 = (bf16[512,1152]{1,0:T(8,128)(2,1)}, bf16[512,1152]{1,0:T(8,128)(2,1)S(1)}, u32[]{:S(2)}, u32[]{:S(2)}) collective-permute-start(bf16[512,1152]{1,0:T(8,128)(2,1)} %get-tuple-element.110.refs_0_), channel_id=1, source_target_pairs={{0,8},{8,0},{16,24},{24,16},{1,9},{9,1},{17,25},{25,17},{2,10},{10... | collective-permute-start | bytes 3538952 | tf_op jit(solution)/shard_map/ppermute | solution.py:1546
  324.0 41.7 %copy-start.6 = (f32[1001,144]{0,1:T(8,128)S(1)}, f32[1001,144]{0,1:T(8,128)}, u32[]{:S(2)}) copy-start(f32[1001,144]{0,1:T(8,128)} %param.55) | copy-start | bytes 1729732
  324.0 41.7 %copy-start.7 = (f32[1001,144]{0,1:T(8,128)S(1)}, f32[1001,144]{0,1:T(8,128)}, u32[]{:S(2)}) copy-start(f32[1001,144]{0,1:T(8,128)} %param.56) | copy-start | bytes 1729732
  325.2 38.7 %collective-permute-start = (bf16[256,1152]{1,0:T(8,128)(2,1)S(1)}, bf16[256,1152]{1,0:T(8,128)(2,1)S(1)}, u32[]{:S(2)}, u32[]{:S(2)}) collective-permute-start(bf16[256,1152]{1,0:T(8,128)(2,1)S(1)} %slice.18), channel_id=1, source_target_pairs={{0,16},{8,24},{16,0},{24,8},{1,17},{9,25},{17,1},{25,9},{2,18},{10... | collective-permute-start | bytes 1769480 | tf_op jit(solution)/shard_map/ppermute | solution.py:1546
  326.7 55.3 %collective-permute-start.1 = (bf16[256,1152]{1,0:T(8,128)(2,1)}, bf16[256,1152]{1,0:T(8,128)(2,1)}, u32[]{:S(2)}, u32[]{:S(2)}) collective-permute-start(bf16[256,1152]{1,0:T(8,128)(2,1)} %get-tuple-element.109.refs_2_), channel_id=1, source_target_pairs={{0,8},{8,0},{16,24},{24,16},{1,9},{9,1},{17,25},{25,17},{2,10},{10... | collective-permute-start | bytes 1769480 | tf_op jit(solution)/shard_map/ppermute | solution.py:1546
  351.3 13.9 %copy-start.14 = (f32[8,128]{1,0:T(8,128)S(1)}, f32[8,128]{1,0:T(8,128)}, u32[]{:S(2)}) copy-start(f32[8,128]{1,0:T(8,128)} %get-tuple-element.111.norm_ref) | copy-start | bytes 12292
  351.3 14.4 %copy-start.4 = (f32[144,1152]{1,0:T(8,128)S(1)}, f32[144,1152]{1,0:T(8,128)}, u32[]{:S(2)}) copy-start(f32[144,1152]{1,0:T(8,128)} %get-tuple-element.114.down_ref) | copy-start | bytes 1990660
  351.3 14.4 %copy-start.5 = (f32[144,1152]{1,0:T(8,128)S(1)}, f32[144,1152]{1,0:T(8,128)}, u32[]{:S(2)}) copy-start(f32[144,1152]{1,0:T(8,128)} %get-tuple-element.112.attn_ref) | copy-start | bytes 1990660
  352.1 13.6 %copy-start.1 = (f32[1001,144]{0,1:T(8,128)S(1)}, f32[1001,144]{0,1:T(8,128)}, u32[]{:S(2)}) copy-start(f32[1001,144]{0,1:T(8,128)} %param.54) | copy-start | bytes 1729732
  352.1 13.6 %copy-start.2 = (f32[288,144]{0,1:T(8,128)S(1)}, f32[288,144]{0,1:T(8,128)}, u32[]{:S(2)}) copy-start(f32[288,144]{0,1:T(8,128)} %param.38) | copy-start | bytes 497668
  352.1 13.6 %copy-start.3 = (f32[144,1152]{1,0:T(8,128)S(1)}, f32[144,1152]{1,0:T(8,128)}, u32[]{:S(2)}) copy-start(f32[144,1152]{1,0:T(8,128)} %get-tuple-element.113.up_ref) | copy-start | bytes 1990660
  352.1 13.6 %copy-start.12 = (s32[64,128]{1,0:T(8,128)S(1)}, s32[64,128]{1,0:T(8,128)}, u32[]{:S(2)}) copy-start(s32[64,128]{1,0:T(8,128)} %get-tuple-element.106.marks_ref) | copy-start | bytes 98308
  352.2 13.6 %copy-start.13 = (f32[64,144]{1,0:T(8,128)S(1)}, f32[64,144]{1,0:T(8,128)}, u32[]{:S(2)}) copy-start(f32[64,144]{1,0:T(8,128)} %get-tuple-element.116.embed_ref) | copy-start | bytes 110596
  352.2 35.9 %collective-permute-start.6 = (bf16[256,1152]{1,0:T(8,128)(2,1)}, bf16[256,1152]{1,0:T(8,128)(2,1)}, u32[]{:S(2)}, u32[]{:S(2)}) collective-permute-start(bf16[256,1152]{1,0:T(8,128)(2,1)} %slice.25), channel_id=1, source_target_pairs={{0,8},{8,0},{16,24},{24,16},{1,9},{9,1},{17,25},{25,17},{2,10},{10... | collective-permute-start | bytes 1769480 | tf_op jit(solution)/shard_map/ppermute | solution.py:1546
  353.4 28.4 %copy-start.16 = (bf16[512,1152]{1,0:T(8,128)(2,1)}, bf16[512,1152]{1,0:T(8,128)(2,1)S(1)}, u32[]{:S(2)}) copy-start(bf16[512,1152]{1,0:T(8,128)(2,1)S(1)} %collective-permute-done.4.refs_1_) | copy-start | bytes 3538948
  354.3 33.7 %collective-permute-start.7 = (bf16[256,1152]{1,0:T(8,128)(2,1)}, bf16[256,1152]{1,0:T(8,128)(2,1)}, u32[]{:S(2)}, u32[]{:S(2)}) collective-permute-start(bf16[256,1152]{1,0:T(8,128)(2,1)} %slice.26), channel_id=1, source_target_pairs={{0,16},{8,24},{16,0},{24,8},{1,17},{9,25},{17,1},{25,9},{2,18},{10... | collective-permute-start | bytes 1769480 | tf_op jit(solution)/shard_map/ppermute | solution.py:1546
  355.9 26.1 %collective-permute-start.3 = (bf16[128,1152]{1,0:T(8,128)(2,1)S(1)}, bf16[128,1152]{1,0:T(8,128)(2,1)S(1)}, u32[]{:S(2)}, u32[]{:S(2)}) collective-permute-start(bf16[128,1152]{1,0:T(8,128)(2,1)S(1)} %slice.20), channel_id=1, source_target_pairs={{0,16},{8,24},{16,0},{24,8},{1,17},{9,25},{17,1},{25,9},{2,18},{10... | collective-permute-start | bytes 884744 | tf_op jit(solution)/shard_map/ppermute | solution.py:1546
  363.9 17.8 %copy-start.17 = (bf16[256,1152]{1,0:T(8,128)(2,1)}, bf16[256,1152]{1,0:T(8,128)(2,1)S(1)}, u32[]{:S(2)}) copy-start(bf16[256,1152]{1,0:T(8,128)(2,1)S(1)} %collective-permute-done.refs_3_) | copy-start | bytes 1769476
  363.9 18.4 %collective-permute-start.2 = (bf16[128,1152]{1,0:T(8,128)(2,1)S(1)}, bf16[128,1152]{1,0:T(8,128)(2,1)S(1)}, u32[]{:S(2)}, u32[]{:S(2)}) collective-permute-start(bf16[128,1152]{1,0:T(8,128)(2,1)S(1)} %slice.24), channel_id=1, source_target_pairs={{0,8},{8,0},{16,24},{24,16},{1,9},{9,1},{17,25},{25,17},{2,10},{10... | collective-permute-start | bytes 884744 | tf_op jit(solution)/shard_map/ppermute | solution.py:1546
  (4 other events, 19.7 us)

commit v7 on v6

--- a/solution.py
+++ b/solution.py
@@ -1581,19 +1581,21 @@
     return [(0, 0, own), (1, 0, near), (2, 0, over), (3, 0, far[0]), (3, half, far[1])]
 
 
-def spread_block(own, near, over):
+def spread_block(own, near, over, before):
     rows = own.shape[0]
     half, rest = rows // 2, 3 * rows // 4
     later = swap(own[half:], 2)
-    return [
+    passed, before = lax.optimization_barrier((later[: rest - half], before))
+    pieces = [
         (0, 0, own),
         (1, 0, near),
         (2, 0, over),
         (2, half, later),
         (3, 0, swap(over, 1)),
-        (3, half, swap(later[: rest - half], 1)),
+        (3, half, swap(passed, 1)),
         (3, rest, swap(near[rest:], 2)),
     ]
+    return pieces, before
 
 
 def update_kernel(
@@ -1817,11 +1819,17 @@
     wide = 0.5 * D ** (-0.5)
     rates = (wide, 4.0 * D ** (-0.5), wide, 0.5 * FF ** (-0.5), wide, 0.5)
     token_pieces = spread_token(token_grad)
-    block_pieces = spread_block(block_out, block_near, block_over)
     fresh = update(
         (norm, attn_reduced, up_reduced, down_reduced, grad_ada, grad_embed, marks), states, rates
     )
-    token_grad, block_out = assemble(token_pieces), assemble(block_pieces)
+    fresh = list(fresh)
+    block_pieces, fresh[4] = spread_block(block_out, block_near, block_over, fresh[4])
+    token_grad = assemble(token_pieces)
+    block_rows = [piece[2] for piece in block_pieces]
+    block_rows, token_grad = lax.optimization_barrier((block_rows, token_grad))
+    block_out = assemble(
+        [(*piece[:2], rows) for piece, rows in zip(block_pieces, block_rows)]
+    )
     return (
         block_out.reshape(row_count, width),
         token_grad.reshape(row_count, width),

time: 401 us -> 397 us (0.990)
  no operation moved by 1% of the time
where the time goes in v7:
time: 397 us; the launch traced here: 390 us
  Pallas kernels  346 us (87%)
  waiting for transfers between devices  28 us (7%)
  starting transfers between devices  8.7 us (2%)
  local copies, waits for them, and re-layouts  5.16 us (1%)
    pallas_call x1, Pallas kernels, back(): pl.pallas_call(functools.partial(back_kernel, planes, small_len), in_spec...  133 us
    pallas_call x1, Pallas kernels, front(): pl.pallas_call(functools.partial(front_kernel, planes, small_len), in_spe...  124 us
    pallas_call x1, Pallas kernels, mlp(): pl.pallas_call(functools.partial(mlp_kernel, planes, small_len), grid=(3,...  64.3 us
    ppermute x8, waiting for transfers between devices, swap(): return lax.ppermute(value, 'tp', [(i, i ^ bit) for i in range(4)])  28 us
    pallas_call x1, Pallas kernels, update(): pl.pallas_call(functools.partial(update_kernel, rates), in_specs=[vmem] *...  16 us
    pallas_call x2, Pallas kernels, assemble(): pl.pallas_call(functools.partial(assemble_kernel, [piece[:2] for piece in...  9.04 us
    ppermute x8, starting transfers between devices, swap(): return lax.ppermute(value, 'tp', [(i, i ^ bit) for i in range(4)])  8.7 us
  transfers between devices with their start and end apart: 8, of which 4 were waited for; matrix products, arithmetic and copies ran while one was open for 1% of the time, Pallas kernels for 5%

profile of v7, /device:TPU:0, one launch (start us, length us, event | category | flops | bytes accessed | tf_op | source)
XLA Modules:
  0.0 389.7 jit_solution(5349931567107669953)
XLA Ops:
  0.7 124.3 %shard_map.484 = (s32[64,128]{1,0:T(8,128)}, f32[64,144]{1,0:T(8,128)}, bf16[64,144]{1,0:T(8,128)(2,1)}, f32[24,1152]{1,0:T(8,128)}, bf16[6,144,288]{2,1,0:T(8,1...) custom-call(s32[8]{0:T(128)} %ids_ref.3, ...), custom_call_target="tpu_custom_call" | custom-call | tf_op jit(solution)/shard_map/pallas_call | solution.py:657
  124.9 64.3 %shard_map.485 = (f32[512,1152]{1,0:T(8,128)}, bf16[512,1152]{1,0:T(8,128)(2,1)}, f32[512,1152]{1,0:T(8,128)}, bf16[512,1152]{1,0:T(8,128)(2,1)}, bf16[4,144,230...) custom-call(bf16[1024,1152]{1,0:T(8,128)(2,1)} %get-tuple-element.95.second_ref, ...), custom_call_target="tpu_custom_call" | custom-call | tf_op jit(solution)/shard_map/pallas_call | solution.py:905
  189.3 0.0 copy-start.9
  189.3 132.8 %shard_map.486 = (bf16[512,1152]{1,0:T(8,128)(2,1)}, bf16[512,1152]{1,0:T(8,128)(2,1)}, bf16[512,1152]{1,0:T(8,128)(2,1)}, bf16[256,1152]{1,0:T(8,128)(2,1)}, f3...) custom-call(s32[8]{0:T(128)} %ids_ref.3, ...), custom_call_target="tpu_custom_call" | custom-call | tf_op jit(solution)/shard_map/pallas_call | solution.py:1494
  322.1 0.7 collective-permute-start.5
  322.8 1.1 collective-permute-start.4
  323.9 1.2 slice.18
  325.2 1.5 collective-permute-start
  326.7 24.5 %collective-permute-done.5.refs_2_ = bf16[512,1152]{1,0:T(8,128)(2,1)S(1)} collective-permute-done((bf16[512,1152]{1,0:T(8,128)(2,1)}, bf16[512,1152]{1,0:T(8,128)(2,1)S(1)}, u32[]{:S(2)}, u32[]{:S(2)}) %collective-permute-start.5) | collective-permute-done | bytes 1179680 | tf_op jit(solution)/shard_map/ppermute | solution.py:1546
  351.3 1.2 collective-permute-start.6
  352.5 0.7 collective-permute-start.7
  353.2 0.9 collective-permute-start.1
  354.1 1.7 slice.20
  355.8 1.4 collective-permute-start.3
  357.3 16.0 %shard_map.487 = (f32[3,144,288]{2,1,0:T(8,128)}, f32[3,144,288]{2,1,0:T(8,128)}, f32[3,144,288]{2,1,0:T(8,128)}, f32[3,144,288]{2,1,0:T(8,128)}, f32[144,288]{1...) custom-call(f32[8,128]{1,0:T(8,128)S(1)} %copy-done.14, ...), custom_call_target="tpu_custom_call" | custom-call | flops 41943040 | bytes 41943040 | tf_op jit(solution)/shard_map/pallas_call | solution.py:1667
  373.3 1.2 collective-permute-start.2
  374.6 0.5 slice.23
  375.1 0.8 copy-done.18
  375.9 0.7 collective-permute-done.7.refs_4_
  376.6 4.5 %shard_map.488 = bf16[4,512,1152]{2,1,0:T(8,128)(2,1)} custom-call(bf16[512,1152]{1,0:T(8,128)(2,1)} %get-tuple-element.128.refs_0_, bf16[512,1152]{1,0:T(8,128)(2,1)} %copy-done.16, bf16[512,1152]{1,0:T(8,128)(2,1)} %copy-done.15, bf16[256,1152]{1,0:T(8,128)(2,1)} %copy-done.18, bf16[256,1152]{1,0:T(8,128)(2,1)} %collective-permute-done.7.refs_4_), custom_call_target="tpu_custom_call" | custom-call | bytes 10485760 | tf_op jit(solution)/shard_map/pallas_call | solution.py:1567
  381.1 0.8 collective-permute-done.3.refs_6_
  382.0 2.0 collective-permute-done.2.refs_5_
  384.0 0.7 copy-done.20
  384.7 4.5 %shard_map.489 = bf16[4,512,1152]{2,1,0:T(8,128)(2,1)} custom-call(bf16[512,1152]{1,0:T(8,128)(2,1)} %get-tuple-element.129.refs_0_, bf16[512,1152]{1,0:T(8,128)(2,1)} %get-tuple-element.130.refs_1_, bf16[256,1152]{1,0:T(8,128)(2,1)} %get-tuple-element.131.refs_2_, bf16[256,1152]{1,0:T(8,128)(2,1)} %copy-done.17, ...), custom_call_target="tpu_custom_call" | custom-call | bytes 10485760 | tf_op jit(solution)/shard_map/pallas_call | solution.py:1567
  (46 shorter events, 0.2 us)
Async XLA Ops:
  189.2 168.0 %copy-start.7 = (f32[1001,144]{0,1:T(8,128)S(1)}, f32[1001,144]{0,1:T(8,128)}, u32[]{:S(2)}) copy-start(f32[1001,144]{0,1:T(8,128)} %param.56) | copy-start | bytes 1729732
  189.2 167.9 %copy-start.8 = (f32[1001,144]{0,1:T(8,128)S(1)}, f32[1001,144]{0,1:T(8,128)}, u32[]{:S(2)}) copy-start(f32[1001,144]{0,1:T(8,128)} %param.57) | copy-start | bytes 1729732
  189.3 167.9 %copy-start.9 = (f32[288,144]{0,1:T(8,128)S(1)}, f32[288,144]{0,1:T(8,128)}, u32[]{:S(2)}) copy-start(f32[288,144]{0,1:T(8,128)} %param.39) | copy-start | bytes 497668
  189.3 167.9 %copy-start.10 = (f32[288,144]{0,1:T(8,128)S(1)}, f32[288,144]{0,1:T(8,128)}, u32[]{:S(2)}) copy-start(f32[288,144]{0,1:T(8,128)} %param.40) | copy-start | bytes 497668
  189.3 167.9 %copy-start.11 = (f32[288,144]{0,1:T(8,128)S(1)}, f32[288,144]{0,1:T(8,128)}, u32[]{:S(2)}) copy-start(f32[288,144]{0,1:T(8,128)} %param.41) | copy-start | bytes 497668
  322.1 29.1 %collective-permute-start.5 = (bf16[512,1152]{1,0:T(8,128)(2,1)}, bf16[512,1152]{1,0:T(8,128)(2,1)S(1)}, u32[]{:S(2)}, u32[]{:S(2)}) collective-permute-start(bf16[512,1152]{1,0:T(8,128)(2,1)} %get-tuple-element.128.refs_0_), channel_id=1, source_target_pairs={{0,16},{8,24},{16,0},{24,8},{1,17},{9,25},{17,1},{25,9},{2,18},{10... | collective-permute-start | bytes 3538952 | tf_op jit(solution)/shard_map/ppermute | solution.py:1546
  322.8 29.7 %collective-permute-start.4 = (bf16[512,1152]{1,0:T(8,128)(2,1)}, bf16[512,1152]{1,0:T(8,128)(2,1)S(1)}, u32[]{:S(2)}, u32[]{:S(2)}) collective-permute-start(bf16[512,1152]{1,0:T(8,128)(2,1)} %get-tuple-element.128.refs_0_), channel_id=1, source_target_pairs={{0,8},{8,0},{16,24},{24,16},{1,9},{9,1},{17,25},{25,17},{2,10},{10... | collective-permute-start | bytes 3538952 | tf_op jit(solution)/shard_map/ppermute | solution.py:1546
  323.9 33.3 %copy-start.5 = (f32[144,1152]{1,0:T(8,128)S(1)}, f32[144,1152]{1,0:T(8,128)}, u32[]{:S(2)}) copy-start(f32[144,1152]{1,0:T(8,128)} %get-tuple-element.121.attn_ref) | copy-start | bytes 1990660
  323.9 33.3 %copy-start.6 = (f32[1001,144]{0,1:T(8,128)S(1)}, f32[1001,144]{0,1:T(8,128)}, u32[]{:S(2)}) copy-start(f32[1001,144]{0,1:T(8,128)} %param.55) | copy-start | bytes 1729732
  325.1 32.1 %copy-start = (f32[144,3,288]{2,0,1:T(8,128)S(1)}, f32[144,3,288]{2,0,1:T(8,128)}, u32[]{:S(2)}) copy-start(f32[144,3,288]{2,0,1:T(8,128)} %param.34) | copy-start | bytes 1492996
  325.1 32.1 %copy-start.1 = (f32[1001,144]{0,1:T(8,128)S(1)}, f32[1001,144]{0,1:T(8,128)}, u32[]{:S(2)}) copy-start(f32[1001,144]{0,1:T(8,128)} %param.54) | copy-start | bytes 1729732
  325.2 32.1 %copy-start.2 = (f32[288,144]{0,1:T(8,128)S(1)}, f32[288,144]{0,1:T(8,128)}, u32[]{:S(2)}) copy-start(f32[288,144]{0,1:T(8,128)} %param.38) | copy-start | bytes 497668
  325.2 32.1 %copy-start.3 = (f32[144,1152]{1,0:T(8,128)S(1)}, f32[144,1152]{1,0:T(8,128)}, u32[]{:S(2)}) copy-start(f32[144,1152]{1,0:T(8,128)} %get-tuple-element.122.up_ref) | copy-start | bytes 1990660
  325.2 32.1 %copy-start.4 = (f32[144,1152]{1,0:T(8,128)S(1)}, f32[144,1152]{1,0:T(8,128)}, u32[]{:S(2)}) copy-start(f32[144,1152]{1,0:T(8,128)} %get-tuple-element.123.down_ref) | copy-start | bytes 1990660
  325.2 32.1 %copy-start.12 = (s32[64,128]{1,0:T(8,128)S(1)}, s32[64,128]{1,0:T(8,128)}, u32[]{:S(2)}) copy-start(s32[64,128]{1,0:T(8,128)} %get-tuple-element.116.marks_ref) | copy-start | bytes 98308
  325.2 32.1 %copy-start.13 = (f32[64,144]{1,0:T(8,128)S(1)}, f32[64,144]{1,0:T(8,128)}, u32[]{:S(2)}) copy-start(f32[64,144]{1,0:T(8,128)} %get-tuple-element.125.embed_ref) | copy-start | bytes 110596
  325.2 32.1 %copy-start.14 = (f32[8,128]{1,0:T(8,128)S(1)}, f32[8,128]{1,0:T(8,128)}, u32[]{:S(2)}) copy-start(f32[8,128]{1,0:T(8,128)} %get-tuple-element.120.norm_ref) | copy-start | bytes 12292
  325.2 48.1 %collective-permute-start = (bf16[256,1152]{1,0:T(8,128)(2,1)S(1)}, bf16[256,1152]{1,0:T(8,128)(2,1)S(1)}, u32[]{:S(2)}, u32[]{:S(2)}) collective-permute-start(bf16[256,1152]{1,0:T(8,128)(2,1)S(1)} %slice.18), channel_id=1, source_target_pairs={{0,16},{8,24},{16,0},{24,8},{1,17},{9,25},{17,1},{25,9},{2,18},{10... | collective-permute-start | bytes 1769480 | tf_op jit(solution)/shard_map/ppermute | solution.py:1546
  351.3 23.8 %collective-permute-start.6 = (bf16[256,1152]{1,0:T(8,128)(2,1)S(1)}, bf16[256,1152]{1,0:T(8,128)(2,1)S(1)}, u32[]{:S(2)}, u32[]{:S(2)}) collective-permute-start(bf16[256,1152]{1,0:T(8,128)(2,1)S(1)} %slice.25), channel_id=1, source_target_pairs={{0,8},{8,0},{16,24},{24,16},{1,9},{9,1},{17,25},{25,17},{2,10},{10... | collective-permute-start | bytes 1769480 | tf_op jit(solution)/shard_map/ppermute | solution.py:1546
  352.5 20.8 %copy-start.16 = (bf16[512,1152]{1,0:T(8,128)(2,1)}, bf16[512,1152]{1,0:T(8,128)(2,1)S(1)}, u32[]{:S(2)}) copy-start(bf16[512,1152]{1,0:T(8,128)(2,1)S(1)} %collective-permute-done.4.refs_1_) | copy-start | bytes 3538948
  352.5 24.1 %collective-permute-start.7 = (bf16[256,1152]{1,0:T(8,128)(2,1)S(1)}, bf16[256,1152]{1,0:T(8,128)(2,1)}, u32[]{:S(2)}, u32[]{:S(2)}) collective-permute-start(bf16[256,1152]{1,0:T(8,128)(2,1)S(1)} %slice.26), channel_id=1, source_target_pairs={{0,16},{8,24},{16,0},{24,8},{1,17},{9,25},{17,1},{25,9},{2,18},{10... | collective-permute-start | bytes 1769480 | tf_op jit(solution)/shard_map/ppermute | solution.py:1546
  353.2 28.8 %collective-permute-start.1 = (bf16[256,1152]{1,0:T(8,128)(2,1)}, bf16[256,1152]{1,0:T(8,128)(2,1)}, u32[]{:S(2)}, u32[]{:S(2)}) collective-permute-start(bf16[256,1152]{1,0:T(8,128)(2,1)} %get-tuple-element.131.refs_2_), channel_id=1, source_target_pairs={{0,8},{8,0},{16,24},{24,16},{1,9},{9,1},{17,25},{25,17},{2,10},{10... | collective-permute-start | bytes 1769480 | tf_op jit(solution)/shard_map/ppermute | solution.py:1546
  355.8 26.2 %collective-permute-start.3 = (bf16[128,1152]{1,0:T(8,128)(2,1)}, bf16[128,1152]{1,0:T(8,128)(2,1)S(1)}, u32[]{:S(2)}, u32[]{:S(2)}) collective-permute-start(bf16[128,1152]{1,0:T(8,128)(2,1)} %slice.20), channel_id=1, source_target_pairs={{0,16},{8,24},{16,0},{24,8},{1,17},{9,25},{17,1},{25,9},{2,18},{10... | collective-permute-start | bytes 884744 | tf_op jit(solution)/shard_map/ppermute | solution.py:1546
  373.3 10.6 %collective-permute-start.2 = (bf16[128,1152]{1,0:T(8,128)(2,1)S(1)}, bf16[128,1152]{1,0:T(8,128)(2,1)S(1)}, u32[]{:S(2)}, u32[]{:S(2)}) collective-permute-start(bf16[128,1152]{1,0:T(8,128)(2,1)S(1)} %slice.24), channel_id=1, source_target_pairs={{0,8},{8,0},{16,24},{24,16},{1,9},{9,1},{17,25},{25,17},{2,10},{10... | collective-permute-start | bytes 884744 | tf_op jit(solution)/shard_map/ppermute | solution.py:1546
  (5 other events, 9.9 us)
